TPU v7x, 32 devices: a whole 2x2x4 slice. The times are simulated.
32 devices in a mesh: row: 4 (over y, x), col: 2 (over core), ctx: 4 (over z).
Axes of the slice: x: 2, y: 2, z: 4, core: 2. Of those that a mesh axis runs over, the one named last changes fastest.
Arguments:
- queries: bfloat16 [4096, 6144], P(('col', 'ctx'), 'row'), may hold values from -16 to 16
- keys: bfloat16 [4096, 6144], P(('col', 'ctx'), 'row'), may hold values from -16 to 16
- values: bfloat16 [4096, 6144], P(('col', 'ctx'), 'row'), may hold values from -6 to 6
- out_weight: bfloat16 [6144, 6144], P('col', 'row'), may hold values from -0.078125 to 0.078125
- cotangent: bfloat16 [4096, 6144], P(('col', 'ctx'), 'row'), may hold values from -0.125 to 0.125
- block_mask: int32 [8, 8], replicated, may hold values from 0 to 1, as said below
Outputs:
- mixed_out: bfloat16 [4096, 6144], P(('col', 'ctx'), 'row')
- grad_weight: bfloat16 [6144, 6144], P(('col', 'ctx'), 'row')
Inputs may be any that keep to these rules, and one draw needn't show every extreme that they name: block_mask[i, i] is 1 for every block i, and block_mask[i, j] is 0 for j > i.
All inputs are finite; a program needn't handle non-finite values.
Results may differ from a plain program's by a relative error of at most 0.013.
Values may be sent and summed in bfloat16 or wider, within the bound.
No kernel may reach another device: no remote copies, remote signals or barrier semaphores. Data moves between devices by JAX's collectives and lax.ppermute only.
A program may use at most 128 MiB of HBM per device.

v0:
```python
import math

import jax
import jax.numpy as jnp
from jax import lax
from jax.sharding import PartitionSpec as P

HD = 128
BLOCK = 512


NEGATIVE_FILL = -1e30


def attend_block(carried, query_heads, key_block, value_block, allowed, score_scale):
    run_max, run_sum, weighted = carried
    tok_rows, head_count, head_size = query_heads.shape
    key_heads = key_block.reshape(key_block.shape[0], head_count, head_size)
    value_heads = value_block.reshape(value_block.shape[0], head_count, head_size)
    scores = (
        jnp.einsum("thd,uhd->thu", query_heads, key_heads, preferred_element_type=jnp.float32)
        * score_scale
    )
    scores = jnp.where(allowed[:, None, None], scores, NEGATIVE_FILL)
    new_max = jnp.maximum(run_max, jnp.max(scores, axis=2))
    correction = jnp.exp(run_max - new_max)
    weights = jnp.where(allowed[:, None, None], jnp.exp(scores - new_max[:, :, None]), 0.0)
    new_sum = run_sum * correction + jnp.sum(weights, axis=2)
    product = jnp.einsum(
        "thu,uhd->thd",
        weights.astype(jnp.bfloat16),
        value_heads,
        preferred_element_type=jnp.float32,
    )
    new_weighted = weighted * correction[:, :, None] + product
    return (new_max, new_sum, new_weighted)


def body(queries, keys, values, out_weight, cotangent, block_mask):
    tok_rows, feature_width = queries.shape
    head_count = feature_width // HD
    query_heads = queries.reshape(tok_rows, head_count, HD)
    score_scale = 1.0 / math.sqrt(HD)
    local_blocks = tok_rows // BLOCK
    first_block = lax.axis_index(("col", "ctx")) * local_blocks
    local_mask = lax.dynamic_slice_in_dim(block_mask, first_block, local_blocks, 0)
    start_state = (
        jnp.full((tok_rows, head_count), NEGATIVE_FILL, jnp.float32),
        jnp.zeros((tok_rows, head_count), jnp.float32),
        jnp.zeros((tok_rows, head_count, HD), jnp.float32),
    )
    key_piece = lax.all_gather(keys, ("col", "ctx"), axis=0, tiled=True)
    value_piece = lax.all_gather(values, ("col", "ctx"), axis=0, tiled=True)
    block_count = key_piece.shape[0] // BLOCK
    key_stack = key_piece.reshape(block_count, BLOCK, feature_width)
    value_stack = value_piece.reshape(block_count, BLOCK, feature_width)
    block_columns = jnp.arange(block_count, dtype=jnp.int32)

    def one_block(state_in, entries):
        key_block, value_block, block_column = entries
        mask_column = lax.dynamic_index_in_dim(local_mask, block_column, 1, keepdims=False)
        allowed = jnp.repeat(mask_column, BLOCK, total_repeat_length=tok_rows) == 1
        updated = attend_block(state_in, query_heads, key_block, value_block, allowed, score_scale)
        return (updated, None)

    state_out, _ = lax.scan(one_block, start_state, (key_stack, value_stack, block_columns))
    run_max, run_sum, weighted = state_out
    attended = (
        (weighted / run_sum[:, :, None]).reshape(tok_rows, feature_width).astype(jnp.bfloat16)
    )
    all_heads = lax.all_gather(attended, "row", axis=1, tiled=True)
    head_columns = all_heads
    mixed_out = jnp.dot(
        head_columns,
        lax.all_gather(out_weight, "col", axis=0, tiled=True),
        preferred_element_type=jnp.float32,
    )
    head_columns = all_heads
    grad_weight = lax.psum_scatter(
        lax.dot_general(
            head_columns, cotangent, (((0,), (0,)), ((), ())), preferred_element_type=jnp.float32
        ),
        ("col", "ctx"),
        scatter_dimension=0,
        tiled=True,
    )
    return (mixed_out.astype(jnp.bfloat16), grad_weight.astype(jnp.bfloat16))


def solution(mesh):
    in_specs = (
        P(("col", "ctx"), "row"),
        P(("col", "ctx"), "row"),
        P(("col", "ctx"), "row"),
        P("col", "row"),
        P(("col", "ctx"), "row"),
        P(),
    )
    out_specs = (P(("col", "ctx"), "row"), P(("col", "ctx"), "row"))
    return jax.shard_map(body, mesh=mesh, in_specs=in_specs, out_specs=out_specs, check_vma=False)
```

profile of v0, /device:TPU:25, one launch (start us, length us, event | category | flops | bytes accessed | tf_op | source)
XLA Modules:
  0.0 1386.7 jit_solution(15641243655177204159)
XLA Ops:
  12.7 112.0 %all-gather.5.cloned.1.call-done = bf16[4096,1536]{1,0:T(8,128)(2,1)} async-done(((bf16[512,1536]{1,0:T(8,128)(2,1)}), bf16[4096,1536]{1,0:T(8,128)(2,1)}) %all-gather.5.cloned.1.call-update) | async-done | bytes 12582928 | tf_op jit(solution)/shard_map/all_gather | solution.py:52
  124.7 116.6 %all-gather.7.cloned.1.call-done = bf16[4096,1536]{1,0:T(8,128)(2,1)} async-done(((bf16[512,1536]{1,0:T(8,128)(2,1)}), bf16[4096,1536]{1,0:T(8,128)(2,1)}) %all-gather.7.cloned.1.call-update) | async-done | bytes 12582928 | tf_op jit(solution)/shard_map/all_gather | solution.py:53
  241.3 300.4 %while.22 = (s32[]{:T(128)}, f32[512,12]{0,1:T(8,128)S(1)}, f32[512,12]{0,1:T(8,128)S(1)}, f32[512,12,128]{0,2,1:T(8,128)}, s32[8]{0:T(128)S(1)}, /*index=5*/s32...) while((s32[]{:T(128)}, f32[512,12]{0,1:T(8,128)S(1)}, ...), condition=%wide.region_3.4_spmd.clone, body=%wide.region_0.3_spmd.clone.sunk | while | flops 1653897216 | bytes 68026592 | solution.py:66
  250.0 8.7 bitcast_reduce_fusion.2
  258.8 7.2 fusion.35
  267.6 10.5 bitcast_add_fusion.2
  286.8 8.7 bitcast_reduce_fusion.2
  295.5 7.2 fusion.35
  304.4 11.4 bitcast_add_fusion.2
  324.5 8.7 bitcast_reduce_fusion.2
  333.2 7.2 fusion.35
  342.1 11.4 bitcast_add_fusion.2
  362.2 8.7 bitcast_reduce_fusion.2
  370.9 7.2 fusion.35
  379.7 11.4 bitcast_add_fusion.2
  399.8 8.7 bitcast_reduce_fusion.2
  408.5 7.2 fusion.35
  417.4 11.4 bitcast_add_fusion.2
  437.5 8.7 bitcast_reduce_fusion.2
  446.2 7.2 fusion.35
  455.1 11.4 bitcast_add_fusion.2
  475.2 8.7 bitcast_reduce_fusion.2
  483.9 7.2 fusion.35
  492.7 11.4 bitcast_add_fusion.2
  512.8 8.7 bitcast_reduce_fusion.2
  521.6 7.2 fusion.35
  530.4 11.4 bitcast_add_fusion.2
  546.1 70.3 %all-gather.9.cloned.1.call-done = bf16[512,6144]{0,1:T(8,128)(2,1)} async-done(((bf16[512,1536]{0,1:T(8,128)(2,1)}), bf16[512,6144]{0,1:T(8,128)(2,1)}) %all-gather.9.cloned.1.call-update) | async-done | bytes 6291472 | tf_op jit(solution)/shard_map/all_gather | solution.py:71
  616.4 27.7 %fusion.15 = f32[6144,1536]{1,0:T(8,128)} fusion(bf16[512,6144]{0,1:T(8,128)(2,1)} %all-gather.9.cloned.1.call-done, bf16[512,1536]{1,0:T(8,128)(2,1)S(1)} %copy-done), kind=kOutput, calls=%fused_computation.26 | convolution fusion | flops 9663676416 | bytes 45613056 | tf_op jit(solution)/shard_map/dot_general | solution.py:80
  644.2 8.3 all-gather.11.cloned.1.call-done
  652.4 16.6 %convolution_convert_fusion = bf16[512,1536]{1,0:T(8,128)(2,1)} fusion(bf16[512,6144]{0,1:T(8,128)(2,1)} %all-gather.9.cloned.1.call-done, bf16[6144,1536]{1,0:T(8,128)(2,1)} %all-gather.11.cloned.1.call-done), kind=kOutput, calls=%fused_computation.23 | convolution fusion | flops 9664462848 | bytes 26738688 | tf_op jit(solution)/shard_map/dot_general | solution.py:73
  669.1 707.1 %reduce-scatter.2.cloned.1.call-done = f32[768,1536]{1,0:T(8,128)} async-done(((f32[6144,1536]{1,0:T(8,128)}), f32[768,1536]{1,0:T(8,128)}) %reduce-scatter.2.cloned.1.call-update) | async-done | bytes 4718608 | tf_op jit(solution)/shard_map/reduce_scatter | solution.py:79
  (101 shorter events, 80.7 us)
Async XLA Ops:
  7.2 609.3 %copy-start = (bf16[512,1536]{1,0:T(8,128)(2,1)S(1)}, bf16[512,1536]{1,0:T(8,128)(2,1)}, u32[]{:S(2)}) copy-start(bf16[512,1536]{1,0:T(8,128)(2,1)} %param.16) | copy-start | bytes 4718596
  7.2 117.6 %all-gather.5.cloned.1.call-start = ((), (), s32[]{:S(2)}) async-start(), calls=%async_computation.1 | async-start | bytes 14155776 | tf_op jit(solution)/shard_map/all_gather | solution.py:52
  7.9 233.4 %all-gather.7.cloned.1.call-start = ((), (), s32[]{:S(2)}) async-start(), calls=%async_computation.2 | async-start | bytes 14155776 | tf_op jit(solution)/shard_map/all_gather | solution.py:53
  8.7 607.8 %all-gather.9.cloned.1.call-start = ((), (), s32[]{:S(2)}) async-start(), calls=%async_computation.3 | async-start | bytes 7864320 | tf_op jit(solution)/shard_map/all_gather | solution.py:71
  258.8 7.3 copy-start.1
  295.5 7.3 copy-start.1
  333.2 7.3 copy-start.1
  370.9 7.3 copy-start.1
  408.5 7.3 copy-start.1
  446.2 7.3 copy-start.1
  483.9 7.3 copy-start.1
  521.5 7.3 copy-start.1
  545.3 107.2 %all-gather.11.cloned.1.call-start = ((), (), s32[]{:S(2)}) async-start(), calls=%async_computation.4 | async-start | bytes 28311552 | tf_op jit(solution)/shard_map/all_gather | solution.py:75
  545.9 830.3 %reduce-scatter.2.cloned.1.call-start = ((), (), s32[]{:S(2)}) async-start(), calls=%async_computation.5 | async-start | bytes 42467328 | tf_op jit(solution)/shard_map/reduce_scatter | solution.py:79
Sparse Core Ops, SparseCore 0:
  9.6 115.0 all-gather.4
  126.3 114.9 all-gather.6
  545.4 70.9 all-gather.8
  617.9 34.5 all-gather.10
  654.7 721.4 reduce-scatter.1
where the time goes:
time: 1390 us
  waiting for transfers between devices  1020 us (73%)
  matrix products  204 us (15%)
  other arithmetic  70.7 us (5%)
  local copies, waits for them, and re-layouts  65.3 us (5%)
  loops' own time  15.9 us (1%)
    reduce_scatter x1, waiting for transfers between devices, body(): lax.psum_scatter(lax.dot_general(head_columns, cotangent, (((0,), (0,)),...  707 us
    all_gather x1, waiting for transfers between devices, body(): value_piece = lax.all_gather(values, ('col', 'ctx'), axis=0, tiled=True)  117 us
    all_gather x1, waiting for transfers between devices, body(): key_piece = lax.all_gather(keys, ('col', 'ctx'), axis=0, tiled=True)  112 us
    dot_general x8, matrix products, attend_block(): jnp.einsum('thu,uhd->thd', weights.astype(jnp.bfloat16), value_heads, pre...  90.3 us
    all_gather x1, waiting for transfers between devices, body(): all_heads = lax.all_gather(attended, 'row', axis=1, tiled=True)  70.3 us
    dot_general x8, matrix products, attend_block(): jnp.einsum('thd,uhd->thu', query_heads, key_heads, preferred_element_type...  69.7 us
    dynamic_slice x32, local copies, waits for them, and re-layouts, body(): lax.scan(one_block, start_state, (key_stack, value_stack, block_columns))  61.3 us
    reduce_sum x8, other arithmetic, attend_block(): new_sum = run_sum * correction + jnp.sum(weights, axis=2)  57.6 us
  transfers between devices with their start and end apart: 5, of which 5 were waited for; matrix products, arithmetic and copies ran while one was open for 3% of the time, Pallas kernels for 0%

commit v1 on v0

--- a/solution.py
+++ b/solution.py
@@ -1,15 +1,22 @@
+import functools
 import math
 
 import jax
 import jax.numpy as jnp
 from jax import lax
+from jax.experimental import pallas as pl
+from jax.experimental.pallas import tpu as pltpu
 from jax.sharding import PartitionSpec as P
 
 HD = 128
 BLOCK = 512
-
-
 NEGATIVE_FILL = -1e30
+HALF = 3
+LOG2E = math.log2(math.e)
+MIB = 1 << 20
+VMEM_MIB = 56
+ANY = pl.BlockSpec(memory_space=pl.ANY)
+SMEM = pl.BlockSpec(memory_space=pltpu.SMEM)
 
 
 def attend_block(carried, query_heads, key_block, value_block, allowed, score_scale):
@@ -36,7 +43,7 @@
     return (new_max, new_sum, new_weighted)
 
 
-def body(queries, keys, values, out_weight, cotangent, block_mask):
+def gathered_body(queries, keys, values, out_weight, cotangent, block_mask):
     tok_rows, feature_width = queries.shape
     head_count = feature_width // HD
     query_heads = queries.reshape(tok_rows, head_count, HD)
@@ -69,22 +76,436 @@
         (weighted / run_sum[:, :, None]).reshape(tok_rows, feature_width).astype(jnp.bfloat16)
     )
     all_heads = lax.all_gather(attended, "row", axis=1, tiled=True)
-    head_columns = all_heads
     mixed_out = jnp.dot(
-        head_columns,
+        all_heads,
         lax.all_gather(out_weight, "col", axis=0, tiled=True),
         preferred_element_type=jnp.float32,
     )
-    head_columns = all_heads
     grad_weight = lax.psum_scatter(
         lax.dot_general(
-            head_columns, cotangent, (((0,), (0,)), ((), ())), preferred_element_type=jnp.float32
+            all_heads, cotangent, (((0,), (0,)), ((), ())), preferred_element_type=jnp.float32
         ),
         ("col", "ctx"),
         scatter_dimension=0,
         tiled=True,
     )
     return (mixed_out.astype(jnp.bfloat16), grad_weight.astype(jnp.bfloat16))
+
+
+def _params(mib):
+    return pltpu.CompilerParams(vmem_limit_bytes=mib * MIB)
+
+
+def _pack_kernel(place, *refs):
+    columns, (send, keep) = refs[:6], refs[6:]
+    for out, first in ((send, 0), (keep, 3)):
+        out[0, 0] = columns[first][...]
+        out[0, 1] = columns[first + 1][...]
+        for n in range(BLOCK // HD):
+            tile = slice(n * HD, (n + 1) * HD)
+            out[0, 2, tile] = columns[first + 2][tile, :].T
+
+
+def pack(head, place, q, k, v):
+    shape = jax.ShapeDtypeStruct((2, 3, BLOCK, HD), jnp.bfloat16)
+
+    def column(kept):
+        def at(low, place_ref):
+            side = place_ref[0] if kept else 1 - place_ref[0]
+            return (0, 6 * low + 3 * side + head)
+
+        return pl.BlockSpec((BLOCK, HD), at)
+
+    out = pl.BlockSpec((1, 3, BLOCK, HD), lambda low, place_ref: (low, 0, 0, 0))
+    return pl.pallas_call(
+        _pack_kernel,
+        grid_spec=pltpu.PrefetchScalarGridSpec(
+            num_scalar_prefetch=1,
+            grid=(2,),
+            in_specs=[column(False)] * 3 + [column(True)] * 3,
+            out_specs=(out, out),
+        ),
+        out_shape=(shape, shape),
+        cost_estimate=pl.CostEstimate(flops=0, bytes_accessed=3 * MIB, transcendentals=0),
+        name="pack",
+    )(place, q, k, v, q, k, v)
+
+
+def _attend_kernel(place, mask, *refs):
+    own, other = refs[0], refs[1]
+    out, out_t = refs[2:4]
+    q_s, k_s, vt_s, sa_s, sb_s, m_s, l_s, acc_s, rows_s, cols_s, sems, other_sems = refs[4:]
+    c, z = place[2], place[3]
+    first = 4 * c
+    copies = []
+    others = []
+    for s in range(4):
+        b = s
+        copies.append(pltpu.make_async_copy(own.at[s, 0], q_s.at[b], sems.at[2 * s]))
+        copies.append(pltpu.make_async_copy(own.at[s, 1], k_s.at[first + b], sems.at[2 * s + 1]))
+        for n in range(4):
+            tile = pl.ds(n * HD, HD)
+            copies.append(
+                pltpu.make_async_copy(
+                    own.at[s, 2, tile], vt_s.at[first + b, :, tile], sems.at[8 + 4 * s + n]
+                )
+            )
+        others.append(pltpu.make_async_copy(other.at[s, 0], k_s.at[b], other_sems.at[s]))
+        for n in range(4):
+            tile = pl.ds(n * HD, HD)
+            others.append(
+                pltpu.make_async_copy(
+                    other.at[s, 1, tile], vt_s.at[b, :, tile], other_sems.at[4 + 4 * s + n]
+                )
+            )
+    for copy in copies:
+        copy.start()
+
+    @pl.when(c == 1)
+    def _():
+        for copy in others:
+            copy.start()
+
+    def listed(n, count):
+        i, j = n // 8, lax.rem(n, 8)
+        rows_s[count] = i
+        cols_s[count] = j
+        taken = (j <= first + i) & (mask[first + i, j] == 1)
+        return count + taken.astype(jnp.int32)
+
+    count = lax.fori_loop(0, 32, listed, 0)
+    for extra in range(3):
+        rows_s[count + extra] = 3
+        cols_s[count + extra] = first + 3
+
+    l_s[...] = jnp.zeros_like(l_s)
+    acc_s[...] = jnp.zeros_like(acc_s)
+    for copy in copies:
+        copy.wait()
+
+    @pl.when(c == 1)
+    def _():
+        for copy in others:
+            copy.wait()
+
+    scale = LOG2E / math.sqrt(HD)
+
+    def scores(t, ref):
+        ref[...] = lax.dot_general(
+            k_s[cols_s[t]], q_s[rows_s[t]], (((1,), (1,)), ((), ())), preferred_element_type=jnp.float32
+        )
+
+    def step(t, now, later):
+        i, j = rows_s[t], cols_s[t]
+        fresh = (t == 0) | (rows_s[jnp.maximum(t - 1, 0)] != i)
+        scores(t + 1, later)
+        old = jnp.where(fresh, NEGATIVE_FILL, m_s[...])
+        s = now[...]
+        m = jnp.maximum(old, jnp.max(s, axis=0, keepdims=True) * scale)
+        p = jnp.exp2(s * scale - m)
+        fix = jnp.exp2(old - m)
+        m_s[...] = m
+        l = l_s[...] * fix + jnp.sum(p, axis=0, keepdims=True)
+        l_s[...] = l
+        acc = acc_s[...] * fix + jnp.dot(vt_s[j], p.astype(jnp.bfloat16), preferred_element_type=jnp.float32)
+        acc_s[...] = acc
+
+        @pl.when((j == first + i) & (t < count))
+        def _():
+            done = acc_s[...] / l_s[...]
+            for n in range(BLOCK // HD):
+                tile = slice(n * HD, (n + 1) * HD)
+                out_t[i, tile] = done[:, tile].astype(jnp.bfloat16)
+            out[lax.rem(i - z + 4, 4)] = done.T.astype(jnp.bfloat16)
+
+    scores(0, sa_s)
+
+    def two(u, _):
+        step(2 * u, sa_s, sb_s)
+        step(2 * u + 1, sb_s, sa_s)
+        return 0
+
+    lax.fori_loop(0, (count + 1) // 2, two, 0)
+
+
+def attend(place, mask, own, other):
+    vmem = pl.BlockSpec(memory_space=pltpu.VMEM)
+    return pl.pallas_call(
+        _attend_kernel,
+        out_shape=(
+            jax.ShapeDtypeStruct((4, BLOCK, HD), jnp.bfloat16),
+            jax.ShapeDtypeStruct((4, BLOCK, HD), jnp.bfloat16),
+        ),
+        in_specs=[SMEM, SMEM, ANY, ANY],
+        out_specs=(vmem, vmem),
+        scratch_shapes=[
+            pltpu.VMEM((4, BLOCK, HD), jnp.bfloat16),
+            pltpu.VMEM((8, BLOCK, HD), jnp.bfloat16),
+            pltpu.VMEM((8, HD, BLOCK), jnp.bfloat16),
+            pltpu.VMEM((BLOCK, BLOCK), jnp.float32),
+            pltpu.VMEM((BLOCK, BLOCK), jnp.float32),
+            pltpu.VMEM((1, BLOCK), jnp.float32),
+            pltpu.VMEM((1, BLOCK), jnp.float32),
+            pltpu.VMEM((HD, BLOCK), jnp.float32),
+            pltpu.SMEM((40,), jnp.int32),
+            pltpu.SMEM((40,), jnp.int32),
+            pltpu.SemaphoreType.DMA((24,)),
+            pltpu.SemaphoreType.DMA((20,)),
+        ],
+        compiler_params=_params(VMEM_MIB),
+        cost_estimate=pl.CostEstimate(
+            flops=20 * 4 * BLOCK * BLOCK * HD,
+            bytes_accessed=4 * MIB,
+            transcendentals=20 * BLOCK * BLOCK,
+        ),
+        name="attend",
+    )(place, mask, own, other)
+
+
+def _mix_kernel(heads, added, place, *refs):
+    count = 4 * len(heads)
+    parts, (w_own, w_other) = refs[:count], refs[count : count + 2]
+    sums = refs[count + 2] if added else None
+    out = refs[count + 2 + added]
+    a_s, w_s, sum_s, a_sem, w_sem = refs[count + 3 + added :]
+    x, y, c, z = place[0], place[1], place[2], place[3]
+    depth = len(heads) * HD
+
+    def attended(n, side):
+        return pltpu.make_async_copy(
+            parts[4 * n + side], a_s.at[side, :, n], a_sem.at[4 * n + side]
+        )
+
+    def weight(side, block, ref):
+        xx = lax.rem(x + side % 2, 2)
+        from_z = lax.rem(z - block + 4, 4)
+        at = pl.multiple_of((6 * from_z + 3 * xx + heads[0]) * HD, HD)
+        return pltpu.make_async_copy(
+            ref.at[pl.ds(at, depth)],
+            w_s.at[pl.ds((4 * side + block) * depth, depth)],
+            w_sem.at[4 * side + block],
+        )
+
+    def fetch(side):
+        yy = lax.rem(y + side // 2, 2)
+        for n in range(len(heads)):
+            attended(n, side).start()
+        for block in range(4):
+            pl.when(yy == c)(weight(side, block, w_own).start)
+            pl.when(yy != c)(weight(side, block, w_other).start)
+
+    fetch(0)
+    fetch(1)
+    width = 512
+    piece = 4 * depth
+    for side in range(4):
+        if 0 < side < 3:
+            fetch(side + 1)
+        for n in range(len(heads)):
+            attended(n, side).wait()
+        for block in range(4):
+            weight(side, block, w_own).wait()
+
+        def tile(t, _, side=side):
+            cut = pl.ds(pl.multiple_of(t * width, width), width)
+            rows = jnp.concatenate(
+                [a_s[side, block, n] for block in range(4) for n in range(len(heads))], axis=1
+            )
+            term = jnp.dot(
+                rows, w_s[side * piece : (side + 1) * piece, cut], preferred_element_type=jnp.float32
+            )
+            if side > 0:
+                term += sum_s[:, cut]
+            elif added:
+                term += sums[:, cut]
+            if side < 3:
+                sum_s[:, cut] = term
+            else:
+                out[:, cut] = term.astype(out.dtype)
+            return 0
+
+        lax.fori_loop(0, out.shape[1] // width, tile, 0)
+
+
+def mix(place, head, parts, w_own, w_other, sums, kind):
+    heads = (head,)
+    columns = w_own.shape[1]
+    depth = 16 * len(heads) * HD
+    vmem = pl.BlockSpec(memory_space=pltpu.VMEM)
+    added = [] if sums is None else [sums]
+    return pl.pallas_call(
+        functools.partial(_mix_kernel, heads, len(added)),
+        out_shape=jax.ShapeDtypeStruct((BLOCK, columns), kind),
+        in_specs=[SMEM] + [ANY] * (len(parts) + 2) + [vmem] * len(added),
+        out_specs=vmem,
+        scratch_shapes=[
+            pltpu.VMEM((4, 4, len(heads), BLOCK, HD), jnp.bfloat16),
+            pltpu.VMEM((depth, columns), jnp.bfloat16),
+            pltpu.VMEM((BLOCK, columns), jnp.float32),
+            pltpu.SemaphoreType.DMA((4 * len(heads),)),
+            pltpu.SemaphoreType.DMA((16,)),
+        ],
+        compiler_params=_params(VMEM_MIB),
+        cost_estimate=pl.CostEstimate(
+            flops=2 * BLOCK * depth * columns, bytes_accessed=9 * len(heads) * MIB, transcendentals=0
+        ),
+        name="mix",
+    )(place, *parts, w_own, w_other, *added)
+
+
+def _grad_kernel(count, place, *refs):
+    parts, cot = refs[: 4 * count], refs[4 * count]
+    sent, kept, left, right, l_sem, r_sem = refs[4 * count + 1 :]
+    x, y, c = place[0], place[1], place[2]
+    step = pl.program_id(0)
+
+    @pl.when(step == 0)
+    def _():
+        rows = pltpu.make_async_copy(cot, right, r_sem)
+        rows.start()
+        for n, ref in enumerate(parts):
+            head, dx, dy = n // 4, n % 2, n // 2 % 2
+            mine = (lax.rem(y + dy, 2) == c).astype(jnp.int32)
+            at = 2 * count * mine + count * lax.rem(x + dx, 2) + head
+            pltpu.make_async_copy(ref, left.at[at], l_sem.at[at]).start()
+        rows.wait()
+
+    for n in range(count):
+        at = count * step + n
+        pltpu.make_async_copy(parts[n], left.at[at], l_sem.at[at]).wait()
+    rows = jnp.concatenate(
+        [
+            jnp.concatenate(
+                [
+                    left[count * step + n, block, tile * HD : (tile + 1) * HD]
+                    for block in range(4)
+                    for tile in range(BLOCK // HD)
+                ],
+                axis=1,
+            )
+            for n in range(count)
+        ]
+    )
+    total = jnp.dot(rows, right[...], preferred_element_type=jnp.float32)
+
+    @pl.when(step < 2)
+    def _():
+        sent[...] = total.astype(jnp.bfloat16)
+
+    @pl.when(step >= 2)
+    def _():
+        kept[...] = total
+
+
+def grad(place, parts, cot):
+    count = len(parts) // 4
+    rows = count * HD
+    tokens, width = cot.shape
+    return pl.pallas_call(
+        functools.partial(_grad_kernel, count),
+        grid=(4,),
+        out_shape=(
+            jax.ShapeDtypeStruct((2 * rows, width), jnp.bfloat16),
+            jax.ShapeDtypeStruct((2 * rows, width), jnp.float32),
+        ),
+        in_specs=[SMEM] + [ANY] * (len(parts) + 1),
+        out_specs=(
+            pl.BlockSpec((rows, width), lambda i: (jnp.minimum(i, 1), 0)),
+            pl.BlockSpec((rows, width), lambda i: (jnp.maximum(i - 2, 0), 0)),
+        ),
+        scratch_shapes=[
+            pltpu.VMEM((4 * count, 4, BLOCK, HD), jnp.bfloat16),
+            pltpu.VMEM((tokens, width), jnp.bfloat16),
+            pltpu.SemaphoreType.DMA((4 * count,)),
+            pltpu.SemaphoreType.DMA,
+        ],
+        compiler_params=_params(VMEM_MIB),
+        cost_estimate=pl.CostEstimate(
+            flops=8 * rows * tokens * width, bytes_accessed=(4 * count + 3) * MIB, transcendentals=0
+        ),
+        name="grad",
+    )(place, *parts, cot)
+
+
+X_SWAP = [(0, 1), (1, 0), (2, 3), (3, 2)]
+Y_SWAP = [(0, 2), (2, 0), (1, 3), (3, 1)]
+
+
+OTHER_CORE = [(0, 1), (1, 0)]
+
+
+def around(shift):
+    return [(i, (i + shift) % 4) for i in range(4)]
+
+
+def over_row(a, x_first):
+    first, second = (X_SWAP, Y_SWAP) if x_first else (Y_SWAP, X_SWAP)
+    near = lax.ppermute(a, "row", first)
+    far = lax.ppermute(near, "row", second)
+    next_to = lax.ppermute(a, "row", second)
+    return [a, near, next_to, far] if x_first else [a, next_to, near, far]
+
+
+def planes_body(queries, keys, values, out_weight, cotangent, block_mask):
+    row, c, z = lax.axis_index("row"), lax.axis_index("col"), lax.axis_index("ctx")
+    x, y = row % 2, row // 2
+    place = jnp.stack([x, y, c, z]).astype(jnp.int32)
+    columns = cotangent.shape[1]
+    cut = columns // 2
+
+    def exchanged(h, place):
+        send, keep = pack(h, place, queries, keys, values)
+        got = lax.ppermute(send, "row", X_SWAP)
+        return keep, got
+
+    def over_ctx(kept, got):
+        pieces = [jnp.where(x == 0, kept, got), jnp.where(x == 0, got, kept)]
+        return lax.all_to_all(jnp.concatenate(pieces), "ctx", 0, 0, tiled=True)
+
+    def attended(h, own, before):
+        other = lax.ppermute(own[:, 1:], "col", [(0, 1)])
+        other, before = lax.optimization_barrier((other, before))
+        out, out_t = attend(place, block_mask, own, other)
+        home = [lax.ppermute(out[s], "ctx", around(s)) for s in range(1, 4)]
+        return jnp.stack([out[0]] + home), over_row(out_t, True), before
+
+    first_cot = lax.all_gather(cotangent[:, :cut], "ctx", axis=0, tiled=True)
+    pair = exchanged(0, place)
+    pair, later = lax.optimization_barrier((pair, place))
+    own0 = over_ctx(*pair)
+    pairs = [exchanged(h, later) for h in range(1, HALF)]
+    w_other = lax.ppermute(out_weight, "col", OTHER_CORE)
+    own0, pairs, w_other, first_cot = lax.optimization_barrier((own0, pairs, w_other, first_cot))
+    own1 = over_ctx(*pairs[0])
+    home0, grad0, _ = attended(0, own0, ())
+    own1, pair, home0, grad0 = lax.optimization_barrier((own1, pairs[1], home0, grad0))
+    own2 = over_ctx(*pair)
+    home1, grad1, _ = attended(1, own1, ())
+    mix0 = over_row(home0, False)
+    own2, last_half, home1, mix0, grad1 = lax.optimization_barrier(
+        (own2, cotangent[:, cut:], home1, mix0, grad1)
+    )
+    last_cot = lax.all_gather(last_half, "ctx", axis=0, tiled=True)
+    mix1 = over_row(home1, False)
+    home2, grad2, _ = attended(2, own2, ())
+    sums = mix(place, 0, mix0, out_weight, w_other, None, jnp.float32)
+    home2, mix1, sums = lax.optimization_barrier((home2, mix1, sums))
+    mix2 = over_row(home2, False)
+
+    def summed(parts, cot):
+        sent, kept = grad(place, parts, cot)
+        received = lax.ppermute(sent, "col", OTHER_CORE)
+        done = (kept + received.astype(jnp.float32)).astype(jnp.bfloat16)
+        return done.reshape(2, -1, cot.shape[1])
+
+    early = summed(grad0 + grad1, first_cot)
+    sums = mix(place, 1, mix1, out_weight, w_other, sums, jnp.float32)
+    late = summed(grad2, first_cot)
+    mixed_out = mix(place, 2, mix2, out_weight, w_other, sums, jnp.bfloat16)
+    last = summed(grad0 + grad1 + grad2, last_cot)
+    grad_weight = jnp.concatenate([jnp.concatenate([early, late], axis=1), last], axis=2)
+    grad_weight = grad_weight.reshape(-1, columns)
+    return (mixed_out, grad_weight)
 
 
 def solution(mesh):
@@ -97,4 +518,14 @@
         P(),
     )
     out_specs = (P(("col", "ctx"), "row"), P(("col", "ctx"), "row"))
-    return jax.shard_map(body, mesh=mesh, in_specs=in_specs, out_specs=out_specs, check_vma=False)
+    four = dict(mesh.shape) == {"row": 4, "col": 2, "ctx": 4}
+
+    def whole(queries, keys, values, out_weight, cotangent, block_mask):
+        fits = queries.shape == (8 * BLOCK, 48 * HD)
+        body = planes_body if four and fits else gathered_body
+        mapped = jax.shard_map(
+            body, mesh=mesh, in_specs=in_specs, out_specs=out_specs, check_vma=False
+        )
+        return mapped(queries, keys, values, out_weight, cotangent, block_mask)
+
+    return whole

time: 1390 us -> 356 us (0.26)
  waiting for transfers between devices: 1020 us -> 167 us
  matrix products: 204 us -> 0 us
  Pallas kernels: 0 us -> 104 us
  other arithmetic: 70.7 us -> 10.6 us
  local copies, waits for them, and re-layouts: 65.3 us -> 14.3 us
  starting transfers between devices: 0.37 us -> 43 us
  loops' own time: 15.9 us -> 0 us
    reduce_scatter x1 -> x0, waiting for transfers between devices: 707 us -> none  [body(): lax.psum_scatter(lax.dot_general(head_columns, cotangent, (((0,), (0,)),...]
    all_gather x4 -> x2, waiting for transfers between devices: 307 us -> 0.01 us  [the longest x1 0.01 us: planes_body(): first_cot = lax.all_gather(cotangent[:, :cut], 'ctx', axis=0, tiled=True)]
    dot_general x18 -> x0, matrix products: 204 us -> none  [the longest x8 90.3 us: attend_block(): jnp.einsum('thu,uhd->thd', weights.astype(jnp.bfloat16), value_heads, pre...]
    ppermute x0 -> x37, waiting for transfers between devices: none -> 144 us  [the longest x3 51.7 us: exchanged(): got = lax.ppermute(send, 'row', X_SWAP)]
    pallas_call x0 -> x12, Pallas kernels: none -> 104 us  [the longest x3 35.5 us: attend(): pl.pallas_call(_attend_kernel, out_shape=(jax.ShapeDtypeStruct((4, BLOCK,...]
    dynamic_slice x33 -> x0, local copies, waits for them, and re-layouts: 62 us -> none  [the longest x32 61.3 us: body(): lax.scan(one_block, start_state, (key_stack, value_stack, block_columns))]
    reduce_sum x8 -> x0, other arithmetic: 57.6 us -> none  [attend_block(): new_sum = run_sum * correction + jnp.sum(weights, axis=2)]
    ppermute x0 -> x37, starting transfers between devices: none -> 27.5 us  [the longest x6 6.44 us: over_row(): near = lax.ppermute(a, 'row', first)]
  transfers between devices with their start and end apart: 5 -> 42, of which waited for: 5 -> 18; matrix products, arithmetic and copies ran while one was open for 3% -> 4% of each run, Pallas kernels for 0% -> 29%
where the time goes in v1:
time: 356 us; the launch traced here: 353 us
  waiting for transfers between devices  167 us (47%)
  Pallas kernels  104 us (29%)
  starting transfers between devices  43 us (12%)
  between operations  14.6 us (4%)
  local copies, waits for them, and re-layouts  14.3 us (4%)
  other arithmetic  10.6 us (3%)
    ppermute x3, waiting for transfers between devices, exchanged(): got = lax.ppermute(send, 'row', X_SWAP)  51.7 us
    ppermute x9, waiting for transfers between devices, attended(): home = [lax.ppermute(out[s], 'ctx', around(s)) for s in range(1, 4)]  46.7 us
    pallas_call x3, Pallas kernels, attend(): pl.pallas_call(_attend_kernel, out_shape=(jax.ShapeDtypeStruct((4, BLOCK,...  35.5 us
    pallas_call x3, Pallas kernels, mix(): pl.pallas_call(functools.partial(_mix_kernel, heads, len(added)), out_sha...  32 us
    ppermute x6, waiting for transfers between devices, over_row(): near = lax.ppermute(a, 'row', first)  31.9 us
    pallas_call x3, Pallas kernels, grad(): pl.pallas_call(functools.partial(_grad_kernel, count), grid=(4,), out_sha...  26.9 us
    all_to_all x3, waiting for transfers between devices, over_ctx(): return lax.all_to_all(jnp.concatenate(pieces), 'ctx', 0, 0, tiled=True)  22.9 us
    all_to_all x3, starting transfers between devices, over_ctx(): return lax.all_to_all(jnp.concatenate(pieces), 'ctx', 0, 0, tiled=True)  15.5 us
  transfers between devices with their start and end apart: 42, of which 18 were waited for; matrix products, arithmetic and copies ran while one was open for 4% of the time, Pallas kernels for 29%

profile of v1, /device:TPU:25, one launch (start us, length us, event | category | flops | bytes accessed | tf_op | source)
XLA Modules:
  0.0 353.2 jit_solution(14091460577643784733)
XLA Ops:
  15.6 18.3 %collective-permute-done = bf16[2,3,512,128]{3,2,1,0:T(8,128)(2,1)S(1)} collective-permute-done((bf16[2,3,512,128]{3,2,1,0:T(8,128)(2,1)}, bf16[2,3,512,128]{3,2,1,0:T(8,128)(2,1)S(1)}, u32[]{:S(2)}, u32[]{:S(2)}) %collective-permute-start) | collective-permute-done | bytes 786464 | tf_op jit(solution)/shard_map/ppermute | solution.py:458
  36.4 4.5 %all-to-all-start = ((bf16[4,3,512,128]{3,2,1,0:T(8,128)(2,1)}), bf16[4,3,512,128]{3,2,1,0:T(8,128)(2,1)S(1)}, u32[]{:S(2)}, u32[]{:S(2)}) async-start(bf16[4,3,512,128]{3,2,1,0:T(8,128)(2,1)} %pad_maximum_fusion.1), calls=%async_computation | async-start | bytes 3145728 | tf_op jit(solution)/shard_map/all_to_all | solution.py:463
  40.9 3.2 pack.4
  44.1 3.3 pack.5
  48.9 16.6 %collective-permute-done.1 = bf16[2,3,512,128]{3,2,1,0:T(8,128)(2,1)S(1)} collective-permute-done((bf16[2,3,512,128]{3,2,1,0:T(8,128)(2,1)}, bf16[2,3,512,128]{3,2,1,0:T(8,128)(2,1)S(1)}, u32[]{:S(2)}, u32[]{:S(2)}) %collective-permute-start.1) | collective-permute-done | bytes 786464 | tf_op jit(solution)/shard_map/ppermute | solution.py:458
  65.5 16.9 %collective-permute-done.2 = bf16[2,3,512,128]{3,2,1,0:T(8,128)(2,1)} collective-permute-done((bf16[2,3,512,128]{3,2,1,0:T(8,128)(2,1)}, bf16[2,3,512,128]{3,2,1,0:T(8,128)(2,1)}, u32[]{:S(2)}, u32[]{:S(2)}) %collective-permute-start.2) | collective-permute-done | bytes 786464 | tf_op jit(solution)/shard_map/ppermute | solution.py:458
  82.4 22.9 %all-to-all-done.refs_0_ = bf16[4,3,512,128]{3,2,1,0:T(8,128)(2,1)S(1)} async-done(((bf16[4,3,512,128]{3,2,1,0:T(8,128)(2,1)}), bf16[4,3,512,128]{3,2,1,0:T(8,128)(2,1)S(1)}, u32[]{:S(2)}, u32[]{:S(2)}) %all-to-all-start) | async-done | bytes 1572896 | tf_op jit(solution)/shard_map/all_to_all | solution.py:463
  106.8 6.3 %all-to-all-start.1 = ((bf16[4,3,512,128]{3,2,1,0:T(8,128)(2,1)}), bf16[4,3,512,128]{3,2,1,0:T(8,128)(2,1)S(1)}, u32[]{:S(2)}, u32[]{:S(2)}) async-start(bf16[4,3,512,128]{3,2,1,0:T(8,128)(2,1)} %pad_maximum_fusion.2), calls=%async_computation.1 | async-start | bytes 3145728 | tf_op jit(solution)/shard_map/all_to_all | solution.py:463
  114.5 3.3 collective-permute-done.4.refs_1_
  118.7 11.9 %attend.3 = (bf16[4,512,128]{2,1,0:T(8,128)(2,1)}, bf16[4,512,128]{2,1,0:T(8,128)(2,1)}) custom-call(s32[4]{0:T(128)} %pad_add_fusion.place, s32[8,8]{1,0:T(8,128)} %mask.5, bf16[4,3,512,128]{3,2,1,0:T(8,128)(2,1)} %copy-done.2, bf16[4,2,512,128]{3,2,1,0:T(8,128)(2,1)} %copy-done.19), custom_call_target="tpu_custom_call" | custom-call | flops 2684354560 | bytes 4194304 | tf_op jit(solution)/shard_map/attend/pallas_call | solution.py:233
  133.1 9.3 %collective-permute-done.8.refs_1_ = bf16[4,512,128]{2,1,0:T(8,128)(2,1)S(1)} collective-permute-done((bf16[4,512,128]{2,1,0:T(8,128)(2,1)}, bf16[4,512,128]{2,1,0:T(8,128)(2,1)S(1)}, u32[]{:S(2)}, u32[]{:S(2)}) %collective-permute-start.8) | collective-permute-done | bytes 524320 | tf_op jit(solution)/shard_map/ppermute | solution.py:443
  146.2 4.9 %collective-permute-done.5 = bf16[512,128]{1,0:T(8,128)(2,1)S(1)} collective-permute-done((bf16[512,128]{1,0:T(8,128)(2,1)S(1)}, bf16[512,128]{1,0:T(8,128)(2,1)S(1)}, u32[]{:S(2)}, u32[]{:S(2)}) %collective-permute-start.5) | collective-permute-done | bytes 131104 | tf_op jit(solution)/shard_map/ppermute | solution.py:469
  151.1 7.5 %collective-permute-done.6 = bf16[512,128]{1,0:T(8,128)(2,1)S(1)} collective-permute-done((bf16[512,128]{1,0:T(8,128)(2,1)S(1)}, bf16[512,128]{1,0:T(8,128)(2,1)S(1)}, u32[]{:S(2)}, u32[]{:S(2)}) %collective-permute-start.6) | collective-permute-done | bytes 131104 | tf_op jit(solution)/shard_map/ppermute | solution.py:469
  165.4 4.7 %all-to-all-start.2 = ((bf16[4,3,512,128]{3,2,1,0:T(8,128)(2,1)}), bf16[4,3,512,128]{3,2,1,0:T(8,128)(2,1)S(1)}, u32[]{:S(2)}, u32[]{:S(2)}) async-start(bf16[4,3,512,128]{3,2,1,0:T(8,128)(2,1)} %pad_maximum_fusion.3), calls=%async_computation.2 | async-start | bytes 3145728 | tf_op jit(solution)/shard_map/all_to_all | solution.py:463
  171.3 11.8 %attend.4 = (bf16[4,512,128]{2,1,0:T(8,128)(2,1)}, bf16[4,512,128]{2,1,0:T(8,128)(2,1)}) custom-call(s32[4]{0:T(128)} %pad_add_fusion.place, s32[8,8]{1,0:T(8,128)} %mask.5, bf16[4,3,512,128]{3,2,1,0:T(8,128)(2,1)} %copy-done.1, bf16[4,2,512,128]{3,2,1,0:T(8,128)(2,1)} %collective-permute-done.11.refs_1_), custom_call_target="tpu_custom_call" | custom-call | flops 2684354560 | bytes 4194304 | tf_op jit(solution)/shard_map/attend/pallas_call | solution.py:233
  186.1 10.6 %collective-permute-done.18.refs_5_ = bf16[4,512,128]{2,1,0:T(8,128)(2,1)S(1)} collective-permute-done((bf16[4,512,128]{2,1,0:T(8,128)(2,1)}, bf16[4,512,128]{2,1,0:T(8,128)(2,1)S(1)}, u32[]{:S(2)}, u32[]{:S(2)}) %collective-permute-start.18) | collective-permute-done | bytes 524320 | tf_op jit(solution)/shard_map/ppermute | solution.py:443
  198.4 9.5 %collective-permute-done.12 = bf16[512,128]{1,0:T(8,128)(2,1)S(1)} collective-permute-done((bf16[512,128]{1,0:T(8,128)(2,1)S(1)}, bf16[512,128]{1,0:T(8,128)(2,1)S(1)}, u32[]{:S(2)}, u32[]{:S(2)}) %collective-permute-start.12) | collective-permute-done | bytes 131104 | tf_op jit(solution)/shard_map/ppermute | solution.py:469
  207.9 6.7 %collective-permute-done.13 = bf16[512,128]{1,0:T(8,128)(2,1)S(1)} collective-permute-done((bf16[512,128]{1,0:T(8,128)(2,1)S(1)}, bf16[512,128]{1,0:T(8,128)(2,1)S(1)}, u32[]{:S(2)}, u32[]{:S(2)}) %collective-permute-start.13) | collective-permute-done | bytes 131104 | tf_op jit(solution)/shard_map/ppermute | solution.py:469
  214.6 5.6 %collective-permute-done.14 = bf16[512,128]{1,0:T(8,128)(2,1)S(1)} collective-permute-done((bf16[512,128]{1,0:T(8,128)(2,1)S(1)}, bf16[512,128]{1,0:T(8,128)(2,1)S(1)}, u32[]{:S(2)}, u32[]{:S(2)}) %collective-permute-start.14) | collective-permute-done | bytes 131104 | tf_op jit(solution)/shard_map/ppermute | solution.py:469
  224.8 3.7 %collective-permute-done.21.refs_1_ = bf16[4,2,512,128]{3,2,1,0:T(8,128)(2,1)S(1)} collective-permute-done((bf16[4,2,512,128]{3,2,1,0:T(8,128)(2,1)S(1)}, bf16[4,2,512,128]{3,2,1,0:T(8,128)(2,1)S(1)}, u32[]{:S(2)}, u32[]{:S(2)}) %collective-permute-start.21) | collective-permute-done | bytes 1048608 | tf_op jit(solution)/shard_map/ppermute | solution.py:466
  229.5 11.8 %attend.5 = (bf16[4,512,128]{2,1,0:T(8,128)(2,1)}, bf16[4,512,128]{2,1,0:T(8,128)(2,1)}) custom-call(s32[4]{0:T(128)} %pad_add_fusion.place, s32[8,8]{1,0:T(8,128)} %mask.5, bf16[4,3,512,128]{3,2,1,0:T(8,128)(2,1)} %copy-done, bf16[4,2,512,128]{3,2,1,0:T(8,128)(2,1)} %copy-done.18), custom_call_target="tpu_custom_call" | custom-call | flops 2684354560 | bytes 4194304 | tf_op jit(solution)/shard_map/attend/pallas_call | solution.py:233
  245.3 7.3 %collective-permute-done.22 = bf16[512,128]{1,0:T(8,128)(2,1)S(1)} collective-permute-done((bf16[512,128]{1,0:T(8,128)(2,1)S(1)}, bf16[512,128]{1,0:T(8,128)(2,1)S(1)}, u32[]{:S(2)}, u32[]{:S(2)}) %collective-permute-start.22) | collective-permute-done | bytes 131104 | tf_op jit(solution)/shard_map/ppermute | solution.py:469
  252.6 10.0 %mix.3.refs_6_ = f32[512,1536]{1,0:T(8,128)} custom-call(s32[4]{0:T(128)} %pad_add_fusion.place, bf16[4,512,128]{2,1,0:T(8,128)(2,1)} %pad_maximum_fusion.5.refs_0_, bf16[4,512,128]{2,1,0:T(8,128)(2,1)} %copy-done.16, bf16[4,512,128]{2,1,0:T(8,128)(2,1)} %copy-done.15, bf16[4,512,128]{2,1,0:T(8,128)(2,1)} %copy-done.17, bf16[3072,1536]{1,0:T(8,128)(2,1)} %refs_4_.11, ...), custom_call_target="tpu_custom_call" | custom-call | flops 3221225472 | bytes 9437184 | tf_op jit(solution)/shard_map/mix/pallas_call | solution.py:336
  262.6 5.2 %collective-permute-done.23 = bf16[512,128]{1,0:T(8,128)(2,1)S(1)} collective-permute-done((bf16[512,128]{1,0:T(8,128)(2,1)S(1)}, bf16[512,128]{1,0:T(8,128)(2,1)S(1)}, u32[]{:S(2)}, u32[]{:S(2)}) %collective-permute-start.23) | collective-permute-done | bytes 131104 | tf_op jit(solution)/shard_map/ppermute | solution.py:469
  269.4 7.2 %collective-permute-done.32.refs_1_.refs_9_ = bf16[4,512,128]{2,1,0:T(8,128)(2,1)S(1)} collective-permute-done((bf16[4,512,128]{2,1,0:T(8,128)(2,1)}, bf16[4,512,128]{2,1,0:T(8,128)(2,1)S(1)}, u32[]{:S(2)}, u32[]{:S(2)}) %collective-permute-start.32) | collective-permute-done | bytes 524320 | tf_op jit(solution)/shard_map/ppermute | solution.py:443
  277.8 9.1 %grad.3 = (bf16[512,768]{1,0:T(8,128)(2,1)}, f32[512,768]{1,0:T(8,128)}) custom-call(s32[4]{0:T(128)} %pad_add_fusion.place, bf16[4,512,128]{2,1,0:T(8,128)(2,1)} %get-tuple-element.91.refs_0_, bf16[4,512,128]{2,1,0:T(8,128)(2,1)} %copy-done.20, bf16[4,512,128]{2,1,0:T(8,128)(2,1)} %copy-done.21, bf16[4,512,128]{2,1,0:T(8,128)(2,1)} %collective-permute-done.10.refs_3_, ...), custom_call_target="tpu_custom_call" | custom-call | flops 3221225472 | bytes 11534336 | tf_op jit(solution)/shard_map/grad/pallas_call | solution.py:404
  288.3 4.8 %collective-permute-done.29.refs_2_ = bf16[4,512,128]{2,1,0:T(8,128)(2,1)S(1)} collective-permute-done((bf16[4,512,128]{2,1,0:T(8,128)(2,1)S(1)}, bf16[4,512,128]{2,1,0:T(8,128)(2,1)S(1)}, u32[]{:S(2)}, u32[]{:S(2)}) %collective-permute-start.29) | collective-permute-done | bytes 524320 | tf_op jit(solution)/shard_map/ppermute | solution.py:443
  295.2 6.5 %collective-permute-done.34.refs_3_.refs_11_ = bf16[4,512,128]{2,1,0:T(8,128)(2,1)} collective-permute-done((bf16[4,512,128]{2,1,0:T(8,128)(2,1)S(1)}, bf16[4,512,128]{2,1,0:T(8,128)(2,1)}, u32[]{:S(2)}, u32[]{:S(2)}) %collective-permute-start.34) | collective-permute-done | bytes 524320 | tf_op jit(solution)/shard_map/ppermute | solution.py:444
  301.7 11.6 %grad.5 = (bf16[768,768]{1,0:T(8,128)(2,1)}, f32[768,768]{1,0:T(8,128)}) custom-call(s32[4]{0:T(128)} %pad_add_fusion.place, bf16[4,512,128]{2,1,0:T(8,128)(2,1)} %get-tuple-element.91.refs_0_, bf16[4,512,128]{2,1,0:T(8,128)(2,1)} %copy-done.20, bf16[4,512,128]{2,1,0:T(8,128)(2,1)} %copy-done.21, bf16[4,512,128]{2,1,0:T(8,128)(2,1)} %collective-permute-done.10.refs_3_, ...), custom_call_target="tpu_custom_call" | custom-call | flops 4831838208 | bytes 15728640 | tf_op jit(solution)/shard_map/grad/pallas_call | solution.py:404
  313.5 6.2 %grad.4 = (bf16[256,768]{1,0:T(8,128)(2,1)}, f32[256,768]{1,0:T(8,128)}) custom-call(s32[4]{0:T(128)} %pad_add_fusion.place, bf16[4,512,128]{2,1,0:T(8,128)(2,1)} %get-tuple-element.102.refs_0_.refs_8_, bf16[4,512,128]{2,1,0:T(8,128)(2,1)} %copy-done.25, bf16[4,512,128]{2,1,0:T(8,128)(2,1)} %copy-done.26, ...), custom_call_target="tpu_custom_call" | custom-call | flops 1610612736 | bytes 7340032 | tf_op jit(solution)/shard_map/grad/pallas_call | solution.py:404
  320.6 11.3 %mix.4.refs_6_ = f32[512,1536]{1,0:T(8,128)} custom-call(s32[4]{0:T(128)} %pad_add_fusion.place, bf16[4,512,128]{2,1,0:T(8,128)(2,1)} %copy-done.4, bf16[4,512,128]{2,1,0:T(8,128)(2,1)} %copy-done.12, bf16[4,512,128]{2,1,0:T(8,128)(2,1)} %copy-done.11, bf16[4,512,128]{2,1,0:T(8,128)(2,1)} %copy-done.13, bf16[3072,1536]{1,0:T(8,128)(2,1)} %refs_4_.11, ...), custom_call_target="tpu_custom_call" | custom-call | flops 3221225472 | bytes 9437184 | tf_op jit(solution)/shard_map/mix/pallas_call | solution.py:336
  331.9 10.7 %mix.5 = bf16[512,1536]{1,0:T(8,128)(2,1)} custom-call(s32[4]{0:T(128)} %pad_add_fusion.place, bf16[4,512,128]{2,1,0:T(8,128)(2,1)} %copy-done.5, bf16[4,512,128]{2,1,0:T(8,128)(2,1)} %collective-permute-done.28.refs_1_, bf16[4,512,128]{2,1,0:T(8,128)(2,1)} %copy-done.14, bf16[4,512,128]{2,1,0:T(8,128)(2,1)} %collective-permute-done.30.refs_3_, ...), custom_call_target="tpu_custom_call" | custom-call | flops 3221225472 | bytes 9437184 | tf_op jit(solution)/shard_map/mix/pallas_call | solution.py:336
  (142 shorter events, 55.7 us)
Async XLA Ops:
  7.2 98.1 %all-gather.3.cloned.1.call-start = ((), (), s32[]{:S(2)}) async-start(), calls=%async_computation.3 | async-start | bytes 3932160 | tf_op jit(solution)/shard_map/all_gather | solution.py:472
  7.2 98.0 %collective-permute-start.3 = (bf16[3072,1536]{1,0:T(8,128)(2,1)}, bf16[3072,1536]{1,0:T(8,128)(2,1)}, u32[]{:S(2)}, u32[]{:S(2)}) collective-permute-start(bf16[3072,1536]{1,0:T(8,128)(2,1)} %refs_4_.11), channel_id=1, source_target_pairs={{0,4},{4,0},{1,5},{5,1},{2,6},{6,2},{3,7},{7,3},{8,12},{12,8},{9,1... | collective-permute-start | bytes 28311560 | tf_op jit(solution)/shard_map/ppermute | solution.py:477
  14.4 19.5 %collective-permute-start = (bf16[2,3,512,128]{3,2,1,0:T(8,128)(2,1)}, bf16[2,3,512,128]{3,2,1,0:T(8,128)(2,1)S(1)}, u32[]{:S(2)}, u32[]{:S(2)}) collective-permute-start(bf16[2,3,512,128]{3,2,1,0:T(8,128)(2,1)} %get-tuple-element.56), channel_id=1, source_target_pairs={{0,8},{8,0},{16,24},{24,16},{1,9},{9,1},{17,25},{25,17},{2,10},{10... | collective-permute-start | bytes 2359304 | tf_op jit(solution)/shard_map/ppermute | solution.py:458
  36.4 68.8 %all-to-all-start = ((bf16[4,3,512,128]{3,2,1,0:T(8,128)(2,1)}), bf16[4,3,512,128]{3,2,1,0:T(8,128)(2,1)S(1)}, u32[]{:S(2)}, u32[]{:S(2)}) async-start(bf16[4,3,512,128]{3,2,1,0:T(8,128)(2,1)} %pad_maximum_fusion.1), calls=%async_computation | async-start | bytes 3145728 | tf_op jit(solution)/shard_map/all_to_all | solution.py:463
  47.4 18.1 %collective-permute-start.1 = (bf16[2,3,512,128]{3,2,1,0:T(8,128)(2,1)}, bf16[2,3,512,128]{3,2,1,0:T(8,128)(2,1)S(1)}, u32[]{:S(2)}, u32[]{:S(2)}) collective-permute-start(bf16[2,3,512,128]{3,2,1,0:T(8,128)(2,1)} %get-tuple-element.61), channel_id=1, source_target_pairs={{0,8},{8,0},{16,24},{24,16},{1,9},{9,1},{17,25},{25,17},{2,10},{10... | collective-permute-start | bytes 2359304 | tf_op jit(solution)/shard_map/ppermute | solution.py:458
  48.6 33.7 %collective-permute-start.2 = (bf16[2,3,512,128]{3,2,1,0:T(8,128)(2,1)}, bf16[2,3,512,128]{3,2,1,0:T(8,128)(2,1)}, u32[]{:S(2)}, u32[]{:S(2)}) collective-permute-start(bf16[2,3,512,128]{3,2,1,0:T(8,128)(2,1)} %get-tuple-element.63), channel_id=1, source_target_pairs={{0,8},{8,0},{16,24},{24,16},{1,9},{9,1},{17,25},{25,17},{2,10},{10... | collective-permute-start | bytes 2359304 | tf_op jit(solution)/shard_map/ppermute | solution.py:458
  106.8 53.5 %all-to-all-start.1 = ((bf16[4,3,512,128]{3,2,1,0:T(8,128)(2,1)}), bf16[4,3,512,128]{3,2,1,0:T(8,128)(2,1)S(1)}, u32[]{:S(2)}, u32[]{:S(2)}) async-start(bf16[4,3,512,128]{3,2,1,0:T(8,128)(2,1)} %pad_maximum_fusion.2), calls=%async_computation.1 | async-start | bytes 3145728 | tf_op jit(solution)/shard_map/all_to_all | solution.py:463
  131.9 27.7 %collective-permute-start.9 = (bf16[4,512,128]{2,1,0:T(8,128)(2,1)}, bf16[4,512,128]{2,1,0:T(8,128)(2,1)S(1)}, u32[]{:S(2)}, u32[]{:S(2)}) collective-permute-start(bf16[4,512,128]{2,1,0:T(8,128)(2,1)} %get-tuple-element.91.refs_0_), channel_id=1, source_target_pairs={{0,16},{16,0},{8,24},{24,8},{1,17},{17,1},{9,25},{25,9},{2,18},{18... | collective-permute-start | bytes 1572872 | tf_op jit(solution)/shard_map/ppermute | solution.py:445
  142.4 18.0 %collective-permute-start.10 = (bf16[4,512,128]{2,1,0:T(8,128)(2,1)S(1)}, bf16[4,512,128]{2,1,0:T(8,128)(2,1)}, u32[]{:S(2)}, u32[]{:S(2)}) collective-permute-start(bf16[4,512,128]{2,1,0:T(8,128)(2,1)S(1)} %collective-permute-done.8.refs_1_), channel_id=1, source_target_pairs={{0,16},{16,0},{8,24},{24,8},{1,17},{17,1},{9,25},{25,9},{2,18},{18... | collective-permute-start | bytes 1572872 | tf_op jit(solution)/shard_map/ppermute | solution.py:444
  144.8 13.8 %collective-permute-start.6 = (bf16[512,128]{1,0:T(8,128)(2,1)S(1)}, bf16[512,128]{1,0:T(8,128)(2,1)S(1)}, u32[]{:S(2)}, u32[]{:S(2)}) collective-permute-start(bf16[512,128]{1,0:T(8,128)(2,1)S(1)} %get-tuple-element.126), channel_id=1, source_target_pairs={{0,2},{1,3},{2,0},{3,1},{4,6},{5,7},{6,4},{7,5},{8,10},{9,11},{10,... | collective-permute-start | bytes 393224 | tf_op jit(solution)/shard_map/ppermute | solution.py:469
  165.4 56.8 %all-to-all-start.2 = ((bf16[4,3,512,128]{3,2,1,0:T(8,128)(2,1)}), bf16[4,3,512,128]{3,2,1,0:T(8,128)(2,1)S(1)}, u32[]{:S(2)}, u32[]{:S(2)}) async-start(bf16[4,3,512,128]{3,2,1,0:T(8,128)(2,1)} %pad_maximum_fusion.3), calls=%async_computation.2 | async-start | bytes 3145728 | tf_op jit(solution)/shard_map/all_to_all | solution.py:463
  170.0 131.7 %all-gather.5.cloned.1.call-start = ((), (), s32[]{:S(2)}) async-start(), calls=%async_computation.4 | async-start | bytes 3932160 | tf_op jit(solution)/shard_map/all_gather | solution.py:488
  170.0 14.6 %collective-permute-start.16 = (bf16[4,512,128]{2,1,0:T(8,128)(2,1)S(1)}, bf16[4,512,128]{2,1,0:T(8,128)(2,1)S(1)}, u32[]{:S(2)}, u32[]{:S(2)}) collective-permute-start(bf16[4,512,128]{2,1,0:T(8,128)(2,1)S(1)} %copy-done.6), channel_id=1, source_target_pairs={{0,16},{16,0},{8,24},{24,8},{1,17},{17,1},{9,25},{25,9},{2,18},{18... | collective-permute-start | bytes 1572872 | tf_op jit(solution)/shard_map/ppermute | solution.py:443
  183.1 13.5 %collective-permute-start.18 = (bf16[4,512,128]{2,1,0:T(8,128)(2,1)}, bf16[4,512,128]{2,1,0:T(8,128)(2,1)S(1)}, u32[]{:S(2)}, u32[]{:S(2)}) collective-permute-start(bf16[4,512,128]{2,1,0:T(8,128)(2,1)} %get-tuple-element.95.refs_4_), channel_id=1, source_target_pairs={{0,8},{8,0},{16,24},{24,16},{1,9},{9,1},{17,25},{25,17},{2,10},{10... | collective-permute-start | bytes 1572872 | tf_op jit(solution)/shard_map/ppermute | solution.py:443
  184.4 35.9 %collective-permute-start.15 = (bf16[4,512,128]{2,1,0:T(8,128)(2,1)S(1)}, bf16[4,512,128]{2,1,0:T(8,128)(2,1)S(1)}, u32[]{:S(2)}, u32[]{:S(2)}) collective-permute-start(bf16[4,512,128]{2,1,0:T(8,128)(2,1)S(1)} %copy-done.6), channel_id=1, source_target_pairs={{0,8},{8,0},{16,24},{24,16},{1,9},{9,1},{17,25},{25,17},{2,10},{10... | collective-permute-start | bytes 1572872 | tf_op jit(solution)/shard_map/ppermute | solution.py:445
  184.7 35.7 %collective-permute-start.17 = (bf16[4,512,128]{2,1,0:T(8,128)(2,1)S(1)}, bf16[4,512,128]{2,1,0:T(8,128)(2,1)S(1)}, u32[]{:S(2)}, u32[]{:S(2)}) collective-permute-start(bf16[4,512,128]{2,1,0:T(8,128)(2,1)S(1)} %collective-permute-done.16.refs_2_), channel_id=1, source_target_pairs={{0,8},{8,0},{16,24},{24,16},{1,9},{9,1},{17,25},{25,17},{2,10},{10... | collective-permute-start | bytes 1572872 | tf_op jit(solution)/shard_map/ppermute | solution.py:444
  185.9 34.5 %collective-permute-start.19 = (bf16[4,512,128]{2,1,0:T(8,128)(2,1)}, bf16[4,512,128]{2,1,0:T(8,128)(2,1)S(1)}, u32[]{:S(2)}, u32[]{:S(2)}) collective-permute-start(bf16[4,512,128]{2,1,0:T(8,128)(2,1)} %get-tuple-element.95.refs_4_), channel_id=1, source_target_pairs={{0,16},{16,0},{8,24},{24,8},{1,17},{17,1},{9,25},{25,9},{2,18},{18... | collective-permute-start | bytes 1572872 | tf_op jit(solution)/shard_map/ppermute | solution.py:445
  196.7 25.5 %collective-permute-start.20 = (bf16[4,512,128]{2,1,0:T(8,128)(2,1)S(1)}, bf16[4,512,128]{2,1,0:T(8,128)(2,1)}, u32[]{:S(2)}, u32[]{:S(2)}) collective-permute-start(bf16[4,512,128]{2,1,0:T(8,128)(2,1)S(1)} %collective-permute-done.18.refs_5_), channel_id=1, source_target_pairs={{0,16},{16,0},{8,24},{24,8},{1,17},{17,1},{9,25},{25,9},{2,18},{18... | collective-permute-start | bytes 1572872 | tf_op jit(solution)/shard_map/ppermute | solution.py:444
  223.6 20.2 %collective-permute-start.26 = (bf16[4,512,128]{2,1,0:T(8,128)(2,1)S(1)}, bf16[4,512,128]{2,1,0:T(8,128)(2,1)S(1)}, u32[]{:S(2)}, u32[]{:S(2)}) collective-permute-start(bf16[4,512,128]{2,1,0:T(8,128)(2,1)S(1)} %pad_maximum_fusion.6.refs_0_), channel_id=1, source_target_pairs={{0,16},{16,0},{8,24},{24,8},{1,17},{17,1},{9,25},{25,9},{2,18},{18... | collective-permute-start | bytes 1572872 | tf_op jit(solution)/shard_map/ppermute | solution.py:443
  242.5 26.6 %collective-permute-start.25 = (bf16[4,512,128]{2,1,0:T(8,128)(2,1)S(1)}, bf16[4,512,128]{2,1,0:T(8,128)(2,1)S(1)}, u32[]{:S(2)}, u32[]{:S(2)}) collective-permute-start(bf16[4,512,128]{2,1,0:T(8,128)(2,1)S(1)} %pad_maximum_fusion.6.refs_0_), channel_id=1, source_target_pairs={{0,8},{8,0},{16,24},{24,16},{1,9},{9,1},{17,25},{25,17},{2,10},{10... | collective-permute-start | bytes 1572872 | tf_op jit(solution)/shard_map/ppermute | solution.py:445
  243.8 25.4 %collective-permute-start.27 = (bf16[4,512,128]{2,1,0:T(8,128)(2,1)S(1)}, bf16[4,512,128]{2,1,0:T(8,128)(2,1)S(1)}, u32[]{:S(2)}, u32[]{:S(2)}) collective-permute-start(bf16[4,512,128]{2,1,0:T(8,128)(2,1)S(1)} %collective-permute-done.26.refs_2_), channel_id=1, source_target_pairs={{0,8},{8,0},{16,24},{24,16},{1,9},{9,1},{17,25},{25,17},{2,10},{10... | collective-permute-start | bytes 1572872 | tf_op jit(solution)/shard_map/ppermute | solution.py:444
  244.1 32.6 %collective-permute-start.32 = (bf16[4,512,128]{2,1,0:T(8,128)(2,1)}, bf16[4,512,128]{2,1,0:T(8,128)(2,1)S(1)}, u32[]{:S(2)}, u32[]{:S(2)}) collective-permute-start(bf16[4,512,128]{2,1,0:T(8,128)(2,1)} %get-tuple-element.102.refs_0_.refs_8_), channel_id=1, source_target_pairs={{0,8},{8,0},{16,24},{24,16},{1,9},{9,1},{17,25},{25,17},{2,10},{10... | collective-permute-start | bytes 1572872 | tf_op jit(solution)/shard_map/ppermute | solution.py:443
  245.3 22.5 %collective-permute-start.23 = (bf16[512,128]{1,0:T(8,128)(2,1)S(1)}, bf16[512,128]{1,0:T(8,128)(2,1)S(1)}, u32[]{:S(2)}, u32[]{:S(2)}) collective-permute-start(bf16[512,128]{1,0:T(8,128)(2,1)S(1)} %get-tuple-element.118), channel_id=1, source_target_pairs={{0,2},{1,3},{2,0},{3,1},{4,6},{5,7},{6,4},{7,5},{8,10},{9,11},{10,... | collective-permute-start | bytes 393224 | tf_op jit(solution)/shard_map/ppermute | solution.py:469
  252.6 16.5 %collective-permute-start.24 = (bf16[512,128]{1,0:T(8,128)(2,1)S(1)}, bf16[512,128]{1,0:T(8,128)(2,1)S(1)}, u32[]{:S(2)}, u32[]{:S(2)}) collective-permute-start(bf16[512,128]{1,0:T(8,128)(2,1)S(1)} %get-tuple-element.117), channel_id=1, source_target_pairs={{0,3},{1,0},{2,1},{3,2},{4,7},{5,4},{6,5},{7,6},{8,11},{9,8},{10,9... | collective-permute-start | bytes 393224 | tf_op jit(solution)/shard_map/ppermute | solution.py:469
  267.8 26.6 %collective-permute-start.33 = (bf16[4,512,128]{2,1,0:T(8,128)(2,1)S(1)}, bf16[4,512,128]{2,1,0:T(8,128)(2,1)S(1)}, u32[]{:S(2)}, u32[]{:S(2)}) collective-permute-start(bf16[4,512,128]{2,1,0:T(8,128)(2,1)S(1)} %copy-done.24), channel_id=1, source_target_pairs={{0,16},{16,0},{8,24},{24,8},{1,17},{17,1},{9,25},{25,9},{2,18},{18... | collective-permute-start | bytes 1572872 | tf_op jit(solution)/shard_map/ppermute | solution.py:445
  269.2 24.0 %collective-permute-start.29 = (bf16[4,512,128]{2,1,0:T(8,128)(2,1)S(1)}, bf16[4,512,128]{2,1,0:T(8,128)(2,1)S(1)}, u32[]{:S(2)}, u32[]{:S(2)}) collective-permute-start(bf16[4,512,128]{2,1,0:T(8,128)(2,1)S(1)} %pad_maximum_fusion.7.refs_0_), channel_id=1, source_target_pairs={{0,16},{16,0},{8,24},{24,8},{1,17},{17,1},{9,25},{25,9},{2,18},{18... | collective-permute-start | bytes 1572872 | tf_op jit(solution)/shard_map/ppermute | solution.py:443
  276.7 25.0 %collective-permute-start.34 = (bf16[4,512,128]{2,1,0:T(8,128)(2,1)S(1)}, bf16[4,512,128]{2,1,0:T(8,128)(2,1)}, u32[]{:S(2)}, u32[]{:S(2)}) collective-permute-start(bf16[4,512,128]{2,1,0:T(8,128)(2,1)S(1)} %collective-permute-done.32.refs_1_.refs_9_), channel_id=1, source_target_pairs={{0,16},{16,0},{8,24},{24,8},{1,17},{17,1},{9,25},{25,9},{2,18},{18... | collective-permute-start | bytes 1572872 | tf_op jit(solution)/shard_map/ppermute | solution.py:444
  287.0 26.4 %collective-permute-start.31 = (bf16[512,768]{1,0:T(8,128)(2,1)}, bf16[512,768]{1,0:T(8,128)(2,1)S(1)}, u32[]{:S(2)}, u32[]{:S(2)}) collective-permute-start(bf16[512,768]{1,0:T(8,128)(2,1)} %get-tuple-element.101), channel_id=1, source_target_pairs={{0,4},{4,0},{1,5},{5,1},{2,6},{6,2},{3,7},{7,3},{8,12},{12,8},{9,1... | collective-permute-start | bytes 2359304 | tf_op jit(solution)/shard_map/ppermute | solution.py:497
  287.1 44.8 %collective-permute-start.28 = (bf16[4,512,128]{2,1,0:T(8,128)(2,1)S(1)}, bf16[4,512,128]{2,1,0:T(8,128)(2,1)}, u32[]{:S(2)}, u32[]{:S(2)}) collective-permute-start(bf16[4,512,128]{2,1,0:T(8,128)(2,1)S(1)} %pad_maximum_fusion.7.refs_0_), channel_id=1, source_target_pairs={{0,8},{8,0},{16,24},{24,16},{1,9},{9,1},{17,25},{25,17},{2,10},{10... | collective-permute-start | bytes 1572872 | tf_op jit(solution)/shard_map/ppermute | solution.py:445
  293.1 38.7 %collective-permute-start.30 = (bf16[4,512,128]{2,1,0:T(8,128)(2,1)S(1)}, bf16[4,512,128]{2,1,0:T(8,128)(2,1)}, u32[]{:S(2)}, u32[]{:S(2)}) collective-permute-start(bf16[4,512,128]{2,1,0:T(8,128)(2,1)S(1)} %collective-permute-done.29.refs_2_), channel_id=1, source_target_pairs={{0,8},{8,0},{16,24},{24,16},{1,9},{9,1},{17,25},{25,17},{2,10},{10... | collective-permute-start | bytes 1572872 | tf_op jit(solution)/shard_map/ppermute | solution.py:444
  313.3 29.5 %collective-permute-start.36 = (bf16[768,768]{1,0:T(8,128)(2,1)}, bf16[768,768]{1,0:T(8,128)(2,1)S(1)}, u32[]{:S(2)}, u32[]{:S(2)}) collective-permute-start(bf16[768,768]{1,0:T(8,128)(2,1)} %get-tuple-element.107), channel_id=1, source_target_pairs={{0,4},{4,0},{1,5},{5,1},{2,6},{6,2},{3,7},{7,3},{8,12},{12,8},{9,1... | collective-permute-start | bytes 3538952 | tf_op jit(solution)/shard_map/ppermute | solution.py:497
  319.7 22.9 %collective-permute-start.35 = (bf16[256,768]{1,0:T(8,128)(2,1)}, bf16[256,768]{1,0:T(8,128)(2,1)S(1)}, u32[]{:S(2)}, u32[]{:S(2)}) collective-permute-start(bf16[256,768]{1,0:T(8,128)(2,1)} %get-tuple-element.104), channel_id=1, source_target_pairs={{0,4},{4,0},{1,5},{5,1},{2,6},{6,2},{3,7},{7,3},{8,12},{12,8},{9,1... | collective-permute-start | bytes 1179656 | tf_op jit(solution)/shard_map/ppermute | solution.py:497
  (37 other events, 433.6 us)
Sparse Core Ops, SparseCore 0:
  10.7 92.6 all-gather.2
  222.3 75.1 all-gather.4

commit v2 on v1

--- a/solution.py
+++ b/solution.py
@@ -267,7 +267,7 @@
     parts, (w_own, w_other) = refs[:count], refs[count : count + 2]
     sums = refs[count + 2] if added else None
     out = refs[count + 2 + added]
-    a_s, w_s, sum_s, a_sem, w_sem = refs[count + 3 + added :]
+    a_s, w_s, sum_s, a_sem, w_sem, s_sem = refs[count + 3 + added :]
     x, y, c, z = place[0], place[1], place[2], place[3]
     depth = len(heads) * HD
 
@@ -294,31 +294,41 @@
             pl.when(yy == c)(weight(side, block, w_own).start)
             pl.when(yy != c)(weight(side, block, w_other).start)
 
+    if added:
+        known = pltpu.make_async_copy(sums, sum_s, s_sem)
+        known.start()
     fetch(0)
     fetch(1)
     width = 512
-    piece = 4 * depth
-    for side in range(4):
-        if 0 < side < 3:
-            fetch(side + 1)
-        for n in range(len(heads)):
-            attended(n, side).wait()
-        for block in range(4):
-            weight(side, block, w_own).wait()
-
-        def tile(t, _, side=side):
+    piece = 8 * depth
+    for half in range(2):
+        for side in (2 * half, 2 * half + 1):
+            if half == 0:
+                fetch(side + 2)
+            for n in range(len(heads)):
+                attended(n, side).wait()
+            for block in range(4):
+                weight(side, block, w_own).wait()
+        if half == 0 and added:
+            known.wait()
+
+        def tile(t, _, half=half):
             cut = pl.ds(pl.multiple_of(t * width, width), width)
             rows = jnp.concatenate(
-                [a_s[side, block, n] for block in range(4) for n in range(len(heads))], axis=1
+                [
+                    a_s[side, block, n]
+                    for side in (2 * half, 2 * half + 1)
+                    for block in range(4)
+                    for n in range(len(heads))
+                ],
+                axis=1,
             )
             term = jnp.dot(
-                rows, w_s[side * piece : (side + 1) * piece, cut], preferred_element_type=jnp.float32
+                rows, w_s[half * piece : (half + 1) * piece, cut], preferred_element_type=jnp.float32
             )
-            if side > 0:
+            if half > 0 or added:
                 term += sum_s[:, cut]
-            elif added:
-                term += sums[:, cut]
-            if side < 3:
+            if half == 0:
                 sum_s[:, cut] = term
             else:
                 out[:, cut] = term.astype(out.dtype)
@@ -327,8 +337,7 @@
         lax.fori_loop(0, out.shape[1] // width, tile, 0)
 
 
-def mix(place, head, parts, w_own, w_other, sums, kind):
-    heads = (head,)
+def mix(place, heads, parts, w_own, w_other, sums, kind):
     columns = w_own.shape[1]
     depth = 16 * len(heads) * HD
     vmem = pl.BlockSpec(memory_space=pltpu.VMEM)
@@ -336,7 +345,7 @@
     return pl.pallas_call(
         functools.partial(_mix_kernel, heads, len(added)),
         out_shape=jax.ShapeDtypeStruct((BLOCK, columns), kind),
-        in_specs=[SMEM] + [ANY] * (len(parts) + 2) + [vmem] * len(added),
+        in_specs=[SMEM] + [ANY] * (len(parts) + 2) + [ANY] * len(added),
         out_specs=vmem,
         scratch_shapes=[
             pltpu.VMEM((4, 4, len(heads), BLOCK, HD), jnp.bfloat16),
@@ -344,6 +353,7 @@
             pltpu.VMEM((BLOCK, columns), jnp.float32),
             pltpu.SemaphoreType.DMA((4 * len(heads),)),
             pltpu.SemaphoreType.DMA((16,)),
+            pltpu.SemaphoreType.DMA,
         ],
         compiler_params=_params(VMEM_MIB),
         cost_estimate=pl.CostEstimate(
@@ -363,12 +373,18 @@
     def _():
         rows = pltpu.make_async_copy(cot, right, r_sem)
         rows.start()
-        for n, ref in enumerate(parts):
-            head, dx, dy = n // 4, n % 2, n // 2 % 2
-            mine = (lax.rem(y + dy, 2) == c).astype(jnp.int32)
-            at = 2 * count * mine + count * lax.rem(x + dx, 2) + head
-            pltpu.make_async_copy(ref, left.at[at], l_sem.at[at]).start()
+
+        def start(turn):
+            for n, ref in enumerate(parts):
+                head, dx, dy = n // 4, n % 2, n // 2 % 2
+                mine = (lax.rem(y + dy, 2) == c).astype(jnp.int32)
+                at = 2 * count * mine + count * lax.rem(x + dx, 2) + head
+                copy = pltpu.make_async_copy(ref, left.at[at], l_sem.at[at])
+                pl.when(mine == turn)(copy.start)
+
+        start(0)
         rows.wait()
+        start(1)
 
     for n in range(count):
         at = count * step + n
@@ -431,6 +447,7 @@
 Y_SWAP = [(0, 2), (2, 0), (1, 3), (3, 1)]
 
 
+XY_SWAP = [(0, 3), (3, 0), (1, 2), (2, 1)]
 OTHER_CORE = [(0, 1), (1, 0)]
 
 
@@ -438,7 +455,9 @@
     return [(i, (i + shift) % 4) for i in range(4)]
 
 
-def over_row(a, x_first):
+def over_row(a, x_first=None):
+    if x_first is None:
+        return [a] + [lax.ppermute(a, "row", pairs) for pairs in (X_SWAP, Y_SWAP, XY_SWAP)]
     first, second = (X_SWAP, Y_SWAP) if x_first else (Y_SWAP, X_SWAP)
     near = lax.ppermute(a, "row", first)
     far = lax.ppermute(near, "row", second)
@@ -462,12 +481,12 @@
         pieces = [jnp.where(x == 0, kept, got), jnp.where(x == 0, got, kept)]
         return lax.all_to_all(jnp.concatenate(pieces), "ctx", 0, 0, tiled=True)
 
-    def attended(h, own, before):
+    def attended(h, own, beside):
         other = lax.ppermute(own[:, 1:], "col", [(0, 1)])
-        other, before = lax.optimization_barrier((other, before))
         out, out_t = attend(place, block_mask, own, other)
+        out, out_t, beside = lax.optimization_barrier((out, out_t, beside))
         home = [lax.ppermute(out[s], "ctx", around(s)) for s in range(1, 4)]
-        return jnp.stack([out[0]] + home), over_row(out_t, True), before
+        return jnp.stack([out[0]] + home), over_row(out_t, True if h < 2 else None), beside
 
     first_cot = lax.all_gather(cotangent[:, :cut], "ctx", axis=0, tiled=True)
     pair = exchanged(0, place)
@@ -486,24 +505,27 @@
         (own2, cotangent[:, cut:], home1, mix0, grad1)
     )
     last_cot = lax.all_gather(last_half, "ctx", axis=0, tiled=True)
-    mix1 = over_row(home1, False)
-    home2, grad2, _ = attended(2, own2, ())
-    sums = mix(place, 0, mix0, out_weight, w_other, None, jnp.float32)
-    home2, mix1, sums = lax.optimization_barrier((home2, mix1, sums))
-    mix2 = over_row(home2, False)
-
-    def summed(parts, cot):
-        sent, kept = grad(place, parts, cot)
+    mix1 = [home1, lax.ppermute(home1, "row", X_SWAP), lax.ppermute(home1, "row", Y_SWAP)]
+    home2, grad2, mix1 = attended(2, own2, mix1)
+    mix1.append(lax.ppermute(mix1[2], "row", X_SWAP))
+    home2, mix1, grad2[1:3] = lax.optimization_barrier((home2, mix1, grad2[1:3]))
+    early = grad(place, grad0 + grad1, first_cot)
+    mix2 = over_row(home2)
+
+    def summed(pairs):
+        sent = jnp.concatenate([p[0].reshape(2, -1, cut) for p in pairs], axis=1)
+        kept = jnp.concatenate([p[1].reshape(2, -1, cut) for p in pairs], axis=1)
         received = lax.ppermute(sent, "col", OTHER_CORE)
-        done = (kept + received.astype(jnp.float32)).astype(jnp.bfloat16)
-        return done.reshape(2, -1, cot.shape[1])
-
-    early = summed(grad0 + grad1, first_cot)
-    sums = mix(place, 1, mix1, out_weight, w_other, sums, jnp.float32)
-    late = summed(grad2, first_cot)
-    mixed_out = mix(place, 2, mix2, out_weight, w_other, sums, jnp.bfloat16)
-    last = summed(grad0 + grad1 + grad2, last_cot)
-    grad_weight = jnp.concatenate([jnp.concatenate([early, late], axis=1), last], axis=2)
+        return (kept + received.astype(jnp.float32)).astype(jnp.bfloat16)
+
+    sums = mix(place, (0, 1), mix0 + mix1, out_weight, w_other, None, jnp.float32)
+    sums, grad2 = lax.optimization_barrier((sums, grad2))
+    sums, early, grad2 = lax.optimization_barrier((sums, early, grad2))
+    late = grad(place, grad2, first_cot)
+    mix2, last_cot = lax.optimization_barrier((mix2, last_cot))
+    last = grad(place, grad0 + grad1 + grad2, last_cot)
+    mixed_out = mix(place, (2,), mix2, out_weight, w_other, sums, jnp.bfloat16)
+    grad_weight = jnp.concatenate([summed([early, late]), summed([last])], axis=2)
     grad_weight = grad_weight.reshape(-1, columns)
     return (mixed_out, grad_weight)
 

time: 356 us -> 339 us (0.952)
  Pallas kernels: 104 us -> 92.8 us
  waiting for transfers between devices: 167 us -> 158 us
    ppermute x6 -> x3, waiting for transfers between devices: 31.9 us -> 19.8 us  [over_row(): near = lax.ppermute(a, 'row', first)]
    ppermute x0 -> x9, starting transfers between devices: none -> 10 us  [the longest x6 6.27 us: over_row(): lax.ppermute(a, 'row', pairs)]
    pallas_call x3 -> x2, Pallas kernels: 32 us -> 24.2 us  [mix(): pl.pallas_call(functools.partial(_mix_kernel, heads, len(added)), out_sha...]
    ppermute x0 -> x9, waiting for transfers between devices: none -> 7.7 us  [the longest x6 7.69 us: over_row(): lax.ppermute(a, 'row', pairs)]
    ppermute x6 -> x3, waiting for transfers between devices: 6.47 us -> 0.01 us  [over_row(): far = lax.ppermute(near, 'row', second)]
    ppermute x6 -> x3, starting transfers between devices: 5.49 us -> 1.72 us  [over_row(): next_to = lax.ppermute(a, 'row', second)]
  transfers between devices with their start and end apart: 42 -> 41, of which waited for: 18 -> 16; matrix products, arithmetic and copies ran while one was open for 4% -> 5% of each run, Pallas kernels for 29% -> 28%
where the time goes in v2:
time: 339 us; the launch traced here: 336 us
  waiting for transfers between devices  158 us (47%)
  Pallas kernels  92.8 us (27%)
  starting transfers between devices  44.2 us (13%)
  local copies, waits for them, and re-layouts  14.7 us (4%)
  between operations  14.6 us (4%)
  other arithmetic  12.6 us (4%)
    ppermute x3, waiting for transfers between devices, exchanged(): got = lax.ppermute(send, 'row', X_SWAP)  51.7 us
    ppermute x9, waiting for transfers between devices, attended(): home = [lax.ppermute(out[s], 'ctx', around(s)) for s in range(1, 4)]  49.8 us
    pallas_call x3, Pallas kernels, attend(): pl.pallas_call(_attend_kernel, out_shape=(jax.ShapeDtypeStruct((4, BLOCK,...  32.7 us
    pallas_call x3, Pallas kernels, grad(): pl.pallas_call(functools.partial(_grad_kernel, count), grid=(4,), out_sha...  26.2 us
    pallas_call x2, Pallas kernels, mix(): pl.pallas_call(functools.partial(_mix_kernel, heads, len(added)), out_sha...  24.2 us
    all_to_all x3, waiting for transfers between devices, over_ctx(): return lax.all_to_all(jnp.concatenate(pieces), 'ctx', 0, 0, tiled=True)  22.9 us
    ppermute x3, waiting for transfers between devices, over_row(): near = lax.ppermute(a, 'row', first)  19.8 us
    all_to_all x3, starting transfers between devices, over_ctx(): return lax.all_to_all(jnp.concatenate(pieces), 'ctx', 0, 0, tiled=True)  15.5 us
  transfers between devices with their start and end apart: 41, of which 16 were waited for; matrix products, arithmetic and copies ran while one was open for 5% of the time, Pallas kernels for 28%

profile of v2, /device:TPU:25, one launch (start us, length us, event | category | flops | bytes accessed | tf_op | source)
XLA Modules:
  0.0 336.4 jit_solution(9508687659430618032)
XLA Ops:
  7.9 2.6 fusion.1
  11.2 3.2 pack.3
  15.6 18.3 %collective-permute-done = bf16[2,3,512,128]{3,2,1,0:T(8,128)(2,1)S(1)} collective-permute-done((bf16[2,3,512,128]{3,2,1,0:T(8,128)(2,1)}, bf16[2,3,512,128]{3,2,1,0:T(8,128)(2,1)S(1)}, u32[]{:S(2)}, u32[]{:S(2)}) %collective-permute-start) | collective-permute-done | bytes 786464 | tf_op jit(solution)/shard_map/ppermute | solution.py:477
  36.4 4.5 %all-to-all-start = ((bf16[4,3,512,128]{3,2,1,0:T(8,128)(2,1)}), bf16[4,3,512,128]{3,2,1,0:T(8,128)(2,1)S(1)}, u32[]{:S(2)}, u32[]{:S(2)}) async-start(bf16[4,3,512,128]{3,2,1,0:T(8,128)(2,1)} %pad_maximum_fusion.1), calls=%async_computation | async-start | bytes 3145728 | tf_op jit(solution)/shard_map/all_to_all | solution.py:482
  40.9 3.2 pack.4
  44.1 3.3 pack.5
  48.9 16.6 %collective-permute-done.1 = bf16[2,3,512,128]{3,2,1,0:T(8,128)(2,1)S(1)} collective-permute-done((bf16[2,3,512,128]{3,2,1,0:T(8,128)(2,1)}, bf16[2,3,512,128]{3,2,1,0:T(8,128)(2,1)S(1)}, u32[]{:S(2)}, u32[]{:S(2)}) %collective-permute-start.1) | collective-permute-done | bytes 786464 | tf_op jit(solution)/shard_map/ppermute | solution.py:477
  65.5 16.9 %collective-permute-done.2 = bf16[2,3,512,128]{3,2,1,0:T(8,128)(2,1)} collective-permute-done((bf16[2,3,512,128]{3,2,1,0:T(8,128)(2,1)}, bf16[2,3,512,128]{3,2,1,0:T(8,128)(2,1)}, u32[]{:S(2)}, u32[]{:S(2)}) %collective-permute-start.2) | collective-permute-done | bytes 786464 | tf_op jit(solution)/shard_map/ppermute | solution.py:477
  82.4 22.9 %all-to-all-done.refs_0_ = bf16[4,3,512,128]{3,2,1,0:T(8,128)(2,1)S(1)} async-done(((bf16[4,3,512,128]{3,2,1,0:T(8,128)(2,1)}), bf16[4,3,512,128]{3,2,1,0:T(8,128)(2,1)S(1)}, u32[]{:S(2)}, u32[]{:S(2)}) %all-to-all-start) | async-done | bytes 1572896 | tf_op jit(solution)/shard_map/all_to_all | solution.py:482
  106.8 6.3 %all-to-all-start.1 = ((bf16[4,3,512,128]{3,2,1,0:T(8,128)(2,1)}), bf16[4,3,512,128]{3,2,1,0:T(8,128)(2,1)S(1)}, u32[]{:S(2)}, u32[]{:S(2)}) async-start(bf16[4,3,512,128]{3,2,1,0:T(8,128)(2,1)} %pad_maximum_fusion.2), calls=%async_computation.1 | async-start | bytes 3145728 | tf_op jit(solution)/shard_map/all_to_all | solution.py:482
  114.5 3.3 collective-permute-done.4.refs_1_
  118.7 10.9 %attend.3 = (bf16[4,512,128]{2,1,0:T(8,128)(2,1)}, bf16[4,512,128]{2,1,0:T(8,128)(2,1)}) custom-call(s32[4]{0:T(128)} %pad_add_fusion.place, s32[8,8]{1,0:T(8,128)} %mask.5, bf16[4,3,512,128]{3,2,1,0:T(8,128)(2,1)} %copy-done.2, bf16[4,2,512,128]{3,2,1,0:T(8,128)(2,1)} %copy-done.21), custom_call_target="tpu_custom_call" | custom-call | flops 2684354560 | bytes 4194304 | tf_op jit(solution)/shard_map/attend/pallas_call | solution.py:233
  132.1 9.3 %collective-permute-done.8.refs_1_ = bf16[4,512,128]{2,1,0:T(8,128)(2,1)S(1)} collective-permute-done((bf16[4,512,128]{2,1,0:T(8,128)(2,1)}, bf16[4,512,128]{2,1,0:T(8,128)(2,1)S(1)}, u32[]{:S(2)}, u32[]{:S(2)}) %collective-permute-start.8) | collective-permute-done | bytes 524320 | tf_op jit(solution)/shard_map/ppermute | solution.py:462
  145.6 5.4 %collective-permute-done.5 = bf16[512,128]{1,0:T(8,128)(2,1)S(1)} collective-permute-done((bf16[512,128]{1,0:T(8,128)(2,1)S(1)}, bf16[512,128]{1,0:T(8,128)(2,1)S(1)}, u32[]{:S(2)}, u32[]{:S(2)}) %collective-permute-start.5) | collective-permute-done | bytes 131104 | tf_op jit(solution)/shard_map/ppermute | solution.py:488
  150.9 7.7 %collective-permute-done.6 = bf16[512,128]{1,0:T(8,128)(2,1)S(1)} collective-permute-done((bf16[512,128]{1,0:T(8,128)(2,1)S(1)}, bf16[512,128]{1,0:T(8,128)(2,1)S(1)}, u32[]{:S(2)}, u32[]{:S(2)}) %collective-permute-start.6) | collective-permute-done | bytes 131104 | tf_op jit(solution)/shard_map/ppermute | solution.py:488
  165.3 4.7 %all-to-all-start.2 = ((bf16[4,3,512,128]{3,2,1,0:T(8,128)(2,1)}), bf16[4,3,512,128]{3,2,1,0:T(8,128)(2,1)S(1)}, u32[]{:S(2)}, u32[]{:S(2)}) async-start(bf16[4,3,512,128]{3,2,1,0:T(8,128)(2,1)} %pad_maximum_fusion.3), calls=%async_computation.2 | async-start | bytes 3145728 | tf_op jit(solution)/shard_map/all_to_all | solution.py:482
  171.2 10.9 %attend.4 = (bf16[4,512,128]{2,1,0:T(8,128)(2,1)}, bf16[4,512,128]{2,1,0:T(8,128)(2,1)}) custom-call(s32[4]{0:T(128)} %pad_add_fusion.place, s32[8,8]{1,0:T(8,128)} %mask.5, bf16[4,3,512,128]{3,2,1,0:T(8,128)(2,1)} %copy-done.1, bf16[4,2,512,128]{3,2,1,0:T(8,128)(2,1)} %collective-permute-done.11.refs_1_), custom_call_target="tpu_custom_call" | custom-call | flops 2684354560 | bytes 4194304 | tf_op jit(solution)/shard_map/attend/pallas_call | solution.py:233
  185.1 10.5 %collective-permute-done.18.refs_5_ = bf16[4,512,128]{2,1,0:T(8,128)(2,1)S(1)} collective-permute-done((bf16[4,512,128]{2,1,0:T(8,128)(2,1)}, bf16[4,512,128]{2,1,0:T(8,128)(2,1)S(1)}, u32[]{:S(2)}, u32[]{:S(2)}) %collective-permute-start.18) | collective-permute-done | bytes 524320 | tf_op jit(solution)/shard_map/ppermute | solution.py:462
  197.4 10.2 %collective-permute-done.12 = bf16[512,128]{1,0:T(8,128)(2,1)S(1)} collective-permute-done((bf16[512,128]{1,0:T(8,128)(2,1)S(1)}, bf16[512,128]{1,0:T(8,128)(2,1)S(1)}, u32[]{:S(2)}, u32[]{:S(2)}) %collective-permute-start.12) | collective-permute-done | bytes 131104 | tf_op jit(solution)/shard_map/ppermute | solution.py:488
  207.6 6.9 %collective-permute-done.13 = bf16[512,128]{1,0:T(8,128)(2,1)S(1)} collective-permute-done((bf16[512,128]{1,0:T(8,128)(2,1)S(1)}, bf16[512,128]{1,0:T(8,128)(2,1)S(1)}, u32[]{:S(2)}, u32[]{:S(2)}) %collective-permute-start.13) | collective-permute-done | bytes 131104 | tf_op jit(solution)/shard_map/ppermute | solution.py:488
  214.5 5.6 %collective-permute-done.14 = bf16[512,128]{1,0:T(8,128)(2,1)S(1)} collective-permute-done((bf16[512,128]{1,0:T(8,128)(2,1)S(1)}, bf16[512,128]{1,0:T(8,128)(2,1)S(1)}, u32[]{:S(2)}, u32[]{:S(2)}) %collective-permute-start.14) | collective-permute-done | bytes 131104 | tf_op jit(solution)/shard_map/ppermute | solution.py:488
  226.0 2.3 collective-permute-done.21.refs_1_
  229.3 10.9 %attend.5 = (bf16[4,512,128]{2,1,0:T(8,128)(2,1)}, bf16[4,512,128]{2,1,0:T(8,128)(2,1)}) custom-call(s32[4]{0:T(128)} %pad_add_fusion.place, s32[8,8]{1,0:T(8,128)} %mask.5, bf16[4,3,512,128]{3,2,1,0:T(8,128)(2,1)} %copy-done, bf16[4,2,512,128]{3,2,1,0:T(8,128)(2,1)} %copy-done.20), custom_call_target="tpu_custom_call" | custom-call | flops 2684354560 | bytes 4194304 | tf_op jit(solution)/shard_map/attend/pallas_call | solution.py:233
  244.6 7.8 %collective-permute-done.24 = bf16[512,128]{1,0:T(8,128)(2,1)S(1)} collective-permute-done((bf16[512,128]{1,0:T(8,128)(2,1)S(1)}, bf16[512,128]{1,0:T(8,128)(2,1)S(1)}, u32[]{:S(2)}, u32[]{:S(2)}) %collective-permute-start.24) | collective-permute-done | bytes 131104 | tf_op jit(solution)/shard_map/ppermute | solution.py:488
  252.3 8.8 %grad.3 = (bf16[512,768]{1,0:T(8,128)(2,1)}, f32[512,768]{1,0:T(8,128)}) custom-call(s32[4]{0:T(128)} %pad_add_fusion.place, bf16[4,512,128]{2,1,0:T(8,128)(2,1)} %get-tuple-element.127.refs_0_, bf16[4,512,128]{2,1,0:T(8,128)(2,1)} %copy-done.22, bf16[4,512,128]{2,1,0:T(8,128)(2,1)} %copy-done.23, bf16[4,512,128]{2,1,0:T(8,128)(2,1)} %collective-permute-done.10.refs_3_, ...), custom_call_target="tpu_custom_call" | custom-call | flops 3221225472 | bytes 11534336 | tf_op jit(solution)/shard_map/grad/pallas_call | solution.py:420
  261.2 6.3 %collective-permute-done.25 = bf16[512,128]{1,0:T(8,128)(2,1)S(1)} collective-permute-done((bf16[512,128]{1,0:T(8,128)(2,1)S(1)}, bf16[512,128]{1,0:T(8,128)(2,1)S(1)}, u32[]{:S(2)}, u32[]{:S(2)}) %collective-permute-start.25) | collective-permute-done | bytes 131104 | tf_op jit(solution)/shard_map/ppermute | solution.py:488
  267.4 2.1 collective-permute-start.33
  272.4 14.1 %mix.2.refs_6_ = f32[512,1536]{1,0:T(8,128)} custom-call(s32[4]{0:T(128)} %pad_add_fusion.place, bf16[4,512,128]{2,1,0:T(8,128)(2,1)} %pad_maximum_fusion.5.refs_0_, bf16[4,512,128]{2,1,0:T(8,128)(2,1)} %copy-done.13, bf16[4,512,128]{2,1,0:T(8,128)(2,1)} %copy-done.12, bf16[4,512,128]{2,1,0:T(8,128)(2,1)} %copy-done.14, bf16[4,512,128]{2,1,0:T(8,128)(2,1)} %copy-done.5, ...), custom_call_target="tpu_custom_call" | custom-call | flops 6442450944 | bytes 18874368 | tf_op jit(solution)/shard_map/mix/pallas_call | solution.py:345
  287.3 6.5 %grad.4 = (bf16[256,768]{1,0:T(8,128)(2,1)}, f32[256,768]{1,0:T(8,128)}) custom-call(s32[4]{0:T(128)} %pad_add_fusion.place, bf16[4,512,128]{2,1,0:T(8,128)(2,1)} %get-tuple-element.144.refs_0_.refs_8_, bf16[4,512,128]{2,1,0:T(8,128)(2,1)} %copy-done.27, bf16[4,512,128]{2,1,0:T(8,128)(2,1)} %copy-done.28, bf16[4,512,128]{2,1,0:T(8,128)(2,1)} %copy-done.29, ...), custom_call_target="tpu_custom_call" | custom-call | flops 1610612736 | bytes 7340032 | tf_op jit(solution)/shard_map/grad/pallas_call | solution.py:420
  296.7 7.7 %collective-permute-done.32.refs_3_ = bf16[4,512,128]{2,1,0:T(8,128)(2,1)} collective-permute-done((bf16[4,512,128]{2,1,0:T(8,128)(2,1)S(1)}, bf16[4,512,128]{2,1,0:T(8,128)(2,1)}, u32[]{:S(2)}, u32[]{:S(2)}) %collective-permute-start.32) | collective-permute-done | bytes 524320 | tf_op jit(solution)/shard_map/ppermute | solution.py:460
  304.3 10.9 %grad.5 = (bf16[768,768]{1,0:T(8,128)(2,1)}, f32[768,768]{1,0:T(8,128)}) custom-call(s32[4]{0:T(128)} %pad_add_fusion.place, bf16[4,512,128]{2,1,0:T(8,128)(2,1)} %get-tuple-element.127.refs_0_, bf16[4,512,128]{2,1,0:T(8,128)(2,1)} %copy-done.22, bf16[4,512,128]{2,1,0:T(8,128)(2,1)} %copy-done.23, bf16[4,512,128]{2,1,0:T(8,128)(2,1)} %collective-permute-done.10.refs_3_, ...), custom_call_target="tpu_custom_call" | custom-call | flops 4831838208 | bytes 15728640 | tf_op jit(solution)/shard_map/grad/pallas_call | solution.py:420
  317.6 10.1 %mix.3 = bf16[512,1536]{1,0:T(8,128)(2,1)} custom-call(s32[4]{0:T(128)} %pad_add_fusion.place, bf16[4,512,128]{2,1,0:T(8,128)(2,1)} %copy-done.6, bf16[4,512,128]{2,1,0:T(8,128)(2,1)} %copy-done.17, bf16[4,512,128]{2,1,0:T(8,128)(2,1)} %copy-done.18, bf16[4,512,128]{2,1,0:T(8,128)(2,1)} %collective-permute-done.32.refs_3_, bf16[3072,1536]{1,0:T(8,128)(2,1)} %refs_4_.7, ...), custom_call_target="tpu_custom_call" | custom-call | flops 3221225472 | bytes 9437184 | tf_op jit(solution)/shard_map/mix/pallas_call | solution.py:345
  (144 shorter events, 51.4 us)
Async XLA Ops:
  7.2 98.1 %all-gather.3.cloned.1.call-start = ((), (), s32[]{:S(2)}) async-start(), calls=%async_computation.3 | async-start | bytes 3932160 | tf_op jit(solution)/shard_map/all_gather | solution.py:491
  7.2 98.0 %collective-permute-start.3 = (bf16[3072,1536]{1,0:T(8,128)(2,1)}, bf16[3072,1536]{1,0:T(8,128)(2,1)}, u32[]{:S(2)}, u32[]{:S(2)}) collective-permute-start(bf16[3072,1536]{1,0:T(8,128)(2,1)} %refs_4_.7), channel_id=1, source_target_pairs={{0,4},{4,0},{1,5},{5,1},{2,6},{6,2},{3,7},{7,3},{8,12},{12,8},{9,1... | collective-permute-start | bytes 28311560 | tf_op jit(solution)/shard_map/ppermute | solution.py:496
  14.4 19.5 %collective-permute-start = (bf16[2,3,512,128]{3,2,1,0:T(8,128)(2,1)}, bf16[2,3,512,128]{3,2,1,0:T(8,128)(2,1)S(1)}, u32[]{:S(2)}, u32[]{:S(2)}) collective-permute-start(bf16[2,3,512,128]{3,2,1,0:T(8,128)(2,1)} %get-tuple-element.79), channel_id=1, source_target_pairs={{0,8},{8,0},{16,24},{24,16},{1,9},{9,1},{17,25},{25,17},{2,10},{10... | collective-permute-start | bytes 2359304 | tf_op jit(solution)/shard_map/ppermute | solution.py:477
  36.4 68.9 %all-to-all-start = ((bf16[4,3,512,128]{3,2,1,0:T(8,128)(2,1)}), bf16[4,3,512,128]{3,2,1,0:T(8,128)(2,1)S(1)}, u32[]{:S(2)}, u32[]{:S(2)}) async-start(bf16[4,3,512,128]{3,2,1,0:T(8,128)(2,1)} %pad_maximum_fusion.1), calls=%async_computation | async-start | bytes 3145728 | tf_op jit(solution)/shard_map/all_to_all | solution.py:482
  47.5 18.1 %collective-permute-start.1 = (bf16[2,3,512,128]{3,2,1,0:T(8,128)(2,1)}, bf16[2,3,512,128]{3,2,1,0:T(8,128)(2,1)S(1)}, u32[]{:S(2)}, u32[]{:S(2)}) collective-permute-start(bf16[2,3,512,128]{3,2,1,0:T(8,128)(2,1)} %get-tuple-element.84), channel_id=1, source_target_pairs={{0,8},{8,0},{16,24},{24,16},{1,9},{9,1},{17,25},{25,17},{2,10},{10... | collective-permute-start | bytes 2359304 | tf_op jit(solution)/shard_map/ppermute | solution.py:477
  48.7 33.7 %collective-permute-start.2 = (bf16[2,3,512,128]{3,2,1,0:T(8,128)(2,1)}, bf16[2,3,512,128]{3,2,1,0:T(8,128)(2,1)}, u32[]{:S(2)}, u32[]{:S(2)}) collective-permute-start(bf16[2,3,512,128]{3,2,1,0:T(8,128)(2,1)} %get-tuple-element.86), channel_id=1, source_target_pairs={{0,8},{8,0},{16,24},{24,16},{1,9},{9,1},{17,25},{25,17},{2,10},{10... | collective-permute-start | bytes 2359304 | tf_op jit(solution)/shard_map/ppermute | solution.py:477
  106.8 53.5 %all-to-all-start.1 = ((bf16[4,3,512,128]{3,2,1,0:T(8,128)(2,1)}), bf16[4,3,512,128]{3,2,1,0:T(8,128)(2,1)S(1)}, u32[]{:S(2)}, u32[]{:S(2)}) async-start(bf16[4,3,512,128]{3,2,1,0:T(8,128)(2,1)} %pad_maximum_fusion.2), calls=%async_computation.1 | async-start | bytes 3145728 | tf_op jit(solution)/shard_map/all_to_all | solution.py:482
  130.9 28.6 %collective-permute-start.9 = (bf16[4,512,128]{2,1,0:T(8,128)(2,1)}, bf16[4,512,128]{2,1,0:T(8,128)(2,1)S(1)}, u32[]{:S(2)}, u32[]{:S(2)}) collective-permute-start(bf16[4,512,128]{2,1,0:T(8,128)(2,1)} %get-tuple-element.127.refs_0_), channel_id=1, source_target_pairs={{0,16},{16,0},{8,24},{24,8},{1,17},{17,1},{9,25},{25,9},{2,18},{18... | collective-permute-start | bytes 1572872 | tf_op jit(solution)/shard_map/ppermute | solution.py:464
  141.4 18.9 %collective-permute-start.10 = (bf16[4,512,128]{2,1,0:T(8,128)(2,1)S(1)}, bf16[4,512,128]{2,1,0:T(8,128)(2,1)}, u32[]{:S(2)}, u32[]{:S(2)}) collective-permute-start(bf16[4,512,128]{2,1,0:T(8,128)(2,1)S(1)} %collective-permute-done.8.refs_1_), channel_id=1, source_target_pairs={{0,16},{16,0},{8,24},{24,8},{1,17},{17,1},{9,25},{25,9},{2,18},{18... | collective-permute-start | bytes 1572872 | tf_op jit(solution)/shard_map/ppermute | solution.py:463
  143.9 14.8 %collective-permute-start.6 = (bf16[512,128]{1,0:T(8,128)(2,1)S(1)}, bf16[512,128]{1,0:T(8,128)(2,1)S(1)}, u32[]{:S(2)}, u32[]{:S(2)}) collective-permute-start(bf16[512,128]{1,0:T(8,128)(2,1)S(1)} %get-tuple-element.172), channel_id=1, source_target_pairs={{0,2},{1,3},{2,0},{3,1},{4,6},{5,7},{6,4},{7,5},{8,10},{9,11},{10,... | collective-permute-start | bytes 393224 | tf_op jit(solution)/shard_map/ppermute | solution.py:488
  145.1 13.6 %collective-permute-start.7 = (bf16[512,128]{1,0:T(8,128)(2,1)S(1)}, bf16[512,128]{1,0:T(8,128)(2,1)S(1)}, u32[]{:S(2)}, u32[]{:S(2)}) collective-permute-start(bf16[512,128]{1,0:T(8,128)(2,1)S(1)} %get-tuple-element.171), channel_id=1, source_target_pairs={{0,3},{1,0},{2,1},{3,2},{4,7},{5,4},{6,5},{7,6},{8,11},{9,8},{10,9... | collective-permute-start | bytes 393224 | tf_op jit(solution)/shard_map/ppermute | solution.py:488
  165.3 56.8 %all-to-all-start.2 = ((bf16[4,3,512,128]{3,2,1,0:T(8,128)(2,1)}), bf16[4,3,512,128]{3,2,1,0:T(8,128)(2,1)S(1)}, u32[]{:S(2)}, u32[]{:S(2)}) async-start(bf16[4,3,512,128]{3,2,1,0:T(8,128)(2,1)} %pad_maximum_fusion.3), calls=%async_computation.2 | async-start | bytes 3145728 | tf_op jit(solution)/shard_map/all_to_all | solution.py:482
  170.0 134.4 %all-gather.5.cloned.1.call-start = ((), (), s32[]{:S(2)}) async-start(), calls=%async_computation.4 | async-start | bytes 3932160 | tf_op jit(solution)/shard_map/all_gather | solution.py:507
  170.0 13.7 %collective-permute-start.16 = (bf16[4,512,128]{2,1,0:T(8,128)(2,1)S(1)}, bf16[4,512,128]{2,1,0:T(8,128)(2,1)S(1)}, u32[]{:S(2)}, u32[]{:S(2)}) collective-permute-start(bf16[4,512,128]{2,1,0:T(8,128)(2,1)S(1)} %copy-done.4), channel_id=1, source_target_pairs={{0,16},{16,0},{8,24},{24,8},{1,17},{17,1},{9,25},{25,9},{2,18},{18... | collective-permute-start | bytes 1572872 | tf_op jit(solution)/shard_map/ppermute | solution.py:462
  182.1 13.5 %collective-permute-start.18 = (bf16[4,512,128]{2,1,0:T(8,128)(2,1)}, bf16[4,512,128]{2,1,0:T(8,128)(2,1)S(1)}, u32[]{:S(2)}, u32[]{:S(2)}) collective-permute-start(bf16[4,512,128]{2,1,0:T(8,128)(2,1)} %get-tuple-element.131.refs_4_), channel_id=1, source_target_pairs={{0,8},{8,0},{16,24},{24,16},{1,9},{9,1},{17,25},{25,17},{2,10},{10... | collective-permute-start | bytes 1572872 | tf_op jit(solution)/shard_map/ppermute | solution.py:462
  183.4 36.8 %collective-permute-start.15 = (bf16[4,512,128]{2,1,0:T(8,128)(2,1)S(1)}, bf16[4,512,128]{2,1,0:T(8,128)(2,1)S(1)}, u32[]{:S(2)}, u32[]{:S(2)}) collective-permute-start(bf16[4,512,128]{2,1,0:T(8,128)(2,1)S(1)} %copy-done.4), channel_id=1, source_target_pairs={{0,8},{8,0},{16,24},{24,16},{1,9},{9,1},{17,25},{25,17},{2,10},{10... | collective-permute-start | bytes 1572872 | tf_op jit(solution)/shard_map/ppermute | solution.py:464
  183.6 36.6 %collective-permute-start.17 = (bf16[4,512,128]{2,1,0:T(8,128)(2,1)S(1)}, bf16[4,512,128]{2,1,0:T(8,128)(2,1)S(1)}, u32[]{:S(2)}, u32[]{:S(2)}) collective-permute-start(bf16[4,512,128]{2,1,0:T(8,128)(2,1)S(1)} %collective-permute-done.16.refs_2_), channel_id=1, source_target_pairs={{0,8},{8,0},{16,24},{24,16},{1,9},{9,1},{17,25},{25,17},{2,10},{10... | collective-permute-start | bytes 1572872 | tf_op jit(solution)/shard_map/ppermute | solution.py:463
  184.8 35.4 %collective-permute-start.19 = (bf16[4,512,128]{2,1,0:T(8,128)(2,1)}, bf16[4,512,128]{2,1,0:T(8,128)(2,1)S(1)}, u32[]{:S(2)}, u32[]{:S(2)}) collective-permute-start(bf16[4,512,128]{2,1,0:T(8,128)(2,1)} %get-tuple-element.131.refs_4_), channel_id=1, source_target_pairs={{0,16},{16,0},{8,24},{24,8},{1,17},{17,1},{9,25},{25,9},{2,18},{18... | collective-permute-start | bytes 1572872 | tf_op jit(solution)/shard_map/ppermute | solution.py:464
  195.6 26.5 %collective-permute-start.20 = (bf16[4,512,128]{2,1,0:T(8,128)(2,1)S(1)}, bf16[4,512,128]{2,1,0:T(8,128)(2,1)}, u32[]{:S(2)}, u32[]{:S(2)}) collective-permute-start(bf16[4,512,128]{2,1,0:T(8,128)(2,1)S(1)} %collective-permute-done.18.refs_5_), channel_id=1, source_target_pairs={{0,16},{16,0},{8,24},{24,8},{1,17},{17,1},{9,25},{25,9},{2,18},{18... | collective-permute-start | bytes 1572872 | tf_op jit(solution)/shard_map/ppermute | solution.py:463
  223.5 16.7 %collective-permute-start.22 = (bf16[4,512,128]{2,1,0:T(8,128)(2,1)S(1)}, bf16[4,512,128]{2,1,0:T(8,128)(2,1)S(1)}, u32[]{:S(2)}, u32[]{:S(2)}) collective-permute-start(bf16[4,512,128]{2,1,0:T(8,128)(2,1)S(1)} %pad_maximum_fusion.6.refs_4_), channel_id=1, source_target_pairs={{0,8},{8,0},{16,24},{24,16},{1,9},{9,1},{17,25},{25,17},{2,10},{10... | collective-permute-start | bytes 1572872 | tf_op jit(solution)/shard_map/ppermute | solution.py:508
  224.8 15.4 %collective-permute-start.23 = (bf16[4,512,128]{2,1,0:T(8,128)(2,1)S(1)}, bf16[4,512,128]{2,1,0:T(8,128)(2,1)S(1)}, u32[]{:S(2)}, u32[]{:S(2)}) collective-permute-start(bf16[4,512,128]{2,1,0:T(8,128)(2,1)S(1)} %pad_maximum_fusion.6.refs_4_), channel_id=1, source_target_pairs={{0,16},{16,0},{8,24},{24,8},{1,17},{17,1},{9,25},{25,9},{2,18},{18... | collective-permute-start | bytes 1572872 | tf_op jit(solution)/shard_map/ppermute | solution.py:508
  241.8 27.8 %collective-permute-start.27 = (bf16[4,512,128]{2,1,0:T(8,128)(2,1)S(1)}, bf16[4,512,128]{2,1,0:T(8,128)(2,1)S(1)}, u32[]{:S(2)}, u32[]{:S(2)}) collective-permute-start(bf16[4,512,128]{2,1,0:T(8,128)(2,1)S(1)} %collective-permute-done.23.refs_6_), channel_id=1, source_target_pairs={{0,8},{8,0},{16,24},{24,16},{1,9},{9,1},{17,25},{25,17},{2,10},{10... | collective-permute-start | bytes 1572872 | tf_op jit(solution)/shard_map/ppermute | solution.py:510
  243.1 26.5 %collective-permute-start.28 = (bf16[4,512,128]{2,1,0:T(8,128)(2,1)}, bf16[4,512,128]{2,1,0:T(8,128)(2,1)S(1)}, u32[]{:S(2)}, u32[]{:S(2)}) collective-permute-start(bf16[4,512,128]{2,1,0:T(8,128)(2,1)} %get-tuple-element.144.refs_0_.refs_8_), channel_id=1, source_target_pairs={{0,8},{8,0},{16,24},{24,16},{1,9},{9,1},{17,25},{25,17},{2,10},{10... | collective-permute-start | bytes 1572872 | tf_op jit(solution)/shard_map/ppermute | solution.py:460
  243.3 26.3 %collective-permute-start.29 = (bf16[4,512,128]{2,1,0:T(8,128)(2,1)}, bf16[4,512,128]{2,1,0:T(8,128)(2,1)S(1)}, u32[]{:S(2)}, u32[]{:S(2)}) collective-permute-start(bf16[4,512,128]{2,1,0:T(8,128)(2,1)} %get-tuple-element.144.refs_0_.refs_8_), channel_id=1, source_target_pairs={{0,16},{16,0},{8,24},{24,8},{1,17},{17,1},{9,25},{25,9},{2,18},{18... | collective-permute-start | bytes 1572872 | tf_op jit(solution)/shard_map/ppermute | solution.py:460
  244.6 22.9 %collective-permute-start.25 = (bf16[512,128]{1,0:T(8,128)(2,1)S(1)}, bf16[512,128]{1,0:T(8,128)(2,1)S(1)}, u32[]{:S(2)}, u32[]{:S(2)}) collective-permute-start(bf16[512,128]{1,0:T(8,128)(2,1)S(1)} %get-tuple-element.164), channel_id=1, source_target_pairs={{0,2},{1,3},{2,0},{3,1},{4,6},{5,7},{6,4},{7,5},{8,10},{9,11},{10,... | collective-permute-start | bytes 393224 | tf_op jit(solution)/shard_map/ppermute | solution.py:488
  252.3 17.2 %collective-permute-start.26 = (bf16[512,128]{1,0:T(8,128)(2,1)S(1)}, bf16[512,128]{1,0:T(8,128)(2,1)S(1)}, u32[]{:S(2)}, u32[]{:S(2)}) collective-permute-start(bf16[512,128]{1,0:T(8,128)(2,1)S(1)} %get-tuple-element.163), channel_id=1, source_target_pairs={{0,3},{1,0},{2,1},{3,2},{4,7},{5,4},{6,5},{7,6},{8,11},{9,8},{10,9... | collective-permute-start | bytes 393224 | tf_op jit(solution)/shard_map/ppermute | solution.py:488
  267.4 19.1 %collective-permute-start.33 = (bf16[4,512,128]{2,1,0:T(8,128)(2,1)S(1)}, bf16[4,512,128]{2,1,0:T(8,128)(2,1)S(1)}, u32[]{:S(2)}, u32[]{:S(2)}) collective-permute-start(bf16[4,512,128]{2,1,0:T(8,128)(2,1)S(1)} %copy-done.26), channel_id=1, source_target_pairs={{0,24},{24,0},{8,16},{16,8},{1,25},{25,1},{9,17},{17,9},{2,26},{26... | collective-permute-start | bytes 1572872 | tf_op jit(solution)/shard_map/ppermute | solution.py:460
  269.6 25.4 %collective-permute-start.30 = (bf16[4,512,128]{2,1,0:T(8,128)(2,1)S(1)}, bf16[4,512,128]{2,1,0:T(8,128)(2,1)S(1)}, u32[]{:S(2)}, u32[]{:S(2)}) collective-permute-start(bf16[4,512,128]{2,1,0:T(8,128)(2,1)S(1)} %pad_maximum_fusion.7.refs_0_), channel_id=1, source_target_pairs={{0,8},{8,0},{16,24},{24,16},{1,9},{9,1},{17,25},{25,17},{2,10},{10... | collective-permute-start | bytes 1572872 | tf_op jit(solution)/shard_map/ppermute | solution.py:460
  270.0 25.1 %collective-permute-start.31 = (bf16[4,512,128]{2,1,0:T(8,128)(2,1)S(1)}, bf16[4,512,128]{2,1,0:T(8,128)(2,1)S(1)}, u32[]{:S(2)}, u32[]{:S(2)}) collective-permute-start(bf16[4,512,128]{2,1,0:T(8,128)(2,1)S(1)} %pad_maximum_fusion.7.refs_0_), channel_id=1, source_target_pairs={{0,16},{16,0},{8,24},{24,8},{1,17},{17,1},{9,25},{25,9},{2,18},{18... | collective-permute-start | bytes 1572872 | tf_op jit(solution)/shard_map/ppermute | solution.py:460
  270.3 34.0 %collective-permute-start.32 = (bf16[4,512,128]{2,1,0:T(8,128)(2,1)S(1)}, bf16[4,512,128]{2,1,0:T(8,128)(2,1)}, u32[]{:S(2)}, u32[]{:S(2)}) collective-permute-start(bf16[4,512,128]{2,1,0:T(8,128)(2,1)S(1)} %pad_maximum_fusion.7.refs_0_), channel_id=1, source_target_pairs={{0,24},{24,0},{8,16},{16,8},{1,25},{25,1},{9,17},{17,9},{2,26},{26... | collective-permute-start | bytes 1572872 | tf_op jit(solution)/shard_map/ppermute | solution.py:460
  295.0 21.1 %collective-permute-start.34 = (bf16[2,384,768]{2,1,0:T(8,128)(2,1)S(1)}, bf16[2,384,768]{2,1,0:T(8,128)(2,1)}, u32[]{:S(2)}, u32[]{:S(2)}) collective-permute-start(bf16[2,384,768]{2,1,0:T(8,128)(2,1)S(1)} %pad_maximum_fusion.4), channel_id=1, source_target_pairs={{0,4},{4,0},{1,5},{5,1},{2,6},{6,2},{3,7},{7,3},{8,12},{12,8},{9,1... | collective-permute-start | bytes 3538952 | tf_op jit(solution)/shard_map/ppermute | solution.py:518
  315.2 12.5 %collective-permute-start.35 = (bf16[2,384,768]{2,1,0:T(8,128)(2,1)}, bf16[2,384,768]{2,1,0:T(8,128)(2,1)S(1)}, u32[]{:S(2)}, u32[]{:S(2)}) collective-permute-start(bf16[2,384,768]{2,1,0:T(8,128)(2,1)} %bitcast.53), channel_id=1, source_target_pairs={{0,4},{4,0},{1,5},{5,1},{2,6},{6,2},{3,7},{7,3},{8,12},{12,8},{9,1... | collective-permute-start | bytes 3538952 | tf_op jit(solution)/shard_map/ppermute | solution.py:518
  (39 other events, 439.2 us)
Sparse Core Ops, SparseCore 0:
  10.7 92.6 all-gather.2
  222.2 75.0 all-gather.4

commit v3 on v2

--- a/solution.py
+++ b/solution.py
@@ -477,9 +477,11 @@
         got = lax.ppermute(send, "row", X_SWAP)
         return keep, got
 
-    def over_ctx(kept, got):
-        pieces = [jnp.where(x == 0, kept, got), jnp.where(x == 0, got, kept)]
-        return lax.all_to_all(jnp.concatenate(pieces), "ctx", 0, 0, tiled=True)
+    def merged(kept, got):
+        return jnp.concatenate([jnp.where(x == 0, kept, got), jnp.where(x == 0, got, kept)])
+
+    def over_ctx(pieces):
+        return lax.all_to_all(pieces, "ctx", 0, 0, tiled=True)
 
     def attended(h, own, beside):
         other = lax.ppermute(own[:, 1:], "col", [(0, 1)])
@@ -491,14 +493,15 @@
     first_cot = lax.all_gather(cotangent[:, :cut], "ctx", axis=0, tiled=True)
     pair = exchanged(0, place)
     pair, later = lax.optimization_barrier((pair, place))
-    own0 = over_ctx(*pair)
+    own0 = over_ctx(merged(*pair))
     pairs = [exchanged(h, later) for h in range(1, HALF)]
     w_other = lax.ppermute(out_weight, "col", OTHER_CORE)
-    own0, pairs, w_other, first_cot = lax.optimization_barrier((own0, pairs, w_other, first_cot))
-    own1 = over_ctx(*pairs[0])
+    one, two = [merged(*pair) for pair in pairs]
+    own0, one, w_other, first_cot = lax.optimization_barrier((own0, one, w_other, first_cot))
+    own1 = over_ctx(one)
     home0, grad0, _ = attended(0, own0, ())
-    own1, pair, home0, grad0 = lax.optimization_barrier((own1, pairs[1], home0, grad0))
-    own2 = over_ctx(*pair)
+    own1, two, home0, grad0 = lax.optimization_barrier((own1, two, home0, grad0))
+    own2 = over_ctx(two)
     home1, grad1, _ = attended(1, own1, ())
     mix0 = over_row(home0, False)
     own2, last_half, home1, mix0, grad1 = lax.optimization_barrier(
@@ -510,15 +513,15 @@
     mix1.append(lax.ppermute(mix1[2], "row", X_SWAP))
     home2, mix1, grad2[1:3] = lax.optimization_barrier((home2, mix1, grad2[1:3]))
     early = grad(place, grad0 + grad1, first_cot)
-    mix2 = over_row(home2)
 
     def summed(pairs):
-        sent = jnp.concatenate([p[0].reshape(2, -1, cut) for p in pairs], axis=1)
-        kept = jnp.concatenate([p[1].reshape(2, -1, cut) for p in pairs], axis=1)
+        sent = jnp.concatenate([p[0].reshape(2, -1, p[0].shape[1]) for p in pairs], axis=1)
+        kept = jnp.concatenate([p[1].reshape(2, -1, p[1].shape[1]) for p in pairs], axis=1)
         received = lax.ppermute(sent, "col", OTHER_CORE)
         return (kept + received.astype(jnp.float32)).astype(jnp.bfloat16)
 
     sums = mix(place, (0, 1), mix0 + mix1, out_weight, w_other, None, jnp.float32)
+    mix2 = over_row(home2)
     sums, grad2 = lax.optimization_barrier((sums, grad2))
     sums, early, grad2 = lax.optimization_barrier((sums, early, grad2))
     late = grad(place, grad2, first_cot)

time: 339 us -> 334 us (0.985)
  waiting for transfers between devices: 158 us -> 152 us
    all_to_all x3, waiting for transfers between devices: 22.9 us -> 19.2 us  [over_ctx(): return lax.all_to_all(pieces, 'ctx', 0, 0, tiled=True)]
    unnamed x60 -> x64, local copies, waits for them, and re-layouts: 7.08 us -> 7.09 us
  transfers between devices with their start and end apart: 41 -> 41, of which waited for: 16 -> 16; matrix products, arithmetic and copies ran while one was open for 5% -> 6% of each run, Pallas kernels for 28% -> 28%
where the time goes in v3:
time: 334 us; the launch traced here: 332 us
  waiting for transfers between devices  152 us (46%)
  Pallas kernels  92.9 us (28%)
  starting transfers between devices  44.1 us (13%)
  local copies, waits for them, and re-layouts  14.7 us (4%)
  between operations  14.6 us (4%)
  other arithmetic  13.6 us (4%)
    ppermute x3, waiting for transfers between devices, exchanged(): got = lax.ppermute(send, 'row', X_SWAP)  51.5 us
    ppermute x9, waiting for transfers between devices, attended(): home = [lax.ppermute(out[s], 'ctx', around(s)) for s in range(1, 4)]  48.3 us
    pallas_call x3, Pallas kernels, attend(): pl.pallas_call(_attend_kernel, out_shape=(jax.ShapeDtypeStruct((4, BLOCK,...  32.8 us
    pallas_call x3, Pallas kernels, grad(): pl.pallas_call(functools.partial(_grad_kernel, count), grid=(4,), out_sha...  26.2 us
    pallas_call x2, Pallas kernels, mix(): pl.pallas_call(functools.partial(_mix_kernel, heads, len(added)), out_sha...  24.2 us
    ppermute x3, waiting for transfers between devices, over_row(): near = lax.ppermute(a, 'row', first)  19.8 us
    all_to_all x3, waiting for transfers between devices, over_ctx(): return lax.all_to_all(pieces, 'ctx', 0, 0, tiled=True)  19.2 us
    all_to_all x3, starting transfers between devices, over_ctx(): return lax.all_to_all(pieces, 'ctx', 0, 0, tiled=True)  15.4 us
  transfers between devices with their start and end apart: 41, of which 16 were waited for; matrix products, arithmetic and copies ran while one was open for 6% of the time, Pallas kernels for 28%

profile of v3, /device:TPU:25, one launch (start us, length us, event | category | flops | bytes accessed | tf_op | source)
XLA Modules:
  0.0 332.1 jit_solution(2520405632325542165)
XLA Ops:
  7.9 2.6 fusion.1
  11.2 3.2 pack.3
  15.6 18.3 %collective-permute-done = bf16[2,3,512,128]{3,2,1,0:T(8,128)(2,1)S(1)} collective-permute-done((bf16[2,3,512,128]{3,2,1,0:T(8,128)(2,1)}, bf16[2,3,512,128]{3,2,1,0:T(8,128)(2,1)S(1)}, u32[]{:S(2)}, u32[]{:S(2)}) %collective-permute-start) | collective-permute-done | bytes 786464 | tf_op jit(solution)/shard_map/ppermute | solution.py:477
  36.3 4.5 %all-to-all-start = ((bf16[4,3,512,128]{3,2,1,0:T(8,128)(2,1)}), bf16[4,3,512,128]{3,2,1,0:T(8,128)(2,1)S(1)}, u32[]{:S(2)}, u32[]{:S(2)}) async-start(bf16[4,3,512,128]{3,2,1,0:T(8,128)(2,1)} %pad_maximum_fusion.1), calls=%async_computation | async-start | bytes 3145728 | tf_op jit(solution)/shard_map/all_to_all | solution.py:484
  40.9 3.2 pack.4
  44.0 3.3 %pack.5 = (bf16[2,3,512,128]{3,2,1,0:T(8,128)(2,1)}, bf16[2,3,512,128]{3,2,1,0:T(8,128)(2,1)}) custom-call(s32[4]{0:T(128)} %pad_add_fusion.place, bf16[512,1536]{1,0:T(8,128)(2,1)} %refs_3_.5, bf16[512,1536]{1,0:T(8,128)(2,1)} %refs_4_.6, bf16[512,1536]{1,0:T(8,128)(2,1)} %refs_5_.5, bf16[512,1536]{1,0:T(8,128)(2,1)} %refs_3_.5, bf16[512,1536]{1,0:T(8,128)(2,1)} %refs_4_.6, ...), custom_call_target="tpu_custom_call" | custom-call | bytes 3145728 | tf_op jit(solution)/shard_map/pack/pallas_call | solution.py:120
  48.9 16.4 %collective-permute-done.1 = bf16[2,3,512,128]{3,2,1,0:T(8,128)(2,1)S(1)} collective-permute-done((bf16[2,3,512,128]{3,2,1,0:T(8,128)(2,1)S(1)}, bf16[2,3,512,128]{3,2,1,0:T(8,128)(2,1)S(1)}, u32[]{:S(2)}, u32[]{:S(2)}) %collective-permute-start.1) | collective-permute-done | bytes 786464 | tf_op jit(solution)/shard_map/ppermute | solution.py:477
  65.3 16.9 %collective-permute-done.3 = bf16[2,3,512,128]{3,2,1,0:T(8,128)(2,1)S(1)} collective-permute-done((bf16[2,3,512,128]{3,2,1,0:T(8,128)(2,1)}, bf16[2,3,512,128]{3,2,1,0:T(8,128)(2,1)S(1)}, u32[]{:S(2)}, u32[]{:S(2)}) %collective-permute-start.3) | collective-permute-done | bytes 786464 | tf_op jit(solution)/shard_map/ppermute | solution.py:477
  82.2 2.5 broadcast_select_fusion.1
  86.0 19.2 %all-to-all-done.refs_0_ = bf16[4,3,512,128]{3,2,1,0:T(8,128)(2,1)S(1)} async-done(((bf16[4,3,512,128]{3,2,1,0:T(8,128)(2,1)}), bf16[4,3,512,128]{3,2,1,0:T(8,128)(2,1)S(1)}, u32[]{:S(2)}, u32[]{:S(2)}) %all-to-all-start) | async-done | bytes 1572896 | tf_op jit(solution)/shard_map/all_to_all | solution.py:484
  105.2 6.3 %all-to-all-start.1 = ((bf16[4,3,512,128]{3,2,1,0:T(8,128)(2,1)}), bf16[4,3,512,128]{3,2,1,0:T(8,128)(2,1)S(1)}, u32[]{:S(2)}, u32[]{:S(2)}) async-start(bf16[4,3,512,128]{3,2,1,0:T(8,128)(2,1)} %pad_maximum_fusion.2), calls=%async_computation.1 | async-start | bytes 3145728 | tf_op jit(solution)/shard_map/all_to_all | solution.py:484
  112.9 3.3 collective-permute-done.4.refs_1_
  117.2 11.1 %attend.3 = (bf16[4,512,128]{2,1,0:T(8,128)(2,1)}, bf16[4,512,128]{2,1,0:T(8,128)(2,1)}) custom-call(s32[4]{0:T(128)} %pad_add_fusion.place, s32[8,8]{1,0:T(8,128)} %mask.5, bf16[4,3,512,128]{3,2,1,0:T(8,128)(2,1)} %copy-done.2, bf16[4,2,512,128]{3,2,1,0:T(8,128)(2,1)} %copy-done.22), custom_call_target="tpu_custom_call" | custom-call | flops 2684354560 | bytes 4194304 | tf_op jit(solution)/shard_map/attend/pallas_call | solution.py:233
  130.7 9.3 %collective-permute-done.8.refs_1_ = bf16[4,512,128]{2,1,0:T(8,128)(2,1)S(1)} collective-permute-done((bf16[4,512,128]{2,1,0:T(8,128)(2,1)}, bf16[4,512,128]{2,1,0:T(8,128)(2,1)S(1)}, u32[]{:S(2)}, u32[]{:S(2)}) %collective-permute-start.8) | collective-permute-done | bytes 524320 | tf_op jit(solution)/shard_map/ppermute | solution.py:462
  145.4 3.9 %collective-permute-done.5 = bf16[512,128]{1,0:T(8,128)(2,1)S(1)} collective-permute-done((bf16[512,128]{1,0:T(8,128)(2,1)S(1)}, bf16[512,128]{1,0:T(8,128)(2,1)S(1)}, u32[]{:S(2)}, u32[]{:S(2)}) %collective-permute-start.5) | collective-permute-done | bytes 131104 | tf_op jit(solution)/shard_map/ppermute | solution.py:490
  149.3 7.7 %collective-permute-done.6 = bf16[512,128]{1,0:T(8,128)(2,1)S(1)} collective-permute-done((bf16[512,128]{1,0:T(8,128)(2,1)S(1)}, bf16[512,128]{1,0:T(8,128)(2,1)S(1)}, u32[]{:S(2)}, u32[]{:S(2)}) %collective-permute-start.6) | collective-permute-done | bytes 131104 | tf_op jit(solution)/shard_map/ppermute | solution.py:490
  161.2 4.5 %all-to-all-start.2 = ((bf16[4,3,512,128]{3,2,1,0:T(8,128)(2,1)}), bf16[4,3,512,128]{3,2,1,0:T(8,128)(2,1)S(1)}, u32[]{:S(2)}, u32[]{:S(2)}) async-start(bf16[4,3,512,128]{3,2,1,0:T(8,128)(2,1)} %pad_maximum_fusion.3), calls=%async_computation.2 | async-start | bytes 3145728 | tf_op jit(solution)/shard_map/all_to_all | solution.py:484
  167.0 10.9 %attend.4 = (bf16[4,512,128]{2,1,0:T(8,128)(2,1)}, bf16[4,512,128]{2,1,0:T(8,128)(2,1)}) custom-call(s32[4]{0:T(128)} %pad_add_fusion.place, s32[8,8]{1,0:T(8,128)} %mask.5, bf16[4,3,512,128]{3,2,1,0:T(8,128)(2,1)} %copy-done.1, bf16[4,2,512,128]{3,2,1,0:T(8,128)(2,1)} %collective-permute-done.11.refs_1_), custom_call_target="tpu_custom_call" | custom-call | flops 2684354560 | bytes 4194304 | tf_op jit(solution)/shard_map/attend/pallas_call | solution.py:233
  180.8 10.5 %collective-permute-done.18.refs_5_ = bf16[4,512,128]{2,1,0:T(8,128)(2,1)S(1)} collective-permute-done((bf16[4,512,128]{2,1,0:T(8,128)(2,1)}, bf16[4,512,128]{2,1,0:T(8,128)(2,1)S(1)}, u32[]{:S(2)}, u32[]{:S(2)}) %collective-permute-start.18) | collective-permute-done | bytes 524320 | tf_op jit(solution)/shard_map/ppermute | solution.py:462
  193.1 10.2 %collective-permute-done.12 = bf16[512,128]{1,0:T(8,128)(2,1)S(1)} collective-permute-done((bf16[512,128]{1,0:T(8,128)(2,1)S(1)}, bf16[512,128]{1,0:T(8,128)(2,1)S(1)}, u32[]{:S(2)}, u32[]{:S(2)}) %collective-permute-start.12) | collective-permute-done | bytes 131104 | tf_op jit(solution)/shard_map/ppermute | solution.py:490
  203.3 6.8 %collective-permute-done.13 = bf16[512,128]{1,0:T(8,128)(2,1)S(1)} collective-permute-done((bf16[512,128]{1,0:T(8,128)(2,1)S(1)}, bf16[512,128]{1,0:T(8,128)(2,1)S(1)}, u32[]{:S(2)}, u32[]{:S(2)}) %collective-permute-start.13) | collective-permute-done | bytes 131104 | tf_op jit(solution)/shard_map/ppermute | solution.py:490
  210.1 5.6 %collective-permute-done.14 = bf16[512,128]{1,0:T(8,128)(2,1)S(1)} collective-permute-done((bf16[512,128]{1,0:T(8,128)(2,1)S(1)}, bf16[512,128]{1,0:T(8,128)(2,1)S(1)}, u32[]{:S(2)}, u32[]{:S(2)}) %collective-permute-start.14) | collective-permute-done | bytes 131104 | tf_op jit(solution)/shard_map/ppermute | solution.py:490
  221.6 2.3 collective-permute-done.21.refs_1_
  224.9 10.9 %attend.5 = (bf16[4,512,128]{2,1,0:T(8,128)(2,1)}, bf16[4,512,128]{2,1,0:T(8,128)(2,1)}) custom-call(s32[4]{0:T(128)} %pad_add_fusion.place, s32[8,8]{1,0:T(8,128)} %mask.5, bf16[4,3,512,128]{3,2,1,0:T(8,128)(2,1)} %copy-done, bf16[4,2,512,128]{3,2,1,0:T(8,128)(2,1)} %copy-done.21), custom_call_target="tpu_custom_call" | custom-call | flops 2684354560 | bytes 4194304 | tf_op jit(solution)/shard_map/attend/pallas_call | solution.py:233
  240.2 7.8 %collective-permute-done.24 = bf16[512,128]{1,0:T(8,128)(2,1)S(1)} collective-permute-done((bf16[512,128]{1,0:T(8,128)(2,1)S(1)}, bf16[512,128]{1,0:T(8,128)(2,1)S(1)}, u32[]{:S(2)}, u32[]{:S(2)}) %collective-permute-start.24) | collective-permute-done | bytes 131104 | tf_op jit(solution)/shard_map/ppermute | solution.py:490
  248.0 8.8 %grad.3 = (bf16[512,768]{1,0:T(8,128)(2,1)}, f32[512,768]{1,0:T(8,128)}) custom-call(s32[4]{0:T(128)} %pad_add_fusion.place, bf16[4,512,128]{2,1,0:T(8,128)(2,1)} %get-tuple-element.119.refs_0_, bf16[4,512,128]{2,1,0:T(8,128)(2,1)} %copy-done.24, bf16[4,512,128]{2,1,0:T(8,128)(2,1)} %copy-done.25, bf16[4,512,128]{2,1,0:T(8,128)(2,1)} %collective-permute-done.10.refs_3_, ...), custom_call_target="tpu_custom_call" | custom-call | flops 3221225472 | bytes 11534336 | tf_op jit(solution)/shard_map/grad/pallas_call | solution.py:420
  256.8 6.2 %collective-permute-done.25 = bf16[512,128]{1,0:T(8,128)(2,1)S(1)} collective-permute-done((bf16[512,128]{1,0:T(8,128)(2,1)S(1)}, bf16[512,128]{1,0:T(8,128)(2,1)S(1)}, u32[]{:S(2)}, u32[]{:S(2)}) %collective-permute-start.25) | collective-permute-done | bytes 131104 | tf_op jit(solution)/shard_map/ppermute | solution.py:490
  268.0 14.1 %mix.2.refs_6_ = f32[512,1536]{1,0:T(8,128)} custom-call(s32[4]{0:T(128)} %pad_add_fusion.place, bf16[4,512,128]{2,1,0:T(8,128)(2,1)} %pad_maximum_fusion.5.refs_0_, bf16[4,512,128]{2,1,0:T(8,128)(2,1)} %copy-done.14, bf16[4,512,128]{2,1,0:T(8,128)(2,1)} %copy-done.13, bf16[4,512,128]{2,1,0:T(8,128)(2,1)} %copy-done.15, bf16[4,512,128]{2,1,0:T(8,128)(2,1)} %copy-done.7, ...), custom_call_target="tpu_custom_call" | custom-call | flops 6442450944 | bytes 18874368 | tf_op jit(solution)/shard_map/mix/pallas_call | solution.py:345
  283.0 6.5 %grad.4 = (bf16[256,768]{1,0:T(8,128)(2,1)}, f32[256,768]{1,0:T(8,128)}) custom-call(s32[4]{0:T(128)} %pad_add_fusion.place, bf16[4,512,128]{2,1,0:T(8,128)(2,1)} %get-tuple-element.136.refs_0_.refs_8_, bf16[4,512,128]{2,1,0:T(8,128)(2,1)} %copy-done.29, bf16[4,512,128]{2,1,0:T(8,128)(2,1)} %copy-done.30, bf16[4,512,128]{2,1,0:T(8,128)(2,1)} %copy-done.31, ...), custom_call_target="tpu_custom_call" | custom-call | flops 1610612736 | bytes 7340032 | tf_op jit(solution)/shard_map/grad/pallas_call | solution.py:420
  292.4 7.6 %collective-permute-done.32.refs_3_ = bf16[4,512,128]{2,1,0:T(8,128)(2,1)} collective-permute-done((bf16[4,512,128]{2,1,0:T(8,128)(2,1)S(1)}, bf16[4,512,128]{2,1,0:T(8,128)(2,1)}, u32[]{:S(2)}, u32[]{:S(2)}) %collective-permute-start.32) | collective-permute-done | bytes 524320 | tf_op jit(solution)/shard_map/ppermute | solution.py:460
  300.0 10.9 %grad.5 = (bf16[768,768]{1,0:T(8,128)(2,1)}, f32[768,768]{1,0:T(8,128)}) custom-call(s32[4]{0:T(128)} %pad_add_fusion.place, bf16[4,512,128]{2,1,0:T(8,128)(2,1)} %get-tuple-element.119.refs_0_, bf16[4,512,128]{2,1,0:T(8,128)(2,1)} %copy-done.24, bf16[4,512,128]{2,1,0:T(8,128)(2,1)} %copy-done.25, bf16[4,512,128]{2,1,0:T(8,128)(2,1)} %collective-permute-done.10.refs_3_, ...), custom_call_target="tpu_custom_call" | custom-call | flops 4831838208 | bytes 15728640 | tf_op jit(solution)/shard_map/grad/pallas_call | solution.py:420
  313.3 10.1 %mix.3 = bf16[512,1536]{1,0:T(8,128)(2,1)} custom-call(s32[4]{0:T(128)} %pad_add_fusion.place, bf16[4,512,128]{2,1,0:T(8,128)(2,1)} %copy-done.8, bf16[4,512,128]{2,1,0:T(8,128)(2,1)} %copy-done.18, bf16[4,512,128]{2,1,0:T(8,128)(2,1)} %copy-done.19, bf16[4,512,128]{2,1,0:T(8,128)(2,1)} %collective-permute-done.32.refs_3_, bf16[3072,1536]{1,0:T(8,128)(2,1)} %refs_4_.7, ...), custom_call_target="tpu_custom_call" | custom-call | flops 3221225472 | bytes 9437184 | tf_op jit(solution)/shard_map/mix/pallas_call | solution.py:345
  (147 shorter events, 52.1 us)
Async XLA Ops:
  7.2 98.1 %all-gather.3.cloned.1.call-start = ((), (), s32[]{:S(2)}) async-start(), calls=%async_computation.3 | async-start | bytes 3932160 | tf_op jit(solution)/shard_map/all_gather | solution.py:493
  7.2 98.0 %collective-permute-start.2 = (bf16[3072,1536]{1,0:T(8,128)(2,1)}, bf16[3072,1536]{1,0:T(8,128)(2,1)}, u32[]{:S(2)}, u32[]{:S(2)}) collective-permute-start(bf16[3072,1536]{1,0:T(8,128)(2,1)} %refs_4_.7), channel_id=1, source_target_pairs={{0,4},{4,0},{1,5},{5,1},{2,6},{6,2},{3,7},{7,3},{8,12},{12,8},{9,1... | collective-permute-start | bytes 28311560 | tf_op jit(solution)/shard_map/ppermute | solution.py:498
  14.3 19.5 %collective-permute-start = (bf16[2,3,512,128]{3,2,1,0:T(8,128)(2,1)}, bf16[2,3,512,128]{3,2,1,0:T(8,128)(2,1)S(1)}, u32[]{:S(2)}, u32[]{:S(2)}) collective-permute-start(bf16[2,3,512,128]{3,2,1,0:T(8,128)(2,1)} %get-tuple-element.75), channel_id=1, source_target_pairs={{0,8},{8,0},{16,24},{24,16},{1,9},{9,1},{17,25},{25,17},{2,10},{10... | collective-permute-start | bytes 2359304 | tf_op jit(solution)/shard_map/ppermute | solution.py:477
  36.3 68.9 %all-to-all-start = ((bf16[4,3,512,128]{3,2,1,0:T(8,128)(2,1)}), bf16[4,3,512,128]{3,2,1,0:T(8,128)(2,1)S(1)}, u32[]{:S(2)}, u32[]{:S(2)}) async-start(bf16[4,3,512,128]{3,2,1,0:T(8,128)(2,1)} %pad_maximum_fusion.1), calls=%async_computation | async-start | bytes 3145728 | tf_op jit(solution)/shard_map/all_to_all | solution.py:484
  47.4 17.9 %collective-permute-start.1 = (bf16[2,3,512,128]{3,2,1,0:T(8,128)(2,1)S(1)}, bf16[2,3,512,128]{3,2,1,0:T(8,128)(2,1)S(1)}, u32[]{:S(2)}, u32[]{:S(2)}) collective-permute-start(bf16[2,3,512,128]{3,2,1,0:T(8,128)(2,1)S(1)} %copy-done.23), channel_id=1, source_target_pairs={{0,8},{8,0},{16,24},{24,16},{1,9},{9,1},{17,25},{25,17},{2,10},{10... | collective-permute-start | bytes 2359304 | tf_op jit(solution)/shard_map/ppermute | solution.py:477
  48.6 33.5 %collective-permute-start.3 = (bf16[2,3,512,128]{3,2,1,0:T(8,128)(2,1)}, bf16[2,3,512,128]{3,2,1,0:T(8,128)(2,1)S(1)}, u32[]{:S(2)}, u32[]{:S(2)}) collective-permute-start(bf16[2,3,512,128]{3,2,1,0:T(8,128)(2,1)} %get-tuple-element.83), channel_id=1, source_target_pairs={{0,8},{8,0},{16,24},{24,16},{1,9},{9,1},{17,25},{25,17},{2,10},{10... | collective-permute-start | bytes 2359304 | tf_op jit(solution)/shard_map/ppermute | solution.py:477
  105.2 53.5 %all-to-all-start.1 = ((bf16[4,3,512,128]{3,2,1,0:T(8,128)(2,1)}), bf16[4,3,512,128]{3,2,1,0:T(8,128)(2,1)S(1)}, u32[]{:S(2)}, u32[]{:S(2)}) async-start(bf16[4,3,512,128]{3,2,1,0:T(8,128)(2,1)} %pad_maximum_fusion.2), calls=%async_computation.1 | async-start | bytes 3145728 | tf_op jit(solution)/shard_map/all_to_all | solution.py:484
  129.5 28.4 %collective-permute-start.9 = (bf16[4,512,128]{2,1,0:T(8,128)(2,1)}, bf16[4,512,128]{2,1,0:T(8,128)(2,1)S(1)}, u32[]{:S(2)}, u32[]{:S(2)}) collective-permute-start(bf16[4,512,128]{2,1,0:T(8,128)(2,1)} %get-tuple-element.119.refs_0_), channel_id=1, source_target_pairs={{0,16},{16,0},{8,24},{24,8},{1,17},{17,1},{9,25},{25,9},{2,18},{18... | collective-permute-start | bytes 1572872 | tf_op jit(solution)/shard_map/ppermute | solution.py:464
  140.0 18.8 %collective-permute-start.10 = (bf16[4,512,128]{2,1,0:T(8,128)(2,1)S(1)}, bf16[4,512,128]{2,1,0:T(8,128)(2,1)}, u32[]{:S(2)}, u32[]{:S(2)}) collective-permute-start(bf16[4,512,128]{2,1,0:T(8,128)(2,1)S(1)} %collective-permute-done.8.refs_1_), channel_id=1, source_target_pairs={{0,16},{16,0},{8,24},{24,8},{1,17},{17,1},{9,25},{25,9},{2,18},{18... | collective-permute-start | bytes 1572872 | tf_op jit(solution)/shard_map/ppermute | solution.py:463
  142.4 14.6 %collective-permute-start.6 = (bf16[512,128]{1,0:T(8,128)(2,1)S(1)}, bf16[512,128]{1,0:T(8,128)(2,1)S(1)}, u32[]{:S(2)}, u32[]{:S(2)}) collective-permute-start(bf16[512,128]{1,0:T(8,128)(2,1)S(1)} %get-tuple-element.164), channel_id=1, source_target_pairs={{0,2},{1,3},{2,0},{3,1},{4,6},{5,7},{6,4},{7,5},{8,10},{9,11},{10,... | collective-permute-start | bytes 393224 | tf_op jit(solution)/shard_map/ppermute | solution.py:490
  143.6 13.5 %collective-permute-start.7 = (bf16[512,128]{1,0:T(8,128)(2,1)S(1)}, bf16[512,128]{1,0:T(8,128)(2,1)S(1)}, u32[]{:S(2)}, u32[]{:S(2)}) collective-permute-start(bf16[512,128]{1,0:T(8,128)(2,1)S(1)} %get-tuple-element.163), channel_id=1, source_target_pairs={{0,3},{1,0},{2,1},{3,2},{4,7},{5,4},{6,5},{7,6},{8,11},{9,8},{10,9... | collective-permute-start | bytes 393224 | tf_op jit(solution)/shard_map/ppermute | solution.py:490
  161.2 56.5 %all-to-all-start.2 = ((bf16[4,3,512,128]{3,2,1,0:T(8,128)(2,1)}), bf16[4,3,512,128]{3,2,1,0:T(8,128)(2,1)S(1)}, u32[]{:S(2)}, u32[]{:S(2)}) async-start(bf16[4,3,512,128]{3,2,1,0:T(8,128)(2,1)} %pad_maximum_fusion.3), calls=%async_computation.2 | async-start | bytes 3145728 | tf_op jit(solution)/shard_map/all_to_all | solution.py:484
  165.7 134.2 %all-gather.5.cloned.1.call-start = ((), (), s32[]{:S(2)}) async-start(), calls=%async_computation.4 | async-start | bytes 3932160 | tf_op jit(solution)/shard_map/all_gather | solution.py:510
  165.8 13.6 %collective-permute-start.16 = (bf16[4,512,128]{2,1,0:T(8,128)(2,1)}, bf16[4,512,128]{2,1,0:T(8,128)(2,1)S(1)}, u32[]{:S(2)}, u32[]{:S(2)}) collective-permute-start(bf16[4,512,128]{2,1,0:T(8,128)(2,1)} %pad_maximum_fusion.5.refs_0_), channel_id=1, source_target_pairs={{0,16},{16,0},{8,24},{24,8},{1,17},{17,1},{9,25},{25,9},{2,18},{18... | collective-permute-start | bytes 1572872 | tf_op jit(solution)/shard_map/ppermute | solution.py:462
  177.9 13.5 %collective-permute-start.18 = (bf16[4,512,128]{2,1,0:T(8,128)(2,1)}, bf16[4,512,128]{2,1,0:T(8,128)(2,1)S(1)}, u32[]{:S(2)}, u32[]{:S(2)}) collective-permute-start(bf16[4,512,128]{2,1,0:T(8,128)(2,1)} %get-tuple-element.123.refs_4_), channel_id=1, source_target_pairs={{0,8},{8,0},{16,24},{24,16},{1,9},{9,1},{17,25},{25,17},{2,10},{10... | collective-permute-start | bytes 1572872 | tf_op jit(solution)/shard_map/ppermute | solution.py:462
  179.1 36.7 %collective-permute-start.15 = (bf16[4,512,128]{2,1,0:T(8,128)(2,1)S(1)}, bf16[4,512,128]{2,1,0:T(8,128)(2,1)S(1)}, u32[]{:S(2)}, u32[]{:S(2)}) collective-permute-start(bf16[4,512,128]{2,1,0:T(8,128)(2,1)S(1)} %copy-done.6), channel_id=1, source_target_pairs={{0,8},{8,0},{16,24},{24,16},{1,9},{9,1},{17,25},{25,17},{2,10},{10... | collective-permute-start | bytes 1572872 | tf_op jit(solution)/shard_map/ppermute | solution.py:464
  179.4 36.4 %collective-permute-start.17 = (bf16[4,512,128]{2,1,0:T(8,128)(2,1)S(1)}, bf16[4,512,128]{2,1,0:T(8,128)(2,1)S(1)}, u32[]{:S(2)}, u32[]{:S(2)}) collective-permute-start(bf16[4,512,128]{2,1,0:T(8,128)(2,1)S(1)} %collective-permute-done.16.refs_2_), channel_id=1, source_target_pairs={{0,8},{8,0},{16,24},{24,16},{1,9},{9,1},{17,25},{25,17},{2,10},{10... | collective-permute-start | bytes 1572872 | tf_op jit(solution)/shard_map/ppermute | solution.py:463
  180.6 35.3 %collective-permute-start.19 = (bf16[4,512,128]{2,1,0:T(8,128)(2,1)}, bf16[4,512,128]{2,1,0:T(8,128)(2,1)S(1)}, u32[]{:S(2)}, u32[]{:S(2)}) collective-permute-start(bf16[4,512,128]{2,1,0:T(8,128)(2,1)} %get-tuple-element.123.refs_4_), channel_id=1, source_target_pairs={{0,16},{16,0},{8,24},{24,8},{1,17},{17,1},{9,25},{25,9},{2,18},{18... | collective-permute-start | bytes 1572872 | tf_op jit(solution)/shard_map/ppermute | solution.py:464
  191.3 26.4 %collective-permute-start.20 = (bf16[4,512,128]{2,1,0:T(8,128)(2,1)S(1)}, bf16[4,512,128]{2,1,0:T(8,128)(2,1)}, u32[]{:S(2)}, u32[]{:S(2)}) collective-permute-start(bf16[4,512,128]{2,1,0:T(8,128)(2,1)S(1)} %collective-permute-done.18.refs_5_), channel_id=1, source_target_pairs={{0,16},{16,0},{8,24},{24,8},{1,17},{17,1},{9,25},{25,9},{2,18},{18... | collective-permute-start | bytes 1572872 | tf_op jit(solution)/shard_map/ppermute | solution.py:463
  219.1 16.7 %collective-permute-start.22 = (bf16[4,512,128]{2,1,0:T(8,128)(2,1)S(1)}, bf16[4,512,128]{2,1,0:T(8,128)(2,1)S(1)}, u32[]{:S(2)}, u32[]{:S(2)}) collective-permute-start(bf16[4,512,128]{2,1,0:T(8,128)(2,1)S(1)} %pad_maximum_fusion.6.refs_4_), channel_id=1, source_target_pairs={{0,8},{8,0},{16,24},{24,16},{1,9},{9,1},{17,25},{25,17},{2,10},{10... | collective-permute-start | bytes 1572872 | tf_op jit(solution)/shard_map/ppermute | solution.py:511
  220.4 15.4 %collective-permute-start.23 = (bf16[4,512,128]{2,1,0:T(8,128)(2,1)S(1)}, bf16[4,512,128]{2,1,0:T(8,128)(2,1)S(1)}, u32[]{:S(2)}, u32[]{:S(2)}) collective-permute-start(bf16[4,512,128]{2,1,0:T(8,128)(2,1)S(1)} %pad_maximum_fusion.6.refs_4_), channel_id=1, source_target_pairs={{0,16},{16,0},{8,24},{24,8},{1,17},{17,1},{9,25},{25,9},{2,18},{18... | collective-permute-start | bytes 1572872 | tf_op jit(solution)/shard_map/ppermute | solution.py:511
  237.4 27.8 %collective-permute-start.27 = (bf16[4,512,128]{2,1,0:T(8,128)(2,1)S(1)}, bf16[4,512,128]{2,1,0:T(8,128)(2,1)S(1)}, u32[]{:S(2)}, u32[]{:S(2)}) collective-permute-start(bf16[4,512,128]{2,1,0:T(8,128)(2,1)S(1)} %collective-permute-done.23.refs_6_), channel_id=1, source_target_pairs={{0,8},{8,0},{16,24},{24,16},{1,9},{9,1},{17,25},{25,17},{2,10},{10... | collective-permute-start | bytes 1572872 | tf_op jit(solution)/shard_map/ppermute | solution.py:513
  238.7 26.6 %collective-permute-start.28 = (bf16[4,512,128]{2,1,0:T(8,128)(2,1)}, bf16[4,512,128]{2,1,0:T(8,128)(2,1)S(1)}, u32[]{:S(2)}, u32[]{:S(2)}) collective-permute-start(bf16[4,512,128]{2,1,0:T(8,128)(2,1)} %get-tuple-element.136.refs_0_.refs_8_), channel_id=1, source_target_pairs={{0,8},{8,0},{16,24},{24,16},{1,9},{9,1},{17,25},{25,17},{2,10},{10... | collective-permute-start | bytes 1572872 | tf_op jit(solution)/shard_map/ppermute | solution.py:460
  239.0 26.3 %collective-permute-start.29 = (bf16[4,512,128]{2,1,0:T(8,128)(2,1)}, bf16[4,512,128]{2,1,0:T(8,128)(2,1)S(1)}, u32[]{:S(2)}, u32[]{:S(2)}) collective-permute-start(bf16[4,512,128]{2,1,0:T(8,128)(2,1)} %get-tuple-element.136.refs_0_.refs_8_), channel_id=1, source_target_pairs={{0,16},{16,0},{8,24},{24,8},{1,17},{17,1},{9,25},{25,9},{2,18},{18... | collective-permute-start | bytes 1572872 | tf_op jit(solution)/shard_map/ppermute | solution.py:460
  240.2 22.9 %collective-permute-start.25 = (bf16[512,128]{1,0:T(8,128)(2,1)S(1)}, bf16[512,128]{1,0:T(8,128)(2,1)S(1)}, u32[]{:S(2)}, u32[]{:S(2)}) collective-permute-start(bf16[512,128]{1,0:T(8,128)(2,1)S(1)} %get-tuple-element.156), channel_id=1, source_target_pairs={{0,2},{1,3},{2,0},{3,1},{4,6},{5,7},{6,4},{7,5},{8,10},{9,11},{10,... | collective-permute-start | bytes 393224 | tf_op jit(solution)/shard_map/ppermute | solution.py:490
  248.0 17.2 %collective-permute-start.26 = (bf16[512,128]{1,0:T(8,128)(2,1)S(1)}, bf16[512,128]{1,0:T(8,128)(2,1)S(1)}, u32[]{:S(2)}, u32[]{:S(2)}) collective-permute-start(bf16[512,128]{1,0:T(8,128)(2,1)S(1)} %get-tuple-element.155), channel_id=1, source_target_pairs={{0,3},{1,0},{2,1},{3,2},{4,7},{5,4},{6,5},{7,6},{8,11},{9,8},{10,9... | collective-permute-start | bytes 393224 | tf_op jit(solution)/shard_map/ppermute | solution.py:490
  263.1 19.1 %collective-permute-start.33 = (bf16[4,512,128]{2,1,0:T(8,128)(2,1)S(1)}, bf16[4,512,128]{2,1,0:T(8,128)(2,1)S(1)}, u32[]{:S(2)}, u32[]{:S(2)}) collective-permute-start(bf16[4,512,128]{2,1,0:T(8,128)(2,1)S(1)} %copy-done.28), channel_id=1, source_target_pairs={{0,24},{24,0},{8,16},{16,8},{1,25},{25,1},{9,17},{17,9},{2,26},{26... | collective-permute-start | bytes 1572872 | tf_op jit(solution)/shard_map/ppermute | solution.py:460
  265.3 25.4 %collective-permute-start.30 = (bf16[4,512,128]{2,1,0:T(8,128)(2,1)S(1)}, bf16[4,512,128]{2,1,0:T(8,128)(2,1)S(1)}, u32[]{:S(2)}, u32[]{:S(2)}) collective-permute-start(bf16[4,512,128]{2,1,0:T(8,128)(2,1)S(1)} %pad_maximum_fusion.7.refs_0_), channel_id=1, source_target_pairs={{0,8},{8,0},{16,24},{24,16},{1,9},{9,1},{17,25},{25,17},{2,10},{10... | collective-permute-start | bytes 1572872 | tf_op jit(solution)/shard_map/ppermute | solution.py:460
  265.7 25.1 %collective-permute-start.31 = (bf16[4,512,128]{2,1,0:T(8,128)(2,1)S(1)}, bf16[4,512,128]{2,1,0:T(8,128)(2,1)S(1)}, u32[]{:S(2)}, u32[]{:S(2)}) collective-permute-start(bf16[4,512,128]{2,1,0:T(8,128)(2,1)S(1)} %pad_maximum_fusion.7.refs_0_), channel_id=1, source_target_pairs={{0,16},{16,0},{8,24},{24,8},{1,17},{17,1},{9,25},{25,9},{2,18},{18... | collective-permute-start | bytes 1572872 | tf_op jit(solution)/shard_map/ppermute | solution.py:460
  266.0 34.0 %collective-permute-start.32 = (bf16[4,512,128]{2,1,0:T(8,128)(2,1)S(1)}, bf16[4,512,128]{2,1,0:T(8,128)(2,1)}, u32[]{:S(2)}, u32[]{:S(2)}) collective-permute-start(bf16[4,512,128]{2,1,0:T(8,128)(2,1)S(1)} %pad_maximum_fusion.7.refs_0_), channel_id=1, source_target_pairs={{0,24},{24,0},{8,16},{16,8},{1,25},{25,1},{9,17},{17,9},{2,26},{26... | collective-permute-start | bytes 1572872 | tf_op jit(solution)/shard_map/ppermute | solution.py:460
  290.7 21.1 %collective-permute-start.34 = (bf16[2,384,768]{2,1,0:T(8,128)(2,1)S(1)}, bf16[2,384,768]{2,1,0:T(8,128)(2,1)}, u32[]{:S(2)}, u32[]{:S(2)}) collective-permute-start(bf16[2,384,768]{2,1,0:T(8,128)(2,1)S(1)} %pad_maximum_fusion.4), channel_id=1, source_target_pairs={{0,4},{4,0},{1,5},{5,1},{2,6},{6,2},{3,7},{7,3},{8,12},{12,8},{9,1... | collective-permute-start | bytes 3538952 | tf_op jit(solution)/shard_map/ppermute | solution.py:520
  310.9 12.5 %collective-permute-start.35 = (bf16[2,384,768]{2,1,0:T(8,128)(2,1)}, bf16[2,384,768]{2,1,0:T(8,128)(2,1)S(1)}, u32[]{:S(2)}, u32[]{:S(2)}) collective-permute-start(bf16[2,384,768]{2,1,0:T(8,128)(2,1)} %bitcast.53), channel_id=1, source_target_pairs={{0,4},{4,0},{1,5},{5,1},{2,6},{6,2},{3,7},{7,3},{8,12},{12,8},{9,1... | collective-permute-start | bytes 3538952 | tf_op jit(solution)/shard_map/ppermute | solution.py:520
  (41 other events, 448.5 us)
Sparse Core Ops, SparseCore 0:
  10.7 92.6 all-gather.2
  217.9 75.1 all-gather.4

commit v4 on v3

--- a/solution.py
+++ b/solution.py
@@ -262,8 +262,8 @@
     )(place, mask, own, other)
 
 
-def _mix_kernel(heads, added, place, *refs):
-    count = 4 * len(heads)
+def _mix_kernel(heads, sides, added, place, *refs):
+    count = len(sides) * len(heads)
     parts, (w_own, w_other) = refs[:count], refs[count : count + 2]
     sums = refs[count + 2] if added else None
     out = refs[count + 2 + added]
@@ -273,11 +273,11 @@
 
     def attended(n, side):
         return pltpu.make_async_copy(
-            parts[4 * n + side], a_s.at[side, :, n], a_sem.at[4 * n + side]
+            parts[len(sides) * n + side], a_s.at[side, :, n], a_sem.at[len(sides) * n + side]
         )
 
     def weight(side, block, ref):
-        xx = lax.rem(x + side % 2, 2)
+        xx = lax.rem(x + sides[side] % 2, 2)
         from_z = lax.rem(z - block + 4, 4)
         at = pl.multiple_of((6 * from_z + 3 * xx + heads[0]) * HD, HD)
         return pltpu.make_async_copy(
@@ -287,7 +287,7 @@
         )
 
     def fetch(side):
-        yy = lax.rem(y + side // 2, 2)
+        yy = lax.rem(y + sides[side] // 2, 2)
         for n in range(len(heads)):
             attended(n, side).start()
         for block in range(4):
@@ -301,9 +301,10 @@
     fetch(1)
     width = 512
     piece = 8 * depth
-    for half in range(2):
+    halves = len(sides) // 2
+    for half in range(halves):
         for side in (2 * half, 2 * half + 1):
-            if half == 0:
+            if half < halves - 1:
                 fetch(side + 2)
             for n in range(len(heads)):
                 attended(n, side).wait()
@@ -328,7 +329,7 @@
             )
             if half > 0 or added:
                 term += sum_s[:, cut]
-            if half == 0:
+            if half < halves - 1:
                 sum_s[:, cut] = term
             else:
                 out[:, cut] = term.astype(out.dtype)
@@ -337,22 +338,22 @@
         lax.fori_loop(0, out.shape[1] // width, tile, 0)
 
 
-def mix(place, heads, parts, w_own, w_other, sums, kind):
+def mix(place, heads, parts, w_own, w_other, sums, kind, sides=(0, 1, 2, 3)):
     columns = w_own.shape[1]
-    depth = 16 * len(heads) * HD
+    depth = 4 * len(sides) * len(heads) * HD
     vmem = pl.BlockSpec(memory_space=pltpu.VMEM)
     added = [] if sums is None else [sums]
     return pl.pallas_call(
-        functools.partial(_mix_kernel, heads, len(added)),
+        functools.partial(_mix_kernel, heads, sides, len(added)),
         out_shape=jax.ShapeDtypeStruct((BLOCK, columns), kind),
         in_specs=[SMEM] + [ANY] * (len(parts) + 2) + [ANY] * len(added),
         out_specs=vmem,
         scratch_shapes=[
-            pltpu.VMEM((4, 4, len(heads), BLOCK, HD), jnp.bfloat16),
+            pltpu.VMEM((len(sides), 4, len(heads), BLOCK, HD), jnp.bfloat16),
             pltpu.VMEM((depth, columns), jnp.bfloat16),
             pltpu.VMEM((BLOCK, columns), jnp.float32),
-            pltpu.SemaphoreType.DMA((4 * len(heads),)),
-            pltpu.SemaphoreType.DMA((16,)),
+            pltpu.SemaphoreType.DMA((len(sides) * len(heads),)),
+            pltpu.SemaphoreType.DMA((4 * len(sides),)),
             pltpu.SemaphoreType.DMA,
         ],
         compiler_params=_params(VMEM_MIB),
@@ -525,9 +526,10 @@
     sums, grad2 = lax.optimization_barrier((sums, grad2))
     sums, early, grad2 = lax.optimization_barrier((sums, early, grad2))
     late = grad(place, grad2, first_cot)
-    mix2, last_cot = lax.optimization_barrier((mix2, last_cot))
+    sums = mix(place, (2,), mix2[:2], out_weight, w_other, sums, jnp.float32, (0, 1))
+    mix2, last_cot, sums = lax.optimization_barrier((mix2, last_cot, sums))
     last = grad(place, grad0 + grad1 + grad2, last_cot)
-    mixed_out = mix(place, (2,), mix2, out_weight, w_other, sums, jnp.bfloat16)
+    mixed_out = mix(place, (2,), mix2[2:], out_weight, w_other, sums, jnp.bfloat16, (2, 3))
     grad_weight = jnp.concatenate([summed([early, late]), summed([last])], axis=2)
     grad_weight = grad_weight.reshape(-1, columns)
     return (mixed_out, grad_weight)

time: 334 us -> 333 us (level)
  waiting for transfers between devices: 152 us -> 141 us
  Pallas kernels: 92.9 us -> 100 us
    ppermute x6, waiting for transfers between devices: 7.65 us -> 0.52 us  [over_row(): lax.ppermute(a, 'row', pairs)]
    pallas_call x2 -> x3, Pallas kernels: 24.2 us -> 29.1 us  [mix(): pl.pallas_call(functools.partial(_mix_kernel, heads, sides, len(added)),...]
  transfers between devices with their start and end apart: 41 -> 41, of which waited for: 16 -> 16; matrix products, arithmetic and copies ran while one was open for 6% -> 6% of each run, Pallas kernels for 28% -> 30%
where the time goes in v4:
time: 333 us; the launch traced here: 331 us
  waiting for transfers between devices  141 us (42%)
  Pallas kernels  100 us (30%)
  starting transfers between devices  46.8 us (14%)
  local copies, waits for them, and re-layouts  14.7 us (4%)
  between operations  14.6 us (4%)
  other arithmetic  13.7 us (4%)
    ppermute x3, waiting for transfers between devices, exchanged(): got = lax.ppermute(send, 'row', X_SWAP)  51.5 us
    ppermute x9, waiting for transfers between devices, attended(): home = [lax.ppermute(out[s], 'ctx', around(s)) for s in range(1, 4)]  45.2 us
    pallas_call x3, Pallas kernels, attend(): pl.pallas_call(_attend_kernel, out_shape=(jax.ShapeDtypeStruct((4, BLOCK,...  35.6 us
    pallas_call x3, Pallas kernels, mix(): pl.pallas_call(functools.partial(_mix_kernel, heads, sides, len(added)),...  29.1 us
    pallas_call x3, Pallas kernels, grad(): pl.pallas_call(functools.partial(_grad_kernel, count), grid=(4,), out_sha...  26 us
    ppermute x3, waiting for transfers between devices, over_row(): near = lax.ppermute(a, 'row', first)  19.6 us
    all_to_all x3, waiting for transfers between devices, over_ctx(): return lax.all_to_all(pieces, 'ctx', 0, 0, tiled=True)  19.1 us
    all_to_all x3, starting transfers between devices, over_ctx(): return lax.all_to_all(pieces, 'ctx', 0, 0, tiled=True)  15.4 us
  transfers between devices with their start and end apart: 41, of which 16 were waited for; matrix products, arithmetic and copies ran while one was open for 6% of the time, Pallas kernels for 30%

profile of v4, /device:TPU:25, one launch (start us, length us, event | category | flops | bytes accessed | tf_op | source)
XLA Modules:
  0.0 331.3 jit_solution(16808640045314540771)
XLA Ops:
  7.9 2.6 fusion.1
  11.2 3.2 pack.3
  15.6 18.3 %collective-permute-done = bf16[2,3,512,128]{3,2,1,0:T(8,128)(2,1)S(1)} collective-permute-done((bf16[2,3,512,128]{3,2,1,0:T(8,128)(2,1)}, bf16[2,3,512,128]{3,2,1,0:T(8,128)(2,1)S(1)}, u32[]{:S(2)}, u32[]{:S(2)}) %collective-permute-start) | collective-permute-done | bytes 786464 | tf_op jit(solution)/shard_map/ppermute | solution.py:478
  36.4 4.5 %all-to-all-start = ((bf16[4,3,512,128]{3,2,1,0:T(8,128)(2,1)}), bf16[4,3,512,128]{3,2,1,0:T(8,128)(2,1)S(1)}, u32[]{:S(2)}, u32[]{:S(2)}) async-start(bf16[4,3,512,128]{3,2,1,0:T(8,128)(2,1)} %pad_maximum_fusion.1), calls=%async_computation | async-start | bytes 3145728 | tf_op jit(solution)/shard_map/all_to_all | solution.py:485
  40.9 3.2 pack.4
  44.1 3.3 %pack.5 = (bf16[2,3,512,128]{3,2,1,0:T(8,128)(2,1)}, bf16[2,3,512,128]{3,2,1,0:T(8,128)(2,1)}) custom-call(s32[4]{0:T(128)} %pad_add_fusion.place, bf16[512,1536]{1,0:T(8,128)(2,1)} %refs_3_.5, bf16[512,1536]{1,0:T(8,128)(2,1)} %refs_4_.5, bf16[512,1536]{1,0:T(8,128)(2,1)} %refs_5_.5, bf16[512,1536]{1,0:T(8,128)(2,1)} %refs_3_.5, bf16[512,1536]{1,0:T(8,128)(2,1)} %refs_4_.5, ...), custom_call_target="tpu_custom_call" | custom-call | bytes 3145728 | tf_op jit(solution)/shard_map/pack/pallas_call | solution.py:120
  49.0 16.4 %collective-permute-done.1 = bf16[2,3,512,128]{3,2,1,0:T(8,128)(2,1)S(1)} collective-permute-done((bf16[2,3,512,128]{3,2,1,0:T(8,128)(2,1)S(1)}, bf16[2,3,512,128]{3,2,1,0:T(8,128)(2,1)S(1)}, u32[]{:S(2)}, u32[]{:S(2)}) %collective-permute-start.1) | collective-permute-done | bytes 786464 | tf_op jit(solution)/shard_map/ppermute | solution.py:478
  65.4 16.9 %collective-permute-done.3 = bf16[2,3,512,128]{3,2,1,0:T(8,128)(2,1)S(1)} collective-permute-done((bf16[2,3,512,128]{3,2,1,0:T(8,128)(2,1)}, bf16[2,3,512,128]{3,2,1,0:T(8,128)(2,1)S(1)}, u32[]{:S(2)}, u32[]{:S(2)}) %collective-permute-start.3) | collective-permute-done | bytes 786464 | tf_op jit(solution)/shard_map/ppermute | solution.py:478
  82.2 2.6 broadcast_select_fusion.1
  86.1 19.1 %all-to-all-done.refs_0_ = bf16[4,3,512,128]{3,2,1,0:T(8,128)(2,1)S(1)} async-done(((bf16[4,3,512,128]{3,2,1,0:T(8,128)(2,1)}), bf16[4,3,512,128]{3,2,1,0:T(8,128)(2,1)S(1)}, u32[]{:S(2)}, u32[]{:S(2)}) %all-to-all-start) | async-done | bytes 1572896 | tf_op jit(solution)/shard_map/all_to_all | solution.py:485
  105.2 6.3 %all-to-all-start.1 = ((bf16[4,3,512,128]{3,2,1,0:T(8,128)(2,1)}), bf16[4,3,512,128]{3,2,1,0:T(8,128)(2,1)S(1)}, u32[]{:S(2)}, u32[]{:S(2)}) async-start(bf16[4,3,512,128]{3,2,1,0:T(8,128)(2,1)} %pad_maximum_fusion.2), calls=%async_computation.1 | async-start | bytes 3145728 | tf_op jit(solution)/shard_map/all_to_all | solution.py:485
  112.9 3.3 collective-permute-done.4.refs_1_
  117.1 12.0 %attend.3 = (bf16[4,512,128]{2,1,0:T(8,128)(2,1)}, bf16[4,512,128]{2,1,0:T(8,128)(2,1)}) custom-call(s32[4]{0:T(128)} %pad_add_fusion.place, s32[8,8]{1,0:T(8,128)} %mask.5, bf16[4,3,512,128]{3,2,1,0:T(8,128)(2,1)} %copy-done.2, bf16[4,2,512,128]{3,2,1,0:T(8,128)(2,1)} %copy-done.22), custom_call_target="tpu_custom_call" | custom-call | flops 2684354560 | bytes 4194304 | tf_op jit(solution)/shard_map/attend/pallas_call | solution.py:233
  131.6 8.4 %collective-permute-done.8.refs_1_ = bf16[4,512,128]{2,1,0:T(8,128)(2,1)S(1)} collective-permute-done((bf16[4,512,128]{2,1,0:T(8,128)(2,1)}, bf16[4,512,128]{2,1,0:T(8,128)(2,1)S(1)}, u32[]{:S(2)}, u32[]{:S(2)}) %collective-permute-start.8) | collective-permute-done | bytes 524320 | tf_op jit(solution)/shard_map/ppermute | solution.py:463
  145.4 4.6 %collective-permute-done.5 = bf16[512,128]{1,0:T(8,128)(2,1)S(1)} collective-permute-done((bf16[512,128]{1,0:T(8,128)(2,1)S(1)}, bf16[512,128]{1,0:T(8,128)(2,1)S(1)}, u32[]{:S(2)}, u32[]{:S(2)}) %collective-permute-start.5) | collective-permute-done | bytes 131104 | tf_op jit(solution)/shard_map/ppermute | solution.py:491
  150.0 7.1 %collective-permute-done.6 = bf16[512,128]{1,0:T(8,128)(2,1)S(1)} collective-permute-done((bf16[512,128]{1,0:T(8,128)(2,1)S(1)}, bf16[512,128]{1,0:T(8,128)(2,1)S(1)}, u32[]{:S(2)}, u32[]{:S(2)}) %collective-permute-start.6) | collective-permute-done | bytes 131104 | tf_op jit(solution)/shard_map/ppermute | solution.py:491
  161.3 4.5 %all-to-all-start.2 = ((bf16[4,3,512,128]{3,2,1,0:T(8,128)(2,1)}), bf16[4,3,512,128]{3,2,1,0:T(8,128)(2,1)S(1)}, u32[]{:S(2)}, u32[]{:S(2)}) async-start(bf16[4,3,512,128]{3,2,1,0:T(8,128)(2,1)} %pad_maximum_fusion.3), calls=%async_computation.2 | async-start | bytes 3145728 | tf_op jit(solution)/shard_map/all_to_all | solution.py:485
  167.1 11.8 %attend.4 = (bf16[4,512,128]{2,1,0:T(8,128)(2,1)}, bf16[4,512,128]{2,1,0:T(8,128)(2,1)}) custom-call(s32[4]{0:T(128)} %pad_add_fusion.place, s32[8,8]{1,0:T(8,128)} %mask.5, bf16[4,3,512,128]{3,2,1,0:T(8,128)(2,1)} %copy-done.1, bf16[4,2,512,128]{3,2,1,0:T(8,128)(2,1)} %collective-permute-done.11.refs_1_), custom_call_target="tpu_custom_call" | custom-call | flops 2684354560 | bytes 4194304 | tf_op jit(solution)/shard_map/attend/pallas_call | solution.py:233
  181.9 11.2 %collective-permute-done.18.refs_5_ = bf16[4,512,128]{2,1,0:T(8,128)(2,1)S(1)} collective-permute-done((bf16[4,512,128]{2,1,0:T(8,128)(2,1)}, bf16[4,512,128]{2,1,0:T(8,128)(2,1)S(1)}, u32[]{:S(2)}, u32[]{:S(2)}) %collective-permute-start.18) | collective-permute-done | bytes 524320 | tf_op jit(solution)/shard_map/ppermute | solution.py:463
  194.6 9.6 %collective-permute-done.12 = bf16[512,128]{1,0:T(8,128)(2,1)S(1)} collective-permute-done((bf16[512,128]{1,0:T(8,128)(2,1)S(1)}, bf16[512,128]{1,0:T(8,128)(2,1)S(1)}, u32[]{:S(2)}, u32[]{:S(2)}) %collective-permute-start.12) | collective-permute-done | bytes 131104 | tf_op jit(solution)/shard_map/ppermute | solution.py:491
  204.1 7.6 %collective-permute-done.13 = bf16[512,128]{1,0:T(8,128)(2,1)S(1)} collective-permute-done((bf16[512,128]{1,0:T(8,128)(2,1)S(1)}, bf16[512,128]{1,0:T(8,128)(2,1)S(1)}, u32[]{:S(2)}, u32[]{:S(2)}) %collective-permute-start.13) | collective-permute-done | bytes 131104 | tf_op jit(solution)/shard_map/ppermute | solution.py:491
  211.7 5.6 %collective-permute-done.14 = bf16[512,128]{1,0:T(8,128)(2,1)S(1)} collective-permute-done((bf16[512,128]{1,0:T(8,128)(2,1)S(1)}, bf16[512,128]{1,0:T(8,128)(2,1)S(1)}, u32[]{:S(2)}, u32[]{:S(2)}) %collective-permute-start.14) | collective-permute-done | bytes 131104 | tf_op jit(solution)/shard_map/ppermute | solution.py:491
  225.8 11.8 %attend.5 = (bf16[4,512,128]{2,1,0:T(8,128)(2,1)}, bf16[4,512,128]{2,1,0:T(8,128)(2,1)}) custom-call(s32[4]{0:T(128)} %pad_add_fusion.place, s32[8,8]{1,0:T(8,128)} %mask.5, bf16[4,3,512,128]{3,2,1,0:T(8,128)(2,1)} %copy-done, bf16[4,2,512,128]{3,2,1,0:T(8,128)(2,1)} %copy-done.21), custom_call_target="tpu_custom_call" | custom-call | flops 2684354560 | bytes 4194304 | tf_op jit(solution)/shard_map/attend/pallas_call | solution.py:233
  242.0 7.1 %collective-permute-done.24 = bf16[512,128]{1,0:T(8,128)(2,1)S(1)} collective-permute-done((bf16[512,128]{1,0:T(8,128)(2,1)S(1)}, bf16[512,128]{1,0:T(8,128)(2,1)S(1)}, u32[]{:S(2)}, u32[]{:S(2)}) %collective-permute-start.24) | collective-permute-done | bytes 131104 | tf_op jit(solution)/shard_map/ppermute | solution.py:491
  249.1 3.7 %collective-permute-start.26 = (bf16[512,128]{1,0:T(8,128)(2,1)S(1)}, bf16[512,128]{1,0:T(8,128)(2,1)S(1)}, u32[]{:S(2)}, u32[]{:S(2)}) collective-permute-start(bf16[512,128]{1,0:T(8,128)(2,1)S(1)} %get-tuple-element.153), channel_id=1, source_target_pairs={{0,3},{1,0},{2,1},{3,2},{4,7},{5,4},{6,5},{7,6},{8,11},{9,8},{10,9... | collective-permute-start | bytes 393224 | tf_op jit(solution)/shard_map/ppermute | solution.py:491
  252.8 8.6 %grad.3 = (bf16[512,768]{1,0:T(8,128)(2,1)}, f32[512,768]{1,0:T(8,128)}) custom-call(s32[4]{0:T(128)} %pad_add_fusion.place, bf16[4,512,128]{2,1,0:T(8,128)(2,1)} %get-tuple-element.114.refs_0_, bf16[4,512,128]{2,1,0:T(8,128)(2,1)} %copy-done.24, bf16[4,512,128]{2,1,0:T(8,128)(2,1)} %copy-done.25, bf16[4,512,128]{2,1,0:T(8,128)(2,1)} %collective-permute-done.10.refs_3_, ...), custom_call_target="tpu_custom_call" | custom-call | flops 3221225472 | bytes 11534336 | tf_op jit(solution)/shard_map/grad/pallas_call | solution.py:421
  261.4 3.7 %collective-permute-done.25 = bf16[512,128]{1,0:T(8,128)(2,1)S(1)} collective-permute-done((bf16[512,128]{1,0:T(8,128)(2,1)S(1)}, bf16[512,128]{1,0:T(8,128)(2,1)S(1)}, u32[]{:S(2)}, u32[]{:S(2)}) %collective-permute-start.25) | collective-permute-done | bytes 131104 | tf_op jit(solution)/shard_map/ppermute | solution.py:491
  269.8 14.1 %mix.3.refs_4_ = f32[512,1536]{1,0:T(8,128)} custom-call(s32[4]{0:T(128)} %pad_add_fusion.place, bf16[4,512,128]{2,1,0:T(8,128)(2,1)} %pad_maximum_fusion.5.refs_0_, bf16[4,512,128]{2,1,0:T(8,128)(2,1)} %copy-done.14, bf16[4,512,128]{2,1,0:T(8,128)(2,1)} %copy-done.13, bf16[4,512,128]{2,1,0:T(8,128)(2,1)} %copy-done.15, bf16[4,512,128]{2,1,0:T(8,128)(2,1)} %copy-done.7, ...), custom_call_target="tpu_custom_call" | custom-call | flops 6442450944 | bytes 18874368 | tf_op jit(solution)/shard_map/mix/pallas_call | solution.py:346
  284.8 6.5 %grad.4 = (bf16[256,768]{1,0:T(8,128)(2,1)}, f32[256,768]{1,0:T(8,128)}) custom-call(s32[4]{0:T(128)} %pad_add_fusion.place, bf16[4,512,128]{2,1,0:T(8,128)(2,1)} %get-tuple-element.134.refs_0_.refs_8_, bf16[4,512,128]{2,1,0:T(8,128)(2,1)} %copy-done.29, bf16[4,512,128]{2,1,0:T(8,128)(2,1)} %copy-done.30, bf16[4,512,128]{2,1,0:T(8,128)(2,1)} %copy-done.31, ...), custom_call_target="tpu_custom_call" | custom-call | flops 1610612736 | bytes 7340032 | tf_op jit(solution)/shard_map/grad/pallas_call | solution.py:421
  293.3 7.7 %mix.4.refs_4_ = f32[512,1536]{1,0:T(8,128)} custom-call(s32[4]{0:T(128)} %pad_add_fusion.place, bf16[4,512,128]{2,1,0:T(8,128)(2,1)} %copy-done.8, bf16[4,512,128]{2,1,0:T(8,128)(2,1)} %copy-done.20, bf16[3072,1536]{1,0:T(8,128)(2,1)} %refs_2_.9, bf16[3072,1536]{1,0:T(8,128)(2,1)} %collective-permute-done.2.refs_9_.refs_3_, f32[512,1536]{1,0:T(8,128)} %mix.3.refs_4_), custom_call_target="tpu_custom_call" | custom-call | flops 1610612736 | bytes 9437184 | tf_op jit(solution)/shard_map/mix/pallas_call | solution.py:346
  302.4 10.9 %grad.5 = (bf16[768,768]{1,0:T(8,128)(2,1)}, f32[768,768]{1,0:T(8,128)}) custom-call(s32[4]{0:T(128)} %pad_add_fusion.place, bf16[4,512,128]{2,1,0:T(8,128)(2,1)} %get-tuple-element.114.refs_0_, bf16[4,512,128]{2,1,0:T(8,128)(2,1)} %copy-done.24, bf16[4,512,128]{2,1,0:T(8,128)(2,1)} %copy-done.25, bf16[4,512,128]{2,1,0:T(8,128)(2,1)} %collective-permute-done.10.refs_3_, ...), custom_call_target="tpu_custom_call" | custom-call | flops 4831838208 | bytes 15728640 | tf_op jit(solution)/shard_map/grad/pallas_call | solution.py:421
  315.3 7.2 %mix.5 = bf16[512,1536]{1,0:T(8,128)(2,1)} custom-call(s32[4]{0:T(128)} %pad_add_fusion.place, bf16[4,512,128]{2,1,0:T(8,128)(2,1)} %copy-done.18, bf16[4,512,128]{2,1,0:T(8,128)(2,1)} %collective-permute-done.32.refs_1_, bf16[3072,1536]{1,0:T(8,128)(2,1)} %refs_2_.9, bf16[3072,1536]{1,0:T(8,128)(2,1)} %collective-permute-done.2.refs_9_.refs_3_, ...), custom_call_target="tpu_custom_call" | custom-call | flops 1610612736 | bytes 9437184 | tf_op jit(solution)/shard_map/mix/pallas_call | solution.py:346
  (148 shorter events, 53.4 us)
Async XLA Ops:
  7.2 98.1 %all-gather.3.cloned.1.call-start = ((), (), s32[]{:S(2)}) async-start(), calls=%async_computation.3 | async-start | bytes 3932160 | tf_op jit(solution)/shard_map/all_gather | solution.py:494
  7.2 98.0 %collective-permute-start.2 = (bf16[3072,1536]{1,0:T(8,128)(2,1)}, bf16[3072,1536]{1,0:T(8,128)(2,1)}, u32[]{:S(2)}, u32[]{:S(2)}) collective-permute-start(bf16[3072,1536]{1,0:T(8,128)(2,1)} %refs_2_.9), channel_id=1, source_target_pairs={{0,4},{4,0},{1,5},{5,1},{2,6},{6,2},{3,7},{7,3},{8,12},{12,8},{9,1... | collective-permute-start | bytes 28311560 | tf_op jit(solution)/shard_map/ppermute | solution.py:499
  14.4 19.5 %collective-permute-start = (bf16[2,3,512,128]{3,2,1,0:T(8,128)(2,1)}, bf16[2,3,512,128]{3,2,1,0:T(8,128)(2,1)S(1)}, u32[]{:S(2)}, u32[]{:S(2)}) collective-permute-start(bf16[2,3,512,128]{3,2,1,0:T(8,128)(2,1)} %get-tuple-element.74), channel_id=1, source_target_pairs={{0,8},{8,0},{16,24},{24,16},{1,9},{9,1},{17,25},{25,17},{2,10},{10... | collective-permute-start | bytes 2359304 | tf_op jit(solution)/shard_map/ppermute | solution.py:478
  36.4 68.8 %all-to-all-start = ((bf16[4,3,512,128]{3,2,1,0:T(8,128)(2,1)}), bf16[4,3,512,128]{3,2,1,0:T(8,128)(2,1)S(1)}, u32[]{:S(2)}, u32[]{:S(2)}) async-start(bf16[4,3,512,128]{3,2,1,0:T(8,128)(2,1)} %pad_maximum_fusion.1), calls=%async_computation | async-start | bytes 3145728 | tf_op jit(solution)/shard_map/all_to_all | solution.py:485
  47.4 17.9 %collective-permute-start.1 = (bf16[2,3,512,128]{3,2,1,0:T(8,128)(2,1)S(1)}, bf16[2,3,512,128]{3,2,1,0:T(8,128)(2,1)S(1)}, u32[]{:S(2)}, u32[]{:S(2)}) collective-permute-start(bf16[2,3,512,128]{3,2,1,0:T(8,128)(2,1)S(1)} %copy-done.23), channel_id=1, source_target_pairs={{0,8},{8,0},{16,24},{24,16},{1,9},{9,1},{17,25},{25,17},{2,10},{10... | collective-permute-start | bytes 2359304 | tf_op jit(solution)/shard_map/ppermute | solution.py:478
  48.7 33.5 %collective-permute-start.3 = (bf16[2,3,512,128]{3,2,1,0:T(8,128)(2,1)}, bf16[2,3,512,128]{3,2,1,0:T(8,128)(2,1)S(1)}, u32[]{:S(2)}, u32[]{:S(2)}) collective-permute-start(bf16[2,3,512,128]{3,2,1,0:T(8,128)(2,1)} %get-tuple-element.82), channel_id=1, source_target_pairs={{0,8},{8,0},{16,24},{24,16},{1,9},{9,1},{17,25},{25,17},{2,10},{10... | collective-permute-start | bytes 2359304 | tf_op jit(solution)/shard_map/ppermute | solution.py:478
  105.2 53.6 %all-to-all-start.1 = ((bf16[4,3,512,128]{3,2,1,0:T(8,128)(2,1)}), bf16[4,3,512,128]{3,2,1,0:T(8,128)(2,1)S(1)}, u32[]{:S(2)}, u32[]{:S(2)}) async-start(bf16[4,3,512,128]{3,2,1,0:T(8,128)(2,1)} %pad_maximum_fusion.2), calls=%async_computation.1 | async-start | bytes 3145728 | tf_op jit(solution)/shard_map/all_to_all | solution.py:485
  129.1 10.9 %collective-permute-start.8 = (bf16[4,512,128]{2,1,0:T(8,128)(2,1)}, bf16[4,512,128]{2,1,0:T(8,128)(2,1)S(1)}, u32[]{:S(2)}, u32[]{:S(2)}) collective-permute-start(bf16[4,512,128]{2,1,0:T(8,128)(2,1)} %get-tuple-element.114.refs_0_), channel_id=1, source_target_pairs={{0,8},{8,0},{16,24},{24,16},{1,9},{9,1},{17,25},{25,17},{2,10},{10... | collective-permute-start | bytes 1572872 | tf_op jit(solution)/shard_map/ppermute | solution.py:463
  130.4 27.6 %collective-permute-start.9 = (bf16[4,512,128]{2,1,0:T(8,128)(2,1)}, bf16[4,512,128]{2,1,0:T(8,128)(2,1)S(1)}, u32[]{:S(2)}, u32[]{:S(2)}) collective-permute-start(bf16[4,512,128]{2,1,0:T(8,128)(2,1)} %get-tuple-element.114.refs_0_), channel_id=1, source_target_pairs={{0,16},{16,0},{8,24},{24,8},{1,17},{17,1},{9,25},{25,9},{2,18},{18... | collective-permute-start | bytes 1572872 | tf_op jit(solution)/shard_map/ppermute | solution.py:465
  140.0 18.8 %collective-permute-start.10 = (bf16[4,512,128]{2,1,0:T(8,128)(2,1)S(1)}, bf16[4,512,128]{2,1,0:T(8,128)(2,1)}, u32[]{:S(2)}, u32[]{:S(2)}) collective-permute-start(bf16[4,512,128]{2,1,0:T(8,128)(2,1)S(1)} %collective-permute-done.8.refs_1_), channel_id=1, source_target_pairs={{0,16},{16,0},{8,24},{24,8},{1,17},{17,1},{9,25},{25,9},{2,18},{18... | collective-permute-start | bytes 1572872 | tf_op jit(solution)/shard_map/ppermute | solution.py:464
  142.4 14.7 %collective-permute-start.6 = (bf16[512,128]{1,0:T(8,128)(2,1)S(1)}, bf16[512,128]{1,0:T(8,128)(2,1)S(1)}, u32[]{:S(2)}, u32[]{:S(2)}) collective-permute-start(bf16[512,128]{1,0:T(8,128)(2,1)S(1)} %get-tuple-element.162), channel_id=1, source_target_pairs={{0,2},{1,3},{2,0},{3,1},{4,6},{5,7},{6,4},{7,5},{8,10},{9,11},{10,... | collective-permute-start | bytes 393224 | tf_op jit(solution)/shard_map/ppermute | solution.py:491
  143.5 13.5 %collective-permute-start.7 = (bf16[512,128]{1,0:T(8,128)(2,1)S(1)}, bf16[512,128]{1,0:T(8,128)(2,1)S(1)}, u32[]{:S(2)}, u32[]{:S(2)}) collective-permute-start(bf16[512,128]{1,0:T(8,128)(2,1)S(1)} %get-tuple-element.161), channel_id=1, source_target_pairs={{0,3},{1,0},{2,1},{3,2},{4,7},{5,4},{6,5},{7,6},{8,11},{9,8},{10,9... | collective-permute-start | bytes 393224 | tf_op jit(solution)/shard_map/ppermute | solution.py:491
  161.3 57.9 %all-to-all-start.2 = ((bf16[4,3,512,128]{3,2,1,0:T(8,128)(2,1)}), bf16[4,3,512,128]{3,2,1,0:T(8,128)(2,1)S(1)}, u32[]{:S(2)}, u32[]{:S(2)}) async-start(bf16[4,3,512,128]{3,2,1,0:T(8,128)(2,1)} %pad_maximum_fusion.3), calls=%async_computation.2 | async-start | bytes 3145728 | tf_op jit(solution)/shard_map/all_to_all | solution.py:485
  165.8 136.5 %all-gather.5.cloned.1.call-start = ((), (), s32[]{:S(2)}) async-start(), calls=%async_computation.4 | async-start | bytes 3932160 | tf_op jit(solution)/shard_map/all_gather | solution.py:511
  165.8 14.6 %collective-permute-start.16 = (bf16[4,512,128]{2,1,0:T(8,128)(2,1)}, bf16[4,512,128]{2,1,0:T(8,128)(2,1)S(1)}, u32[]{:S(2)}, u32[]{:S(2)}) collective-permute-start(bf16[4,512,128]{2,1,0:T(8,128)(2,1)} %pad_maximum_fusion.5.refs_0_), channel_id=1, source_target_pairs={{0,16},{16,0},{8,24},{24,8},{1,17},{17,1},{9,25},{25,9},{2,18},{18... | collective-permute-start | bytes 1572872 | tf_op jit(solution)/shard_map/ppermute | solution.py:463
  178.9 14.2 %collective-permute-start.18 = (bf16[4,512,128]{2,1,0:T(8,128)(2,1)}, bf16[4,512,128]{2,1,0:T(8,128)(2,1)S(1)}, u32[]{:S(2)}, u32[]{:S(2)}) collective-permute-start(bf16[4,512,128]{2,1,0:T(8,128)(2,1)} %get-tuple-element.118.refs_4_), channel_id=1, source_target_pairs={{0,8},{8,0},{16,24},{24,16},{1,9},{9,1},{17,25},{25,17},{2,10},{10... | collective-permute-start | bytes 1572872 | tf_op jit(solution)/shard_map/ppermute | solution.py:463
  180.2 37.3 %collective-permute-start.15 = (bf16[4,512,128]{2,1,0:T(8,128)(2,1)S(1)}, bf16[4,512,128]{2,1,0:T(8,128)(2,1)S(1)}, u32[]{:S(2)}, u32[]{:S(2)}) collective-permute-start(bf16[4,512,128]{2,1,0:T(8,128)(2,1)S(1)} %copy-done.6), channel_id=1, source_target_pairs={{0,8},{8,0},{16,24},{24,16},{1,9},{9,1},{17,25},{25,17},{2,10},{10... | collective-permute-start | bytes 1572872 | tf_op jit(solution)/shard_map/ppermute | solution.py:465
  180.4 37.0 %collective-permute-start.17 = (bf16[4,512,128]{2,1,0:T(8,128)(2,1)S(1)}, bf16[4,512,128]{2,1,0:T(8,128)(2,1)S(1)}, u32[]{:S(2)}, u32[]{:S(2)}) collective-permute-start(bf16[4,512,128]{2,1,0:T(8,128)(2,1)S(1)} %collective-permute-done.16.refs_2_), channel_id=1, source_target_pairs={{0,8},{8,0},{16,24},{24,16},{1,9},{9,1},{17,25},{25,17},{2,10},{10... | collective-permute-start | bytes 1572872 | tf_op jit(solution)/shard_map/ppermute | solution.py:464
  181.6 35.8 %collective-permute-start.19 = (bf16[4,512,128]{2,1,0:T(8,128)(2,1)}, bf16[4,512,128]{2,1,0:T(8,128)(2,1)S(1)}, u32[]{:S(2)}, u32[]{:S(2)}) collective-permute-start(bf16[4,512,128]{2,1,0:T(8,128)(2,1)} %get-tuple-element.118.refs_4_), channel_id=1, source_target_pairs={{0,16},{16,0},{8,24},{24,8},{1,17},{17,1},{9,25},{25,9},{2,18},{18... | collective-permute-start | bytes 1572872 | tf_op jit(solution)/shard_map/ppermute | solution.py:465
  193.1 26.1 %collective-permute-start.20 = (bf16[4,512,128]{2,1,0:T(8,128)(2,1)S(1)}, bf16[4,512,128]{2,1,0:T(8,128)(2,1)}, u32[]{:S(2)}, u32[]{:S(2)}) collective-permute-start(bf16[4,512,128]{2,1,0:T(8,128)(2,1)S(1)} %collective-permute-done.18.refs_5_), channel_id=1, source_target_pairs={{0,16},{16,0},{8,24},{24,8},{1,17},{17,1},{9,25},{25,9},{2,18},{18... | collective-permute-start | bytes 1572872 | tf_op jit(solution)/shard_map/ppermute | solution.py:464
  220.6 17.1 %collective-permute-start.22 = (bf16[4,512,128]{2,1,0:T(8,128)(2,1)S(1)}, bf16[4,512,128]{2,1,0:T(8,128)(2,1)S(1)}, u32[]{:S(2)}, u32[]{:S(2)}) collective-permute-start(bf16[4,512,128]{2,1,0:T(8,128)(2,1)S(1)} %pad_maximum_fusion.6.refs_4_), channel_id=1, source_target_pairs={{0,8},{8,0},{16,24},{24,16},{1,9},{9,1},{17,25},{25,17},{2,10},{10... | collective-permute-start | bytes 1572872 | tf_op jit(solution)/shard_map/ppermute | solution.py:512
  221.9 15.8 %collective-permute-start.23 = (bf16[4,512,128]{2,1,0:T(8,128)(2,1)S(1)}, bf16[4,512,128]{2,1,0:T(8,128)(2,1)S(1)}, u32[]{:S(2)}, u32[]{:S(2)}) collective-permute-start(bf16[4,512,128]{2,1,0:T(8,128)(2,1)S(1)} %pad_maximum_fusion.6.refs_4_), channel_id=1, source_target_pairs={{0,16},{16,0},{8,24},{24,8},{1,17},{17,1},{9,25},{25,9},{2,18},{18... | collective-permute-start | bytes 1572872 | tf_op jit(solution)/shard_map/ppermute | solution.py:512
  239.3 27.7 %collective-permute-start.27 = (bf16[4,512,128]{2,1,0:T(8,128)(2,1)S(1)}, bf16[4,512,128]{2,1,0:T(8,128)(2,1)S(1)}, u32[]{:S(2)}, u32[]{:S(2)}) collective-permute-start(bf16[4,512,128]{2,1,0:T(8,128)(2,1)S(1)} %collective-permute-done.23.refs_6_), channel_id=1, source_target_pairs={{0,8},{8,0},{16,24},{24,16},{1,9},{9,1},{17,25},{25,17},{2,10},{10... | collective-permute-start | bytes 1572872 | tf_op jit(solution)/shard_map/ppermute | solution.py:514
  240.6 26.5 %collective-permute-start.28 = (bf16[4,512,128]{2,1,0:T(8,128)(2,1)}, bf16[4,512,128]{2,1,0:T(8,128)(2,1)S(1)}, u32[]{:S(2)}, u32[]{:S(2)}) collective-permute-start(bf16[4,512,128]{2,1,0:T(8,128)(2,1)} %get-tuple-element.134.refs_0_.refs_8_), channel_id=1, source_target_pairs={{0,8},{8,0},{16,24},{24,16},{1,9},{9,1},{17,25},{25,17},{2,10},{10... | collective-permute-start | bytes 1572872 | tf_op jit(solution)/shard_map/ppermute | solution.py:461
  240.8 26.2 %collective-permute-start.29 = (bf16[4,512,128]{2,1,0:T(8,128)(2,1)}, bf16[4,512,128]{2,1,0:T(8,128)(2,1)S(1)}, u32[]{:S(2)}, u32[]{:S(2)}) collective-permute-start(bf16[4,512,128]{2,1,0:T(8,128)(2,1)} %get-tuple-element.134.refs_0_.refs_8_), channel_id=1, source_target_pairs={{0,16},{16,0},{8,24},{24,8},{1,17},{17,1},{9,25},{25,9},{2,18},{18... | collective-permute-start | bytes 1572872 | tf_op jit(solution)/shard_map/ppermute | solution.py:461
  242.0 23.1 %collective-permute-start.25 = (bf16[512,128]{1,0:T(8,128)(2,1)S(1)}, bf16[512,128]{1,0:T(8,128)(2,1)S(1)}, u32[]{:S(2)}, u32[]{:S(2)}) collective-permute-start(bf16[512,128]{1,0:T(8,128)(2,1)S(1)} %get-tuple-element.154), channel_id=1, source_target_pairs={{0,2},{1,3},{2,0},{3,1},{4,6},{5,7},{6,4},{7,5},{8,10},{9,11},{10,... | collective-permute-start | bytes 393224 | tf_op jit(solution)/shard_map/ppermute | solution.py:491
  249.1 17.8 %collective-permute-start.26 = (bf16[512,128]{1,0:T(8,128)(2,1)S(1)}, bf16[512,128]{1,0:T(8,128)(2,1)S(1)}, u32[]{:S(2)}, u32[]{:S(2)}) collective-permute-start(bf16[512,128]{1,0:T(8,128)(2,1)S(1)} %get-tuple-element.153), channel_id=1, source_target_pairs={{0,3},{1,0},{2,1},{3,2},{4,7},{5,4},{6,5},{7,6},{8,11},{9,8},{10,9... | collective-permute-start | bytes 393224 | tf_op jit(solution)/shard_map/ppermute | solution.py:491
  265.1 18.9 %collective-permute-start.33 = (bf16[4,512,128]{2,1,0:T(8,128)(2,1)S(1)}, bf16[4,512,128]{2,1,0:T(8,128)(2,1)S(1)}, u32[]{:S(2)}, u32[]{:S(2)}) collective-permute-start(bf16[4,512,128]{2,1,0:T(8,128)(2,1)S(1)} %copy-done.28), channel_id=1, source_target_pairs={{0,24},{24,0},{8,16},{16,8},{1,25},{25,1},{9,17},{17,9},{2,26},{26... | collective-permute-start | bytes 1572872 | tf_op jit(solution)/shard_map/ppermute | solution.py:461
  267.1 25.4 %collective-permute-start.30 = (bf16[4,512,128]{2,1,0:T(8,128)(2,1)S(1)}, bf16[4,512,128]{2,1,0:T(8,128)(2,1)S(1)}, u32[]{:S(2)}, u32[]{:S(2)}) collective-permute-start(bf16[4,512,128]{2,1,0:T(8,128)(2,1)S(1)} %pad_maximum_fusion.7.refs_0_), channel_id=1, source_target_pairs={{0,8},{8,0},{16,24},{24,16},{1,9},{9,1},{17,25},{25,17},{2,10},{10... | collective-permute-start | bytes 1572872 | tf_op jit(solution)/shard_map/ppermute | solution.py:461
  267.7 33.3 %collective-permute-start.31 = (bf16[4,512,128]{2,1,0:T(8,128)(2,1)S(1)}, bf16[4,512,128]{2,1,0:T(8,128)(2,1)S(1)}, u32[]{:S(2)}, u32[]{:S(2)}) collective-permute-start(bf16[4,512,128]{2,1,0:T(8,128)(2,1)S(1)} %pad_maximum_fusion.7.refs_0_), channel_id=1, source_target_pairs={{0,16},{16,0},{8,24},{24,8},{1,17},{17,1},{9,25},{25,9},{2,18},{18... | collective-permute-start | bytes 1572872 | tf_op jit(solution)/shard_map/ppermute | solution.py:461
  268.0 34.4 %collective-permute-start.32 = (bf16[4,512,128]{2,1,0:T(8,128)(2,1)S(1)}, bf16[4,512,128]{2,1,0:T(8,128)(2,1)}, u32[]{:S(2)}, u32[]{:S(2)}) collective-permute-start(bf16[4,512,128]{2,1,0:T(8,128)(2,1)S(1)} %pad_maximum_fusion.7.refs_0_), channel_id=1, source_target_pairs={{0,24},{24,0},{8,16},{16,8},{1,25},{25,1},{9,17},{17,9},{2,26},{26... | collective-permute-start | bytes 1572872 | tf_op jit(solution)/shard_map/ppermute | solution.py:461
  292.4 21.3 %collective-permute-start.34 = (bf16[2,384,768]{2,1,0:T(8,128)(2,1)S(1)}, bf16[2,384,768]{2,1,0:T(8,128)(2,1)}, u32[]{:S(2)}, u32[]{:S(2)}) collective-permute-start(bf16[2,384,768]{2,1,0:T(8,128)(2,1)S(1)} %pad_maximum_fusion.4), channel_id=1, source_target_pairs={{0,4},{4,0},{1,5},{5,1},{2,6},{6,2},{3,7},{7,3},{8,12},{12,8},{9,1... | collective-permute-start | bytes 3538952 | tf_op jit(solution)/shard_map/ppermute | solution.py:521
  (41 other events, 432.0 us)
Sparse Core Ops, SparseCore 0:
  10.7 92.6 all-gather.2
  219.4 74.5 all-gather.4

commit v5 on v4

--- a/solution.py
+++ b/solution.py
@@ -527,10 +527,11 @@
     sums, early, grad2 = lax.optimization_barrier((sums, early, grad2))
     late = grad(place, grad2, first_cot)
     sums = mix(place, (2,), mix2[:2], out_weight, w_other, sums, jnp.float32, (0, 1))
-    mix2, last_cot, sums = lax.optimization_barrier((mix2, last_cot, sums))
+    first = summed([early, late])
+    mix2, last_cot, sums, first = lax.optimization_barrier((mix2, last_cot, sums, first))
     last = grad(place, grad0 + grad1 + grad2, last_cot)
     mixed_out = mix(place, (2,), mix2[2:], out_weight, w_other, sums, jnp.bfloat16, (2, 3))
-    grad_weight = jnp.concatenate([summed([early, late]), summed([last])], axis=2)
+    grad_weight = jnp.concatenate([first, summed([last])], axis=2)
     grad_weight = grad_weight.reshape(-1, columns)
     return (mixed_out, grad_weight)
 

time: 333 us -> 346 us (1.039)
  waiting for transfers between devices: 141 us -> 153 us
    ppermute x6, waiting for transfers between devices: 0.52 us -> 12.7 us  [over_row(): lax.ppermute(a, 'row', pairs)]
    unnamed x64 -> x66, local copies, waits for them, and re-layouts: 7.02 us -> 7.18 us
  transfers between devices with their start and end apart: 41 -> 41, of which waited for: 16 -> 17; matrix products, arithmetic and copies ran while one was open for 6% -> 5% of each run, Pallas kernels for 30% -> 26%
where the time goes in v5:
time: 346 us; the launch traced here: 344 us
  waiting for transfers between devices  153 us (44%)
  Pallas kernels  100 us (29%)
  starting transfers between devices  48.3 us (14%)
  local copies, waits for them, and re-layouts  14.8 us (4%)
  between operations  14.6 us (4%)
  other arithmetic  12.5 us (4%)
    ppermute x3, waiting for transfers between devices, exchanged(): got = lax.ppermute(send, 'row', X_SWAP)  51.5 us
    ppermute x9, waiting for transfers between devices, attended(): home = [lax.ppermute(out[s], 'ctx', around(s)) for s in range(1, 4)]  45.3 us
    pallas_call x3, Pallas kernels, attend(): pl.pallas_call(_attend_kernel, out_shape=(jax.ShapeDtypeStruct((4, BLOCK,...  35.5 us
    pallas_call x3, Pallas kernels, mix(): pl.pallas_call(functools.partial(_mix_kernel, heads, sides, len(added)),...  29.1 us
    pallas_call x3, Pallas kernels, grad(): pl.pallas_call(functools.partial(_grad_kernel, count), grid=(4,), out_sha...  26 us
    ppermute x3, waiting for transfers between devices, over_row(): near = lax.ppermute(a, 'row', first)  19.6 us
    all_to_all x3, waiting for transfers between devices, over_ctx(): return lax.all_to_all(pieces, 'ctx', 0, 0, tiled=True)  19.1 us
    all_to_all x3, starting transfers between devices, over_ctx(): return lax.all_to_all(pieces, 'ctx', 0, 0, tiled=True)  15.4 us
  transfers between devices with their start and end apart: 41, of which 17 were waited for; matrix products, arithmetic and copies ran while one was open for 5% of the time, Pallas kernels for 26%

profile of v5, /device:TPU:25, one launch (start us, length us, event | category | flops | bytes accessed | tf_op | source)
XLA Modules:
  0.0 343.9 jit_solution(5362197735220684708)
XLA Ops:
  7.9 2.6 fusion.1
  11.3 3.2 pack.3
  15.6 18.3 %collective-permute-done = bf16[2,3,512,128]{3,2,1,0:T(8,128)(2,1)S(1)} collective-permute-done((bf16[2,3,512,128]{3,2,1,0:T(8,128)(2,1)}, bf16[2,3,512,128]{3,2,1,0:T(8,128)(2,1)S(1)}, u32[]{:S(2)}, u32[]{:S(2)}) %collective-permute-start) | collective-permute-done | bytes 786464 | tf_op jit(solution)/shard_map/ppermute | solution.py:478
  36.4 4.5 %all-to-all-start = ((bf16[4,3,512,128]{3,2,1,0:T(8,128)(2,1)}), bf16[4,3,512,128]{3,2,1,0:T(8,128)(2,1)S(1)}, u32[]{:S(2)}, u32[]{:S(2)}) async-start(bf16[4,3,512,128]{3,2,1,0:T(8,128)(2,1)} %pad_maximum_fusion.1), calls=%async_computation | async-start | bytes 3145728 | tf_op jit(solution)/shard_map/all_to_all | solution.py:485
  40.9 3.2 pack.4
  44.1 3.3 pack.5
  49.0 16.4 %collective-permute-done.1 = bf16[2,3,512,128]{3,2,1,0:T(8,128)(2,1)S(1)} collective-permute-done((bf16[2,3,512,128]{3,2,1,0:T(8,128)(2,1)S(1)}, bf16[2,3,512,128]{3,2,1,0:T(8,128)(2,1)S(1)}, u32[]{:S(2)}, u32[]{:S(2)}) %collective-permute-start.1) | collective-permute-done | bytes 786464 | tf_op jit(solution)/shard_map/ppermute | solution.py:478
  65.4 16.9 %collective-permute-done.3 = bf16[2,3,512,128]{3,2,1,0:T(8,128)(2,1)S(1)} collective-permute-done((bf16[2,3,512,128]{3,2,1,0:T(8,128)(2,1)}, bf16[2,3,512,128]{3,2,1,0:T(8,128)(2,1)S(1)}, u32[]{:S(2)}, u32[]{:S(2)}) %collective-permute-start.3) | collective-permute-done | bytes 786464 | tf_op jit(solution)/shard_map/ppermute | solution.py:478
  86.1 19.1 %all-to-all-done.refs_0_ = bf16[4,3,512,128]{3,2,1,0:T(8,128)(2,1)S(1)} async-done(((bf16[4,3,512,128]{3,2,1,0:T(8,128)(2,1)}), bf16[4,3,512,128]{3,2,1,0:T(8,128)(2,1)S(1)}, u32[]{:S(2)}, u32[]{:S(2)}) %all-to-all-start) | async-done | bytes 1572896 | tf_op jit(solution)/shard_map/all_to_all | solution.py:485
  105.2 6.3 %all-to-all-start.1 = ((bf16[4,3,512,128]{3,2,1,0:T(8,128)(2,1)}), bf16[4,3,512,128]{3,2,1,0:T(8,128)(2,1)S(1)}, u32[]{:S(2)}, u32[]{:S(2)}) async-start(bf16[4,3,512,128]{3,2,1,0:T(8,128)(2,1)} %pad_maximum_fusion.2), calls=%async_computation.1 | async-start | bytes 3145728 | tf_op jit(solution)/shard_map/all_to_all | solution.py:485
  112.9 3.3 collective-permute-done.4.refs_1_
  117.1 11.9 %attend.3 = (bf16[4,512,128]{2,1,0:T(8,128)(2,1)}, bf16[4,512,128]{2,1,0:T(8,128)(2,1)}) custom-call(s32[4]{0:T(128)} %pad_add_fusion.place, s32[8,8]{1,0:T(8,128)} %mask.5, bf16[4,3,512,128]{3,2,1,0:T(8,128)(2,1)} %copy-done.2, bf16[4,2,512,128]{3,2,1,0:T(8,128)(2,1)} %copy-done.23), custom_call_target="tpu_custom_call" | custom-call | flops 2684354560 | bytes 4194304 | tf_op jit(solution)/shard_map/attend/pallas_call | solution.py:233
  131.6 8.4 %collective-permute-done.8.refs_1_ = bf16[4,512,128]{2,1,0:T(8,128)(2,1)S(1)} collective-permute-done((bf16[4,512,128]{2,1,0:T(8,128)(2,1)}, bf16[4,512,128]{2,1,0:T(8,128)(2,1)S(1)}, u32[]{:S(2)}, u32[]{:S(2)}) %collective-permute-start.8) | collective-permute-done | bytes 524320 | tf_op jit(solution)/shard_map/ppermute | solution.py:463
  145.4 4.7 %collective-permute-done.5 = bf16[512,128]{1,0:T(8,128)(2,1)S(1)} collective-permute-done((bf16[512,128]{1,0:T(8,128)(2,1)S(1)}, bf16[512,128]{1,0:T(8,128)(2,1)S(1)}, u32[]{:S(2)}, u32[]{:S(2)}) %collective-permute-start.5) | collective-permute-done | bytes 131104 | tf_op jit(solution)/shard_map/ppermute | solution.py:491
  150.0 7.1 %collective-permute-done.6 = bf16[512,128]{1,0:T(8,128)(2,1)S(1)} collective-permute-done((bf16[512,128]{1,0:T(8,128)(2,1)S(1)}, bf16[512,128]{1,0:T(8,128)(2,1)S(1)}, u32[]{:S(2)}, u32[]{:S(2)}) %collective-permute-start.6) | collective-permute-done | bytes 131104 | tf_op jit(solution)/shard_map/ppermute | solution.py:491
  161.3 4.5 %all-to-all-start.2 = ((bf16[4,3,512,128]{3,2,1,0:T(8,128)(2,1)}), bf16[4,3,512,128]{3,2,1,0:T(8,128)(2,1)S(1)}, u32[]{:S(2)}, u32[]{:S(2)}) async-start(bf16[4,3,512,128]{3,2,1,0:T(8,128)(2,1)} %pad_maximum_fusion.3), calls=%async_computation.2 | async-start | bytes 3145728 | tf_op jit(solution)/shard_map/all_to_all | solution.py:485
  167.0 11.8 %attend.4 = (bf16[4,512,128]{2,1,0:T(8,128)(2,1)}, bf16[4,512,128]{2,1,0:T(8,128)(2,1)}) custom-call(s32[4]{0:T(128)} %pad_add_fusion.place, s32[8,8]{1,0:T(8,128)} %mask.5, bf16[4,3,512,128]{3,2,1,0:T(8,128)(2,1)} %copy-done.1, bf16[4,2,512,128]{3,2,1,0:T(8,128)(2,1)} %collective-permute-done.11.refs_1_), custom_call_target="tpu_custom_call" | custom-call | flops 2684354560 | bytes 4194304 | tf_op jit(solution)/shard_map/attend/pallas_call | solution.py:233
  181.8 11.2 %collective-permute-done.18.refs_5_ = bf16[4,512,128]{2,1,0:T(8,128)(2,1)S(1)} collective-permute-done((bf16[4,512,128]{2,1,0:T(8,128)(2,1)}, bf16[4,512,128]{2,1,0:T(8,128)(2,1)S(1)}, u32[]{:S(2)}, u32[]{:S(2)}) %collective-permute-start.18) | collective-permute-done | bytes 524320 | tf_op jit(solution)/shard_map/ppermute | solution.py:463
  194.5 9.6 %collective-permute-done.12 = bf16[512,128]{1,0:T(8,128)(2,1)S(1)} collective-permute-done((bf16[512,128]{1,0:T(8,128)(2,1)S(1)}, bf16[512,128]{1,0:T(8,128)(2,1)S(1)}, u32[]{:S(2)}, u32[]{:S(2)}) %collective-permute-start.12) | collective-permute-done | bytes 131104 | tf_op jit(solution)/shard_map/ppermute | solution.py:491
  204.1 7.6 %collective-permute-done.13 = bf16[512,128]{1,0:T(8,128)(2,1)S(1)} collective-permute-done((bf16[512,128]{1,0:T(8,128)(2,1)S(1)}, bf16[512,128]{1,0:T(8,128)(2,1)S(1)}, u32[]{:S(2)}, u32[]{:S(2)}) %collective-permute-start.13) | collective-permute-done | bytes 131104 | tf_op jit(solution)/shard_map/ppermute | solution.py:491
  211.7 5.6 %collective-permute-done.14 = bf16[512,128]{1,0:T(8,128)(2,1)S(1)} collective-permute-done((bf16[512,128]{1,0:T(8,128)(2,1)S(1)}, bf16[512,128]{1,0:T(8,128)(2,1)S(1)}, u32[]{:S(2)}, u32[]{:S(2)}) %collective-permute-start.14) | collective-permute-done | bytes 131104 | tf_op jit(solution)/shard_map/ppermute | solution.py:491
  226.0 11.8 %attend.5 = (bf16[4,512,128]{2,1,0:T(8,128)(2,1)}, bf16[4,512,128]{2,1,0:T(8,128)(2,1)}) custom-call(s32[4]{0:T(128)} %pad_add_fusion.place, s32[8,8]{1,0:T(8,128)} %mask.5, bf16[4,3,512,128]{3,2,1,0:T(8,128)(2,1)} %copy-done, bf16[4,2,512,128]{3,2,1,0:T(8,128)(2,1)} %copy-done.22), custom_call_target="tpu_custom_call" | custom-call | flops 2684354560 | bytes 4194304 | tf_op jit(solution)/shard_map/attend/pallas_call | solution.py:233
  242.2 7.1 %collective-permute-done.24 = bf16[512,128]{1,0:T(8,128)(2,1)S(1)} collective-permute-done((bf16[512,128]{1,0:T(8,128)(2,1)S(1)}, bf16[512,128]{1,0:T(8,128)(2,1)S(1)}, u32[]{:S(2)}, u32[]{:S(2)}) %collective-permute-start.24) | collective-permute-done | bytes 131104 | tf_op jit(solution)/shard_map/ppermute | solution.py:491
  249.3 3.6 %collective-permute-start.26 = (bf16[512,128]{1,0:T(8,128)(2,1)S(1)}, bf16[512,128]{1,0:T(8,128)(2,1)S(1)}, u32[]{:S(2)}, u32[]{:S(2)}) collective-permute-start(bf16[512,128]{1,0:T(8,128)(2,1)S(1)} %get-tuple-element.155), channel_id=1, source_target_pairs={{0,3},{1,0},{2,1},{3,2},{4,7},{5,4},{6,5},{7,6},{8,11},{9,8},{10,9... | collective-permute-start | bytes 393224 | tf_op jit(solution)/shard_map/ppermute | solution.py:491
  252.9 8.6 %grad.3 = (bf16[512,768]{1,0:T(8,128)(2,1)}, f32[512,768]{1,0:T(8,128)}) custom-call(s32[4]{0:T(128)} %pad_add_fusion.place, bf16[4,512,128]{2,1,0:T(8,128)(2,1)} %get-tuple-element.115.refs_0_, bf16[4,512,128]{2,1,0:T(8,128)(2,1)} %copy-done.25, bf16[4,512,128]{2,1,0:T(8,128)(2,1)} %copy-done.26, bf16[4,512,128]{2,1,0:T(8,128)(2,1)} %collective-permute-done.10.refs_3_, ...), custom_call_target="tpu_custom_call" | custom-call | flops 3221225472 | bytes 11534336 | tf_op jit(solution)/shard_map/grad/pallas_call | solution.py:421
  261.6 3.7 %collective-permute-done.25 = bf16[512,128]{1,0:T(8,128)(2,1)S(1)} collective-permute-done((bf16[512,128]{1,0:T(8,128)(2,1)S(1)}, bf16[512,128]{1,0:T(8,128)(2,1)S(1)}, u32[]{:S(2)}, u32[]{:S(2)}) %collective-permute-start.25) | collective-permute-done | bytes 131104 | tf_op jit(solution)/shard_map/ppermute | solution.py:491
  268.1 14.2 %mix.3.refs_4_ = f32[512,1536]{1,0:T(8,128)} custom-call(s32[4]{0:T(128)} %pad_add_fusion.place, bf16[4,512,128]{2,1,0:T(8,128)(2,1)} %pad_maximum_fusion.5.refs_0_, bf16[4,512,128]{2,1,0:T(8,128)(2,1)} %copy-done.14, bf16[4,512,128]{2,1,0:T(8,128)(2,1)} %copy-done.13, bf16[4,512,128]{2,1,0:T(8,128)(2,1)} %copy-done.15, bf16[4,512,128]{2,1,0:T(8,128)(2,1)} %copy-done.7, ...), custom_call_target="tpu_custom_call" | custom-call | flops 6442450944 | bytes 18874368 | tf_op jit(solution)/shard_map/mix/pallas_call | solution.py:346
  283.1 6.5 %grad.4 = (bf16[256,768]{1,0:T(8,128)(2,1)}, f32[256,768]{1,0:T(8,128)}) custom-call(s32[4]{0:T(128)} %pad_add_fusion.place, bf16[4,512,128]{2,1,0:T(8,128)(2,1)} %get-tuple-element.132.refs_0_.refs_8_, bf16[4,512,128]{2,1,0:T(8,128)(2,1)} %copy-done.30, bf16[4,512,128]{2,1,0:T(8,128)(2,1)} %copy-done.31, bf16[4,512,128]{2,1,0:T(8,128)(2,1)} %copy-done.32, ...), custom_call_target="tpu_custom_call" | custom-call | flops 1610612736 | bytes 7340032 | tf_op jit(solution)/shard_map/grad/pallas_call | solution.py:421
  293.5 10.4 %collective-permute-done.30.refs_1_ = bf16[4,512,128]{2,1,0:T(8,128)(2,1)S(1)} collective-permute-done((bf16[4,512,128]{2,1,0:T(8,128)(2,1)S(1)}, bf16[4,512,128]{2,1,0:T(8,128)(2,1)S(1)}, u32[]{:S(2)}, u32[]{:S(2)}) %collective-permute-start.30) | collective-permute-done | bytes 524320 | tf_op jit(solution)/shard_map/ppermute | solution.py:461
  304.7 7.7 %mix.4.refs_4_ = f32[512,1536]{1,0:T(8,128)} custom-call(s32[4]{0:T(128)} %pad_add_fusion.place, bf16[4,512,128]{2,1,0:T(8,128)(2,1)} %copy-done.8, bf16[4,512,128]{2,1,0:T(8,128)(2,1)} %copy-done.21, bf16[3072,1536]{1,0:T(8,128)(2,1)} %refs_2_.9, bf16[3072,1536]{1,0:T(8,128)(2,1)} %collective-permute-done.2.refs_9_.refs_3_, f32[512,1536]{1,0:T(8,128)} %mix.3.refs_4_), custom_call_target="tpu_custom_call" | custom-call | flops 1610612736 | bytes 9437184 | tf_op jit(solution)/shard_map/mix/pallas_call | solution.py:346
  315.0 10.9 %grad.5 = (bf16[768,768]{1,0:T(8,128)(2,1)}, f32[768,768]{1,0:T(8,128)}) custom-call(s32[4]{0:T(128)} %pad_add_fusion.place, bf16[4,512,128]{2,1,0:T(8,128)(2,1)} %get-tuple-element.115.refs_0_, bf16[4,512,128]{2,1,0:T(8,128)(2,1)} %copy-done.25, bf16[4,512,128]{2,1,0:T(8,128)(2,1)} %copy-done.26, bf16[4,512,128]{2,1,0:T(8,128)(2,1)} %collective-permute-done.10.refs_3_, ...), custom_call_target="tpu_custom_call" | custom-call | flops 4831838208 | bytes 15728640 | tf_op jit(solution)/shard_map/grad/pallas_call | solution.py:421
  327.9 7.2 %mix.5 = bf16[512,1536]{1,0:T(8,128)(2,1)} custom-call(s32[4]{0:T(128)} %pad_add_fusion.place, bf16[4,512,128]{2,1,0:T(8,128)(2,1)} %copy-done.19, bf16[4,512,128]{2,1,0:T(8,128)(2,1)} %copy-done.20, bf16[3072,1536]{1,0:T(8,128)(2,1)} %refs_2_.9, bf16[3072,1536]{1,0:T(8,128)(2,1)} %collective-permute-done.2.refs_9_.refs_3_, f32[512,1536]{1,0:T(8,128)} %mix.4.refs_4_), custom_call_target="tpu_custom_call" | custom-call | flops 1610612736 | bytes 9437184 | tf_op jit(solution)/shard_map/mix/pallas_call | solution.py:346
  (150 shorter events, 58.1 us)
Async XLA Ops:
  7.2 98.1 %all-gather.3.cloned.1.call-start = ((), (), s32[]{:S(2)}) async-start(), calls=%async_computation.3 | async-start | bytes 3932160 | tf_op jit(solution)/shard_map/all_gather | solution.py:494
  7.2 98.0 %collective-permute-start.2 = (bf16[3072,1536]{1,0:T(8,128)(2,1)}, bf16[3072,1536]{1,0:T(8,128)(2,1)}, u32[]{:S(2)}, u32[]{:S(2)}) collective-permute-start(bf16[3072,1536]{1,0:T(8,128)(2,1)} %refs_2_.9), channel_id=1, source_target_pairs={{0,4},{4,0},{1,5},{5,1},{2,6},{6,2},{3,7},{7,3},{8,12},{12,8},{9,1... | collective-permute-start | bytes 28311560 | tf_op jit(solution)/shard_map/ppermute | solution.py:499
  14.4 19.5 %collective-permute-start = (bf16[2,3,512,128]{3,2,1,0:T(8,128)(2,1)}, bf16[2,3,512,128]{3,2,1,0:T(8,128)(2,1)S(1)}, u32[]{:S(2)}, u32[]{:S(2)}) collective-permute-start(bf16[2,3,512,128]{3,2,1,0:T(8,128)(2,1)} %get-tuple-element.75), channel_id=1, source_target_pairs={{0,8},{8,0},{16,24},{24,16},{1,9},{9,1},{17,25},{25,17},{2,10},{10... | collective-permute-start | bytes 2359304 | tf_op jit(solution)/shard_map/ppermute | solution.py:478
  36.4 68.8 %all-to-all-start = ((bf16[4,3,512,128]{3,2,1,0:T(8,128)(2,1)}), bf16[4,3,512,128]{3,2,1,0:T(8,128)(2,1)S(1)}, u32[]{:S(2)}, u32[]{:S(2)}) async-start(bf16[4,3,512,128]{3,2,1,0:T(8,128)(2,1)} %pad_maximum_fusion.1), calls=%async_computation | async-start | bytes 3145728 | tf_op jit(solution)/shard_map/all_to_all | solution.py:485
  47.5 17.9 %collective-permute-start.1 = (bf16[2,3,512,128]{3,2,1,0:T(8,128)(2,1)S(1)}, bf16[2,3,512,128]{3,2,1,0:T(8,128)(2,1)S(1)}, u32[]{:S(2)}, u32[]{:S(2)}) collective-permute-start(bf16[2,3,512,128]{3,2,1,0:T(8,128)(2,1)S(1)} %copy-done.24), channel_id=1, source_target_pairs={{0,8},{8,0},{16,24},{24,16},{1,9},{9,1},{17,25},{25,17},{2,10},{10... | collective-permute-start | bytes 2359304 | tf_op jit(solution)/shard_map/ppermute | solution.py:478
  48.7 33.5 %collective-permute-start.3 = (bf16[2,3,512,128]{3,2,1,0:T(8,128)(2,1)}, bf16[2,3,512,128]{3,2,1,0:T(8,128)(2,1)S(1)}, u32[]{:S(2)}, u32[]{:S(2)}) collective-permute-start(bf16[2,3,512,128]{3,2,1,0:T(8,128)(2,1)} %get-tuple-element.83), channel_id=1, source_target_pairs={{0,8},{8,0},{16,24},{24,16},{1,9},{9,1},{17,25},{25,17},{2,10},{10... | collective-permute-start | bytes 2359304 | tf_op jit(solution)/shard_map/ppermute | solution.py:478
  105.2 53.6 %all-to-all-start.1 = ((bf16[4,3,512,128]{3,2,1,0:T(8,128)(2,1)}), bf16[4,3,512,128]{3,2,1,0:T(8,128)(2,1)S(1)}, u32[]{:S(2)}, u32[]{:S(2)}) async-start(bf16[4,3,512,128]{3,2,1,0:T(8,128)(2,1)} %pad_maximum_fusion.2), calls=%async_computation.1 | async-start | bytes 3145728 | tf_op jit(solution)/shard_map/all_to_all | solution.py:485
  129.1 10.9 %collective-permute-start.8 = (bf16[4,512,128]{2,1,0:T(8,128)(2,1)}, bf16[4,512,128]{2,1,0:T(8,128)(2,1)S(1)}, u32[]{:S(2)}, u32[]{:S(2)}) collective-permute-start(bf16[4,512,128]{2,1,0:T(8,128)(2,1)} %get-tuple-element.115.refs_0_), channel_id=1, source_target_pairs={{0,8},{8,0},{16,24},{24,16},{1,9},{9,1},{17,25},{25,17},{2,10},{10... | collective-permute-start | bytes 1572872 | tf_op jit(solution)/shard_map/ppermute | solution.py:463
  130.3 27.7 %collective-permute-start.9 = (bf16[4,512,128]{2,1,0:T(8,128)(2,1)}, bf16[4,512,128]{2,1,0:T(8,128)(2,1)S(1)}, u32[]{:S(2)}, u32[]{:S(2)}) collective-permute-start(bf16[4,512,128]{2,1,0:T(8,128)(2,1)} %get-tuple-element.115.refs_0_), channel_id=1, source_target_pairs={{0,16},{16,0},{8,24},{24,8},{1,17},{17,1},{9,25},{25,9},{2,18},{18... | collective-permute-start | bytes 1572872 | tf_op jit(solution)/shard_map/ppermute | solution.py:465
  139.9 18.9 %collective-permute-start.10 = (bf16[4,512,128]{2,1,0:T(8,128)(2,1)S(1)}, bf16[4,512,128]{2,1,0:T(8,128)(2,1)}, u32[]{:S(2)}, u32[]{:S(2)}) collective-permute-start(bf16[4,512,128]{2,1,0:T(8,128)(2,1)S(1)} %collective-permute-done.8.refs_1_), channel_id=1, source_target_pairs={{0,16},{16,0},{8,24},{24,8},{1,17},{17,1},{9,25},{25,9},{2,18},{18... | collective-permute-start | bytes 1572872 | tf_op jit(solution)/shard_map/ppermute | solution.py:464
  142.4 14.7 %collective-permute-start.6 = (bf16[512,128]{1,0:T(8,128)(2,1)S(1)}, bf16[512,128]{1,0:T(8,128)(2,1)S(1)}, u32[]{:S(2)}, u32[]{:S(2)}) collective-permute-start(bf16[512,128]{1,0:T(8,128)(2,1)S(1)} %get-tuple-element.164), channel_id=1, source_target_pairs={{0,2},{1,3},{2,0},{3,1},{4,6},{5,7},{6,4},{7,5},{8,10},{9,11},{10,... | collective-permute-start | bytes 393224 | tf_op jit(solution)/shard_map/ppermute | solution.py:491
  143.5 13.6 %collective-permute-start.7 = (bf16[512,128]{1,0:T(8,128)(2,1)S(1)}, bf16[512,128]{1,0:T(8,128)(2,1)S(1)}, u32[]{:S(2)}, u32[]{:S(2)}) collective-permute-start(bf16[512,128]{1,0:T(8,128)(2,1)S(1)} %get-tuple-element.163), channel_id=1, source_target_pairs={{0,3},{1,0},{2,1},{3,2},{4,7},{5,4},{6,5},{7,6},{8,11},{9,8},{10,9... | collective-permute-start | bytes 393224 | tf_op jit(solution)/shard_map/ppermute | solution.py:491
  161.3 58.1 %all-to-all-start.2 = ((bf16[4,3,512,128]{3,2,1,0:T(8,128)(2,1)}), bf16[4,3,512,128]{3,2,1,0:T(8,128)(2,1)S(1)}, u32[]{:S(2)}, u32[]{:S(2)}) async-start(bf16[4,3,512,128]{3,2,1,0:T(8,128)(2,1)} %pad_maximum_fusion.3), calls=%async_computation.2 | async-start | bytes 3145728 | tf_op jit(solution)/shard_map/all_to_all | solution.py:485
  165.8 149.1 %all-gather.5.cloned.1.call-start = ((), (), s32[]{:S(2)}) async-start(), calls=%async_computation.4 | async-start | bytes 3932160 | tf_op jit(solution)/shard_map/all_gather | solution.py:511
  165.8 14.6 %collective-permute-start.16 = (bf16[4,512,128]{2,1,0:T(8,128)(2,1)}, bf16[4,512,128]{2,1,0:T(8,128)(2,1)S(1)}, u32[]{:S(2)}, u32[]{:S(2)}) collective-permute-start(bf16[4,512,128]{2,1,0:T(8,128)(2,1)} %pad_maximum_fusion.5.refs_0_), channel_id=1, source_target_pairs={{0,16},{16,0},{8,24},{24,8},{1,17},{17,1},{9,25},{25,9},{2,18},{18... | collective-permute-start | bytes 1572872 | tf_op jit(solution)/shard_map/ppermute | solution.py:463
  178.8 14.2 %collective-permute-start.18 = (bf16[4,512,128]{2,1,0:T(8,128)(2,1)}, bf16[4,512,128]{2,1,0:T(8,128)(2,1)S(1)}, u32[]{:S(2)}, u32[]{:S(2)}) collective-permute-start(bf16[4,512,128]{2,1,0:T(8,128)(2,1)} %get-tuple-element.119.refs_4_), channel_id=1, source_target_pairs={{0,8},{8,0},{16,24},{24,16},{1,9},{9,1},{17,25},{25,17},{2,10},{10... | collective-permute-start | bytes 1572872 | tf_op jit(solution)/shard_map/ppermute | solution.py:463
  180.1 37.3 %collective-permute-start.15 = (bf16[4,512,128]{2,1,0:T(8,128)(2,1)S(1)}, bf16[4,512,128]{2,1,0:T(8,128)(2,1)S(1)}, u32[]{:S(2)}, u32[]{:S(2)}) collective-permute-start(bf16[4,512,128]{2,1,0:T(8,128)(2,1)S(1)} %copy-done.6), channel_id=1, source_target_pairs={{0,8},{8,0},{16,24},{24,16},{1,9},{9,1},{17,25},{25,17},{2,10},{10... | collective-permute-start | bytes 1572872 | tf_op jit(solution)/shard_map/ppermute | solution.py:465
  180.4 37.1 %collective-permute-start.17 = (bf16[4,512,128]{2,1,0:T(8,128)(2,1)S(1)}, bf16[4,512,128]{2,1,0:T(8,128)(2,1)S(1)}, u32[]{:S(2)}, u32[]{:S(2)}) collective-permute-start(bf16[4,512,128]{2,1,0:T(8,128)(2,1)S(1)} %collective-permute-done.16.refs_2_), channel_id=1, source_target_pairs={{0,8},{8,0},{16,24},{24,16},{1,9},{9,1},{17,25},{25,17},{2,10},{10... | collective-permute-start | bytes 1572872 | tf_op jit(solution)/shard_map/ppermute | solution.py:464
  181.6 35.9 %collective-permute-start.19 = (bf16[4,512,128]{2,1,0:T(8,128)(2,1)}, bf16[4,512,128]{2,1,0:T(8,128)(2,1)S(1)}, u32[]{:S(2)}, u32[]{:S(2)}) collective-permute-start(bf16[4,512,128]{2,1,0:T(8,128)(2,1)} %get-tuple-element.119.refs_4_), channel_id=1, source_target_pairs={{0,16},{16,0},{8,24},{24,8},{1,17},{17,1},{9,25},{25,9},{2,18},{18... | collective-permute-start | bytes 1572872 | tf_op jit(solution)/shard_map/ppermute | solution.py:465
  193.1 26.3 %collective-permute-start.20 = (bf16[4,512,128]{2,1,0:T(8,128)(2,1)S(1)}, bf16[4,512,128]{2,1,0:T(8,128)(2,1)}, u32[]{:S(2)}, u32[]{:S(2)}) collective-permute-start(bf16[4,512,128]{2,1,0:T(8,128)(2,1)S(1)} %collective-permute-done.18.refs_5_), channel_id=1, source_target_pairs={{0,16},{16,0},{8,24},{24,8},{1,17},{17,1},{9,25},{25,9},{2,18},{18... | collective-permute-start | bytes 1572872 | tf_op jit(solution)/shard_map/ppermute | solution.py:464
  220.8 17.0 %collective-permute-start.22 = (bf16[4,512,128]{2,1,0:T(8,128)(2,1)S(1)}, bf16[4,512,128]{2,1,0:T(8,128)(2,1)S(1)}, u32[]{:S(2)}, u32[]{:S(2)}) collective-permute-start(bf16[4,512,128]{2,1,0:T(8,128)(2,1)S(1)} %pad_maximum_fusion.6.refs_4_), channel_id=1, source_target_pairs={{0,8},{8,0},{16,24},{24,16},{1,9},{9,1},{17,25},{25,17},{2,10},{10... | collective-permute-start | bytes 1572872 | tf_op jit(solution)/shard_map/ppermute | solution.py:512
  222.1 15.8 %collective-permute-start.23 = (bf16[4,512,128]{2,1,0:T(8,128)(2,1)S(1)}, bf16[4,512,128]{2,1,0:T(8,128)(2,1)S(1)}, u32[]{:S(2)}, u32[]{:S(2)}) collective-permute-start(bf16[4,512,128]{2,1,0:T(8,128)(2,1)S(1)} %pad_maximum_fusion.6.refs_4_), channel_id=1, source_target_pairs={{0,16},{16,0},{8,24},{24,8},{1,17},{17,1},{9,25},{25,9},{2,18},{18... | collective-permute-start | bytes 1572872 | tf_op jit(solution)/shard_map/ppermute | solution.py:512
  239.4 27.8 %collective-permute-start.27 = (bf16[4,512,128]{2,1,0:T(8,128)(2,1)S(1)}, bf16[4,512,128]{2,1,0:T(8,128)(2,1)S(1)}, u32[]{:S(2)}, u32[]{:S(2)}) collective-permute-start(bf16[4,512,128]{2,1,0:T(8,128)(2,1)S(1)} %collective-permute-done.23.refs_6_), channel_id=1, source_target_pairs={{0,8},{8,0},{16,24},{24,16},{1,9},{9,1},{17,25},{25,17},{2,10},{10... | collective-permute-start | bytes 1572872 | tf_op jit(solution)/shard_map/ppermute | solution.py:514
  240.7 26.5 %collective-permute-start.28 = (bf16[4,512,128]{2,1,0:T(8,128)(2,1)}, bf16[4,512,128]{2,1,0:T(8,128)(2,1)S(1)}, u32[]{:S(2)}, u32[]{:S(2)}) collective-permute-start(bf16[4,512,128]{2,1,0:T(8,128)(2,1)} %get-tuple-element.132.refs_0_.refs_8_), channel_id=1, source_target_pairs={{0,8},{8,0},{16,24},{24,16},{1,9},{9,1},{17,25},{25,17},{2,10},{10... | collective-permute-start | bytes 1572872 | tf_op jit(solution)/shard_map/ppermute | solution.py:461
  241.0 26.3 %collective-permute-start.29 = (bf16[4,512,128]{2,1,0:T(8,128)(2,1)}, bf16[4,512,128]{2,1,0:T(8,128)(2,1)S(1)}, u32[]{:S(2)}, u32[]{:S(2)}) collective-permute-start(bf16[4,512,128]{2,1,0:T(8,128)(2,1)} %get-tuple-element.132.refs_0_.refs_8_), channel_id=1, source_target_pairs={{0,16},{16,0},{8,24},{24,8},{1,17},{17,1},{9,25},{25,9},{2,18},{18... | collective-permute-start | bytes 1572872 | tf_op jit(solution)/shard_map/ppermute | solution.py:461
  242.2 23.1 %collective-permute-start.25 = (bf16[512,128]{1,0:T(8,128)(2,1)S(1)}, bf16[512,128]{1,0:T(8,128)(2,1)S(1)}, u32[]{:S(2)}, u32[]{:S(2)}) collective-permute-start(bf16[512,128]{1,0:T(8,128)(2,1)S(1)} %get-tuple-element.156), channel_id=1, source_target_pairs={{0,2},{1,3},{2,0},{3,1},{4,6},{5,7},{6,4},{7,5},{8,10},{9,11},{10,... | collective-permute-start | bytes 393224 | tf_op jit(solution)/shard_map/ppermute | solution.py:491
  249.3 17.8 %collective-permute-start.26 = (bf16[512,128]{1,0:T(8,128)(2,1)S(1)}, bf16[512,128]{1,0:T(8,128)(2,1)S(1)}, u32[]{:S(2)}, u32[]{:S(2)}) collective-permute-start(bf16[512,128]{1,0:T(8,128)(2,1)S(1)} %get-tuple-element.155), channel_id=1, source_target_pairs={{0,3},{1,0},{2,1},{3,2},{4,7},{5,4},{6,5},{7,6},{8,11},{9,8},{10,9... | collective-permute-start | bytes 393224 | tf_op jit(solution)/shard_map/ppermute | solution.py:491
  265.3 17.0 %collective-permute-start.33 = (bf16[4,512,128]{2,1,0:T(8,128)(2,1)S(1)}, bf16[4,512,128]{2,1,0:T(8,128)(2,1)S(1)}, u32[]{:S(2)}, u32[]{:S(2)}) collective-permute-start(bf16[4,512,128]{2,1,0:T(8,128)(2,1)S(1)} %copy-done.29), channel_id=1, source_target_pairs={{0,24},{24,0},{8,16},{16,8},{1,25},{25,1},{9,17},{17,9},{2,26},{26... | collective-permute-start | bytes 1572872 | tf_op jit(solution)/shard_map/ppermute | solution.py:461
  290.7 21.7 %collective-permute-start.34 = (bf16[2,384,768]{2,1,0:T(8,128)(2,1)S(1)}, bf16[2,384,768]{2,1,0:T(8,128)(2,1)S(1)}, u32[]{:S(2)}, u32[]{:S(2)}) collective-permute-start(bf16[2,384,768]{2,1,0:T(8,128)(2,1)S(1)} %pad_maximum_fusion.4), channel_id=1, source_target_pairs={{0,4},{4,0},{1,5},{5,1},{2,6},{6,2},{3,7},{7,3},{8,12},{12,8},{9,1... | collective-permute-start | bytes 3538952 | tf_op jit(solution)/shard_map/ppermute | solution.py:521
  290.8 13.1 %collective-permute-start.30 = (bf16[4,512,128]{2,1,0:T(8,128)(2,1)S(1)}, bf16[4,512,128]{2,1,0:T(8,128)(2,1)S(1)}, u32[]{:S(2)}, u32[]{:S(2)}) collective-permute-start(bf16[4,512,128]{2,1,0:T(8,128)(2,1)S(1)} %pad_maximum_fusion.7.refs_0_), channel_id=1, source_target_pairs={{0,8},{8,0},{16,24},{24,16},{1,9},{9,1},{17,25},{25,17},{2,10},{10... | collective-permute-start | bytes 1572872 | tf_op jit(solution)/shard_map/ppermute | solution.py:461
  291.4 21.3 %collective-permute-start.31 = (bf16[4,512,128]{2,1,0:T(8,128)(2,1)S(1)}, bf16[4,512,128]{2,1,0:T(8,128)(2,1)S(1)}, u32[]{:S(2)}, u32[]{:S(2)}) collective-permute-start(bf16[4,512,128]{2,1,0:T(8,128)(2,1)S(1)} %pad_maximum_fusion.7.refs_0_), channel_id=1, source_target_pairs={{0,16},{16,0},{8,24},{24,8},{1,17},{17,1},{9,25},{25,9},{2,18},{18... | collective-permute-start | bytes 1572872 | tf_op jit(solution)/shard_map/ppermute | solution.py:461
  291.6 23.3 %collective-permute-start.32 = (bf16[4,512,128]{2,1,0:T(8,128)(2,1)S(1)}, bf16[4,512,128]{2,1,0:T(8,128)(2,1)S(1)}, u32[]{:S(2)}, u32[]{:S(2)}) collective-permute-start(bf16[4,512,128]{2,1,0:T(8,128)(2,1)S(1)} %pad_maximum_fusion.7.refs_0_), channel_id=1, source_target_pairs={{0,24},{24,0},{8,16},{16,8},{1,25},{25,1},{9,17},{17,9},{2,26},{26... | collective-permute-start | bytes 1572872 | tf_op jit(solution)/shard_map/ppermute | solution.py:461
  (42 other events, 474.7 us)
Sparse Core Ops, SparseCore 0:
  10.7 92.6 all-gather.2
  219.5 74.5 all-gather.4
